TPU v7x, 256 devices: a whole 4x4x8 slice. The times are simulated.
256 devices in a mesh: dom: 64 (over x, z, core), feat: 4 (over y).
Axes of the slice: x: 4, y: 4, z: 8, core: 2. Of those that a mesh axis runs over, the one named last changes fastest.
Arguments:
- features: bfloat16 [262144, 128], P('dom', 'feat'), may hold values from -6 to 6
- weight_one: bfloat16 [128, 256], replicated, may hold values from -0.5 to 0.5
- weight_two: bfloat16 [256, 172], replicated, may hold values from -0.375 to 0.375
- grad_logits: bfloat16 [262144, 172], P('dom', 'feat'), may hold values from -0.15625 to 0.15625
- send_idx: int32 [4096, 64], P('dom'), may hold values from 0 to 4095
- send_count: int32 [4096], P('dom'), may hold values from 16 to 64, as said below
- tile_cols: int32 [2048, 10], P('dom'), may hold values from 0 to 63, as said below
- tile_vals: bfloat16 [2048, 10, 128, 128], P('dom'), may hold values from 0 to 0.06982422
Outputs:
- logits: bfloat16 [262144, 172], P('dom', 'feat')
- grad_one: float32 [128, 256], replicated
- grad_two: float32 [256, 172], replicated
Inputs may be any that keep to these rules, and one draw needn't show every extreme that they name: `send_count`: some partition receives 64 live rows from every partition. `tile_cols`: tiles below 32 are a partition's own rows, the others its boundary panel; each row tile lists its own diagonal tile first, and every tile of the boundary panel is listed by some row tile of the partition; tiles may repeat.
All inputs are finite; a program needn't handle non-finite values.
Results may differ from a plain program's by a relative error of at most 0.005.
Values may be sent and summed in bfloat16 or wider, within the bound.
No kernel may reach another device: no remote copies, remote signals or barrier semaphores. Data moves between devices by JAX's collectives and lax.ppermute only.
A program may use at most 128 MiB of HBM per device.

v0:
```python
import jax
import jax.numpy as jnp
from jax import lax
from jax.sharding import PartitionSpec as P


def on_device(
    features, weight_one, weight_two, grad_logits, send_idx, send_count, tile_cols, tile_vals
):
    partitions = lax.axis_size("dom")
    feat_count = lax.axis_size("feat")
    feat_index = lax.axis_index("feat")
    rows_dev = features.shape[0]
    tile_rows = tile_vals.shape[2]
    bound_rows = send_idx.shape[1]
    live_slots = jnp.arange(bound_rows, dtype=jnp.int32)[None, :] < send_count[:, None]

    def outgoing(panel_in):
        picked = jnp.take(panel_in, send_idx.reshape(-1), axis=0).reshape(
            partitions, bound_rows, -1
        )
        picked = jnp.where(live_slots[:, :, None], picked, jnp.zeros((), panel_in.dtype))
        return picked.reshape(partitions, -1)

    def combine(panel_in, received):
        panel_cols = panel_in.shape[1]
        extended = jnp.concatenate(
            [panel_in, received.reshape(partitions * bound_rows, panel_cols)], axis=0
        )
        extended = extended.reshape(-1, tile_rows, panel_cols)
        picked = jnp.take(extended, tile_cols, axis=0)
        result = jnp.einsum("tkij,tkjc->tic", tile_vals, picked, preferred_element_type=jnp.float32)
        return result.reshape(rows_dev, panel_cols)

    received_one = lax.all_to_all(
        outgoing(features), "dom", split_axis=0, concat_axis=0, tiled=True
    )
    mixed_one = combine(features, received_one).astype(jnp.bfloat16)
    mixed_full = lax.all_gather(mixed_one, "feat", axis=1, tiled=True)
    hid_cols = weight_one.shape[1] // feat_count
    weight_cols = lax.dynamic_slice_in_dim(weight_one, feat_index * hid_cols, hid_cols, 1)
    pre_one = jnp.dot(mixed_full, weight_cols, preferred_element_type=jnp.float32)
    hidden_one = jax.nn.silu(pre_one).astype(jnp.bfloat16)
    received_two = lax.all_to_all(
        outgoing(hidden_one), "dom", split_axis=0, concat_axis=0, tiled=True
    )
    mixed_two = combine(hidden_one, received_two).astype(jnp.bfloat16)
    class_cols = weight_two.shape[1] // feat_count
    second_full = lax.all_gather(mixed_two, "feat", axis=1, tiled=True)
    weight_part = lax.dynamic_slice_in_dim(weight_two, feat_index * class_cols, class_cols, 1)
    logits = jnp.dot(second_full, weight_part, preferred_element_type=jnp.float32).astype(
        jnp.bfloat16
    )
    part_two = jnp.dot(second_full.T, grad_logits, preferred_element_type=jnp.float32)
    grad_mixed = lax.psum_scatter(
        lax.dot_general(
            weight_part, grad_logits, (((1,), (1,)), ((), ())), preferred_element_type=jnp.float32
        ),
        "feat",
        scatter_dimension=0,
        tiled=True,
    ).T.astype(jnp.bfloat16)
    total_two = lax.psum(part_two, "dom")
    grad_cols = grad_mixed.shape[1]
    slab_rows = grad_mixed.reshape(-1, tile_rows, grad_cols)
    contrib = jnp.einsum("tkij,tic->tkjc", tile_vals, slab_rows, preferred_element_type=jnp.float32)
    count_tiles = rows_dev // tile_rows + partitions * bound_rows // tile_rows
    owners = (
        tile_cols.reshape(-1)[:, None] == jnp.arange(count_tiles, dtype=jnp.int32)[None, :]
    ).astype(jnp.float32)
    ext_grad = jnp.einsum(
        "ne,njc->ejc",
        owners,
        contrib.reshape(-1, tile_rows, grad_cols),
        precision=lax.Precision.HIGHEST,
    )
    ext_grad = ext_grad.reshape(-1, grad_cols)
    local_grad = ext_grad[:rows_dev]
    remote_grad = ext_grad[rows_dev:].reshape(partitions, bound_rows * grad_cols)
    returned = (
        lax.all_to_all(
            remote_grad.astype(jnp.bfloat16), "dom", split_axis=0, concat_axis=0, tiled=True
        )
        .astype(remote_grad.dtype)
        .reshape(partitions, bound_rows, grad_cols)
    )
    returned = jnp.where(live_slots[:, :, None], returned, 0.0)
    grad_hidden = local_grad.at[send_idx.reshape(-1)].add(returned.reshape(-1, grad_cols))
    sigmoid_z = jax.nn.sigmoid(pre_one)
    grad_pre = (grad_hidden * sigmoid_z * (1.0 + pre_one * (1.0 - sigmoid_z))).astype(jnp.bfloat16)
    part_one = jnp.dot(mixed_full.T, grad_pre, preferred_element_type=jnp.float32)
    total_one = lax.psum(part_one, "dom")
    grad_one, grad_two = (
        lax.all_gather(total_one, "feat", axis=1, tiled=True),
        lax.all_gather(total_two, "feat", axis=1, tiled=True),
    )
    return (logits, grad_one, grad_two)


def solution(mesh):
    return jax.shard_map(
        on_device,
        mesh=mesh,
        in_specs=(
            P("dom", "feat"),
            P(),
            P(),
            P("dom", "feat"),
            P("dom", None),
            P("dom"),
            P("dom", None),
            P("dom", None, None, None),
        ),
        out_specs=(P("dom", "feat"), P(), P()),
        check_vma=False,
    )
```

profile of v0, /device:TPU:2, one launch (start us, length us, event | category | flops | bytes accessed | tf_op | source)
XLA Modules:
  0.0 462.5 jit_solution(14310072128050194322)
XLA Ops:
  11.1 12.1 %gather_fusion = bf16[4096,32]{1,0:T(8,128)(2,1)S(1)} fusion(bf16[4096,32]{1,0:T(8,128)(2,1)S(1)} %copy.68, s32[4096]{0:T(1024)S(1)} %broadcast_clamp_fusion), kind=kCustom, calls=%fused_computation | custom fusion | bytes 540672 | tf_op jit(solution)/shard_map/jit(_take)/gather | solution.py:19
  27.9 12.0 %all-to-all-start = ((bf16[64,2,1024]{2,1,0:T(2,128)(2,1)}), bf16[64,2,1024]{2,1,0:T(2,128)(2,1)S(1)}, u32[]{:S(2)}, u32[]{:S(2)}) async-start(bf16[64,2,1024]{2,1,0:T(2,128)(2,1)} %reshape.266), calls=%async_computation | async-start | bytes 524288 | tf_op jit(solution)/shard_map/all_to_all | solution.py:35
  40.3 11.2 %all-to-all-done = bf16[64,2,1024]{2,1,0:T(2,128)(2,1)S(1)} async-done(((bf16[64,2,1024]{2,1,0:T(2,128)(2,1)}), bf16[64,2,1024]{2,1,0:T(2,128)(2,1)S(1)}, u32[]{:S(2)}, u32[]{:S(2)}) %all-to-all-start) | async-done | bytes 262176 | tf_op jit(solution)/shard_map/all_to_all | solution.py:35
  56.8 6.4 %fusion.27 = bf16[32,4,8,128]{3,2,1,0:T(8,128)(2,1)S(1)} fusion(bf16[32,10,128,128]{3,2,1,0:T(8,128)(2,1)} %param.15, bf16[32,10,128,32]{2,3,1,0:T(8,128)(2,1)S(1)} %bitcast.79, pred[32,10]{1,0:T(8,128)(4,1)S(1)} %copy.64), kind=kOutput, calls=%fused_computation.23 | convolution fusion | flops 336986112 | bytes 13369664 | tf_op jit(solution)/shard_map/tkij,tkjc->tic/dot_general | solution.py:32
  64.1 3.5 fusion.40
  71.1 17.0 %all-gather.4.cloned.1.call-done = bf16[4096,128]{0,1:T(8,128)(2,1)} async-done(((bf16[4096,32]{0,1:T(8,128)(2,1)}), bf16[4096,128]{0,1:T(8,128)(2,1)}) %all-gather.4.cloned.1.call-update) | async-done | bytes 1048592 | tf_op jit(solution)/shard_map/all_gather | solution.py:39
  91.3 14.1 %gather_fusion.2 = bf16[4096,64]{1,0:T(8,128)(2,1)S(1)} fusion(bf16[4096,64]{1,0:T(8,128)(2,1)S(1)} %copy.75, s32[4096]{0:T(1024)} %copy-done.3), kind=kCustom, calls=%fused_computation.2 | custom fusion | bytes 1064960 | tf_op jit(solution)/shard_map/jit(_take)/gather | solution.py:19
  107.8 27.0 %all_to_all.18 = bf16[64,2,2048]{2,1,0:T(2,128)(2,1)S(1)} all-to-all(bf16[64,2,2048]{2,1,0:T(2,128)(2,1)S(1)} %reshape.268), channel_id=1, replica_groups=mesh['dom'=64,'feat'=4] {'dom'}, dimensions={0} | all-to-all | bytes 1048576 | tf_op jit(solution)/shard_map/all_to_all | solution.py:44
  135.3 3.1 reduce.1
  140.3 13.3 %gather_fusion.3 = bf16[320,128,64]{1,2,0:T(8,128)(2,1)} fusion(bf16[64,128,64]{1,2,0:T(8,128)(2,1)S(1)} %copy_bitcast_fusion, s32[1024]{0:T(1024)S(1)} %pad_clamp_fusion), kind=kCustom, calls=%fused_computation.3 | custom fusion | bytes 10487040 | tf_op jit(solution)/shard_map/jit(_take)/gather | solution.py:31
  153.6 9.3 %fusion.18 = bf16[32,8,8,128]{3,2,1,0:T(8,128)(2,1)S(1)} fusion(bf16[32,10,128,128]{3,2,1,0:T(8,128)(2,1)} %param.15, bf16[32,10,128,64]{2,3,1,0:T(8,128)(2,1)} %bitcast.80, pred[32,10]{1,0:T(8,128)(4,1)S(1)} %copy.64), kind=kOutput, calls=%fused_computation.20 | convolution fusion | flops 673972224 | bytes 16253248 | tf_op jit(solution)/shard_map/tkij,tkjc->tic/dot_general | solution.py:32
  165.5 13.7 %fusion.32 = f32[32,64,10,128]{3,1,2,0:T(8,128)S(1)} fusion(bf16[32,10,128,128]{3,2,1,0:T(8,128)(2,1)} %param.15, bf16[32,128,64,1]{1,0,2,3:T(8,128)(2,1)S(1)} %bitcast.82), kind=kOutput, calls=%fused_computation.38 | convolution fusion | flops 671088640 | bytes 21495808 | tf_op jit(solution)/shard_map/tkij,tic->tkjc/dot_general | solution.py:66
  179.2 10.5 %fusion = f32[64,128,64]{1,0,2:T(8,128)S(1)} fusion(f32[320,128,64]{1,2,0:T(8,128)S(1)} %bitcast.78, s32[320]{0:T(512)S(1)} %eq.15), kind=kOutput, calls=%fused_computation.5 | convolution fusion | flops 2013286400 | bytes 12584192 | tf_op jit(solution)/shard_map/ne,njc->ejc/dot_general | solution.py:71
  191.4 4.0 convert_element_type.68
  195.4 4.6 %reduce.6 = bf16[64,4096]{1,0:T(8,128)(2,1)} reduce(bf16[64,1,4096]{2,1,0:T(2,128)(2,1)S(1)} %convert_element_type.68, bf16[]{:T(256)} %broadcast.107), dimensions={1}, to_apply=%convert_element_type.68.reduce_sub_computation | reduce | bytes 1048578 | tf_op jit(solution)/shard_map/convert_element_type | solution.py:82
  202.3 7.5 %all-to-all-start.2 = ((bf16[64,2,2048]{2,1,0:T(2,128)(2,1)}), bf16[64,2,2048]{2,1,0:T(2,128)(2,1)}, u32[]{:S(2)}, u32[]{:S(2)}) async-start(bf16[64,2,2048]{2,1,0:T(2,128)(2,1)} %reshape.270), calls=%async_computation.3 | async-start | bytes 1048576 | tf_op jit(solution)/shard_map/all_to_all | solution.py:81
  209.9 3.0 fusion.49
  215.0 11.4 %all-to-all-done.2 = bf16[64,2,2048]{2,1,0:T(2,128)(2,1)} async-done(((bf16[64,2,2048]{2,1,0:T(2,128)(2,1)}), bf16[64,2,2048]{2,1,0:T(2,128)(2,1)}, u32[]{:S(2)}, u32[]{:S(2)}) %all-to-all-start.2) | async-done | bytes 524320 | tf_op jit(solution)/shard_map/all_to_all | solution.py:81
  226.4 3.9 reshape.271
  230.3 3.0 convert_reduce_fusion
  234.1 25.4 %scatter_custom_fusion = f32[4096,64]{1,0:T(8,128)} fusion(f32[4096,64]{1,0:T(8,128)} %bitcast.81, s32[4096]{0:T(1024)} %bitcast.88, f32[4096,64]{1,0:T(8,128)S(1)} %reshape.210, f32[]{:T(128)} %constant.75.clone.1, pred[4096]{0:T(1024)(128)(4,1)S(1)} %lt.78), kind=kCustom, calls=%fused_computation.15 | custom fusion | flops 524288 | bytes 2101760 | tf_op jit(solution)/shard_map/scatter-add | solution.py:88
  266.6 162.6 %all-reduce.3.cloned.1.call-done = (f32[128,64]{0,1:T(8,128)}, f32[256,43]{0,1:T(8,128)}) async-done(((f32[128,64]{0,1:T(8,128)}, f32[256,43]{0,1:T(8,128)}), (f32[128,64]{0,1:T(8,128)}, f32[256,43]{0,1:T(8,128)})) %all-reduce.3.cloned.1.call-update) | async-done | bytes 76816 | tf_op jit(solution)/shard_map/psum | solution.py:92
  429.2 12.7 %all-gather = f32[4,43,256]{2,1,0:T(8,128)S(1)} all-gather(f32[1,43,256]{2,1,0:T(8,128)} %bitcast.89), channel_id=1, replica_groups=mesh['dom'=64,'feat'=4] {'feat'}, dimensions={0}, use_global_device_ids=true | all-gather | bytes 220160 | tf_op jit(solution)/shard_map/all_gather | solution.py:95
  442.6 12.2 %all_gather.14 = f32[128,256]{0,1:T(8,128)S(1)} all-gather(f32[128,64]{0,1:T(8,128)} %get-tuple-element.15), channel_id=1, replica_groups=mesh['dom'=64,'feat'=4] {'feat'}, dimensions={1}, use_global_device_ids=true | all-gather | bytes 163840 | tf_op jit(solution)/shard_map/all_gather | solution.py:94
  (90 shorter events, 44.2 us)
Async XLA Ops:
  7.2 56.9 %copy-start = (bf16[4096,43]{0,1:T(8,128)(2,1)S(1)}, bf16[4096,43]{0,1:T(8,128)(2,1)}, u32[]{:S(2)}) copy-start(bf16[4096,43]{0,1:T(8,128)(2,1)} %param.11) | copy-start | bytes 1056772
  8.9 15.9 %copy-start.4 = (pred[64,64]{1,0:T(8,128)(4,1)}, pred[64,64]{1,0:T(8,128)(4,1)S(1)}, u32[]{:S(2)}) copy-start(pred[64,64]{1,0:T(8,128)(4,1)S(1)} %compare_and_fusion) | copy-start | bytes 12292
  9.6 13.6 %copy-start.8 = (s32[4096,1]{0,1:T(1,128)}, s32[4096,1]{0,1:T(1,128)S(1)}, u32[]{:S(2)}) copy-start(s32[4096,1]{0,1:T(1,128)S(1)} %compare_select_fusion) | copy-start | bytes 49156
  9.7 13.6 %copy-start.3 = (s32[4096]{0:T(1024)}, s32[4096]{0:T(1024)S(1)}, u32[]{:S(2)}) copy-start(s32[4096]{0:T(1024)S(1)} %broadcast_clamp_fusion) | copy-start | bytes 49156
  24.4 15.6 %copy-start.6 = (s32[32,10]{0,1:T(8,128)S(1)}, s32[32,10]{0,1:T(8,128)}, u32[]{:S(2)}) copy-start(s32[32,10]{0,1:T(8,128)} %param.14) | copy-start | bytes 3844
  27.0 27.3 %copy-start.2 = (bf16[4096,32]{0,1:T(8,128)(2,1)S(1)}, bf16[4096,32]{0,1:T(8,128)(2,1)}, u32[]{:S(2)}) copy-start(bf16[4096,32]{0,1:T(8,128)(2,1)} %param.8) | copy-start | bytes 786436
  27.9 23.6 %all-to-all-start = ((bf16[64,2,1024]{2,1,0:T(2,128)(2,1)}), bf16[64,2,1024]{2,1,0:T(2,128)(2,1)S(1)}, u32[]{:S(2)}, u32[]{:S(2)}) async-start(bf16[64,2,1024]{2,1,0:T(2,128)(2,1)} %reshape.266), calls=%async_computation | async-start | bytes 524288 | tf_op jit(solution)/shard_map/all_to_all | solution.py:35
  39.9 48.2 %all-gather.4.cloned.1.call-start = ((), (), s32[]{:S(2)}) async-start(), calls=%async_computation.4 | async-start | bytes 1310720 | tf_op jit(solution)/shard_map/all_gather | solution.py:39
  64.0 100.1 %reduce-scatter.2.cloned.1.call-start = ((), (), s32[]{:S(2)}) async-start(), calls=%async_computation.6 | async-start | bytes 5242880 | tf_op jit(solution)/shard_map/reduce_scatter | solution.py:55
  67.6 1.9 copy-start.5
  67.6 20.6 %copy-start.9 = (bf16[128,256]{1,0:T(8,128)(2,1)S(1)}, bf16[128,256]{1,0:T(8,128)(2,1)}, u32[]{:S(2)}) copy-start(bf16[128,256]{1,0:T(8,128)(2,1)} %param.9) | copy-start | bytes 196612
  67.6 142.3 %all-gather.6.cloned.1.call-start = ((), (), s32[]{:S(2)}) async-start(), calls=%async_computation.5 | async-start | bytes 2621440 | tf_op jit(solution)/shard_map/all_gather | solution.py:49
  153.6 10.3 %copy-start.7 = (s32[32,10]{0,1:T(8,128)S(1)}, s32[32,10]{0,1:T(8,128)}, u32[]{:S(2)}) copy-start(s32[32,10]{0,1:T(8,128)} %param.14) | copy-start | bytes 3844
  202.3 24.1 %all-to-all-start.2 = ((bf16[64,2,2048]{2,1,0:T(2,128)(2,1)}), bf16[64,2,2048]{2,1,0:T(2,128)(2,1)}, u32[]{:S(2)}, u32[]{:S(2)}) async-start(bf16[64,2,2048]{2,1,0:T(2,128)(2,1)} %reshape.270), calls=%async_computation.3 | async-start | bytes 1048576 | tf_op jit(solution)/shard_map/all_to_all | solution.py:81
  209.8 219.4 %all-reduce.3.cloned.1.call-start = ((), (), s32[]{:S(2)}) async-start(), calls=%async_computation.7 | async-start | bytes 163840 | tf_op jit(solution)/shard_map/psum | solution.py:92
  261.7 2.9 copy-start.1
Sparse Core Ops, SparseCore 0:
  64.1 23.9 all-gather.3
  90.7 49.7 reduce-scatter.1
  164.0 30.0 all-gather.5
  264.7 164.4 all-reduce.2
where the time goes:
time: 471 us; the launch traced here: 462 us
  waiting for transfers between devices  202 us (43%)
  local copies, waits for them, and re-layouts  76.4 us (16%)
  matrix products  53.9 us (11%)
  blocking collectives  51.9 us (11%)
  other arithmetic  43.4 us (9%)
  starting transfers between devices  19.9 us (4%)
  between operations  14.7 us (3%)
    psum x1, waiting for transfers between devices, on_device(): total_one = lax.psum(part_one, 'dom')  163 us
    gather x5, local copies, waits for them, and re-layouts, outgoing(): jnp.take(panel_in, send_idx.reshape(-1), axis=0)  28.4 us
    all_to_all x1, blocking collectives, on_device(): lax.all_to_all(outgoing(hidden_one), 'dom', split_axis=0, concat_axis=0,...  27 us
    scatter-add x1, other arithmetic, on_device(): local_grad.at[send_idx.reshape(-1)].add(returned.reshape(-1, grad_cols))  25.4 us
    all_gather x1, waiting for transfers between devices, on_device(): mixed_full = lax.all_gather(mixed_one, 'feat', axis=1, tiled=True)  17 us
    dot_general x2, matrix products, combine(): jnp.einsum('tkij,tkjc->tic', tile_vals, picked, preferred_element_type=jn...  15.7 us
    gather x2, local copies, waits for them, and re-layouts, combine(): picked = jnp.take(extended, tile_cols, axis=0)  15.7 us
    dot_general x1, matrix products, on_device(): jnp.einsum('tkij,tic->tkjc', tile_vals, slab_rows, preferred_element_type...  13.7 us
  transfers between devices with their start and end apart: 6, of which 4 were waited for; matrix products, arithmetic and copies ran while one was open for 22% of the time, Pallas kernels for 0%

commit v1 on v0

v1 whole, which is shorter than its diff:
```python
import functools

import jax
import jax.numpy as jnp
from jax import lax
from jax.experimental import pallas as pl
from jax.experimental.pallas import tpu as pltpu
from jax.sharding import PartitionSpec as P

BF = jnp.bfloat16
F32 = jnp.float32
VMEM = pltpu.VMEM
LIMIT = 48 * 1024 * 1024
NT = (((1,), (1,)), ((), ()))
NN = (((1,), (0,)), ((), ()))


def dot(a, b, dims=NN):
    return lax.dot_general(a, b, dims, preferred_element_type=F32)


def params():
    return pltpu.CompilerParams(vmem_limit_bytes=LIMIT)


def cost(flops, nbytes):
    return pl.CostEstimate(flops=flops, bytes_accessed=nbytes, transcendentals=0)


def whole():
    return pl.BlockSpec(memory_space=VMEM)


def gather_packed(stack_ref, idx_ref, out_ref, cols):
    chunks = stack_ref.shape[0] // cols
    lanes = stack_ref.shape[1]
    row_ids = lax.broadcasted_iota(jnp.int32, (lanes, 256), 0)
    low = lax.broadcasted_iota(jnp.int32, (16, 128), 1) < 64

    def step(j, carry):
        idx = idx_ref[pl.ds(j, 1), :]
        hot = (row_ids == (idx & (lanes - 1))).astype(BF)
        part = idx >> (lanes.bit_length() - 1)
        got = jnp.zeros((cols, 256), F32)
        for base in range(0, chunks, 4):
            wide = dot(stack_ref[base * cols : (base + 4) * cols, :], hot)
            for c in range(4):
                got = jnp.where(part == base + c, wide[c * cols : (c + 1) * cols], got)
        for pair in range(2):
            top = got[:16, pair * 128 : (pair + 1) * 128]
            bottom = got[16:, pair * 128 : (pair + 1) * 128]
            first = jnp.where(low, top, pltpu.roll(bottom, 64, 1))
            second = jnp.where(low, pltpu.roll(top, 64, 1), bottom)
            out_ref[j * 4 + pair * 2] = first.astype(BF)
            out_ref[j * 4 + pair * 2 + 1] = second.astype(BF)
        return carry

    lax.fori_loop(0, idx_ref.shape[0], step, 0)


def unpack_pair(first, second):
    low = lax.broadcasted_iota(jnp.int32, (16, 128), 1) < 64
    first, second = first.astype(F32), second.astype(F32)
    top = jnp.where(low, first, pltpu.roll(second, 64, 1))
    bottom = jnp.where(low, pltpu.roll(first, 64, 1), second)
    return jnp.concatenate([top, bottom], axis=0).astype(BF)


def fill_stack(stack_ref, panel_ref):
    cols, rows = panel_ref.shape
    for c in range(rows // 256):
        stack_ref[c * cols : (c + 1) * cols, :] = panel_ref[:, c * 256 : (c + 1) * 256]


def gather_kernel(panel_ref, idx_ref, out_ref, stack_ref):
    fill_stack(stack_ref, panel_ref)
    gather_packed(stack_ref, idx_ref, out_ref, panel_ref.shape[0])


def gather_call(panel, idx):
    cols, rows = panel.shape
    pieces = idx.size // 64
    return pl.pallas_call(
        gather_kernel,
        out_shape=jax.ShapeDtypeStruct((pieces, 16, 128), BF),
        in_specs=[whole(), whole()],
        out_specs=whole(),
        scratch_shapes=[VMEM((rows // 256 * cols, 256), BF)],
        compiler_params=params(),
        cost_estimate=cost(2 * 512 * 256 * 4096, 1 << 20),
        name="gather_rows",
    )(panel, idx)


STEP = 4


def transpose_agg_kernel(cols_ref, me_ref, grad_ref, vals_ref, o0, o1, o2, o3, acc):
    step = pl.program_id(0)
    tiles = vals_ref.shape[1]

    @pl.when(step == 0)
    def _():
        acc[...] = jnp.zeros_like(acc)

    for r in range(STEP):
        t = step * STEP + r
        slab = grad_ref[:, r * 128 : (r + 1) * 128]
        side = jnp.concatenate([vals_ref[r, k] for k in range(tiles)], axis=1)
        part = dot(slab, side)
        for k in range(tiles):
            acc[cols_ref[t, k]] += part[:, k * 128 : (k + 1) * 128]

    @pl.when(step == pl.num_programs(0) - 1)
    def _():
        me = me_ref[0]
        for d, out in enumerate((o0, o1, o2, o3)):
            chunk = (me ^ d) * 8
            for j in range(8):
                out[:, j * 128 : (j + 1) * 128] = acc[chunk + j].astype(BF)
                out[:, (8 + j) * 128 : (9 + j) * 128] = acc[32 + chunk + j].astype(BF)


def transpose_agg_call(grad, cols, vals, me):
    width, rows = grad.shape
    row_tiles, tiles = cols.shape
    out = jax.ShapeDtypeStruct((width, 2048), BF)
    return pl.pallas_call(
        transpose_agg_kernel,
        out_shape=(out,) * 4,
        grid_spec=pltpu.PrefetchScalarGridSpec(
            num_scalar_prefetch=2,
            grid=(row_tiles // STEP,),
            in_specs=[
                pl.BlockSpec((width, STEP * 128), lambda s, *_: (0, s)),
                pl.BlockSpec((STEP, tiles, 128, 128), lambda s, *_: (s, 0, 0, 0)),
            ],
            out_specs=[pl.BlockSpec((width, 2048), lambda s, *_: (0, 0))] * 4,
            scratch_shapes=[VMEM((64, width, 128), F32)],
        ),
        compiler_params=params(),
        cost_estimate=cost(2 * 48 * 128 * 128 * 320 * 4, 11 << 20),
        name="agg_transposed",
    )(cols, me, grad, vals)


def agg_rows(step, cols_ref, ext, vals_ref, r):
    tiles = vals_ref.shape[1]
    t = step * STEP + r
    total = None
    for k in range(0, tiles, 2):
        left = jnp.concatenate([ext[cols_ref[t, k]], ext[cols_ref[t, k + 1]]], axis=1)
        right = jnp.concatenate([vals_ref[r, k], vals_ref[r, k + 1]], axis=1)
        part = dot(left, right, NT)
        total = part if total is None else total + part
    return total


def agg_one_kernel(cols_ref, me_ref, panel_ref, recv_ref, idx_ref, vals_ref, packed_ref, o0, o1, o2, o3, ext, stack):
    step = pl.program_id(0)

    @pl.when(step == 0)
    def _():
        for e in range(32):
            ext[e] = panel_ref[:, e * 128 : (e + 1) * 128]
            ext[32 + e] = unpack_pair(recv_ref[2 * e], recv_ref[2 * e + 1])

    for r in range(STEP):
        total = agg_rows(step, cols_ref, ext, vals_ref, r).astype(BF)
        place = pl.multiple_of((step * STEP + r) // 2 * 32, 32)
        stack[pl.ds(place, 32), (r % 2) * 128 : (r % 2 + 1) * 128] = total

    @pl.when(step == pl.num_programs(0) - 1)
    def _():
        me = me_ref[0]
        for d, out in enumerate((o0, o1, o2, o3)):
            for j in range(4):
                place = pl.multiple_of(((me ^ d) * 4 + j) * 32, 32)
                out[:, j * 256 : (j + 1) * 256] = stack[pl.ds(place, 32), :]
        gather_packed(stack, idx_ref, packed_ref, 32)


def agg_one_call(panel, received, idx, cols, vals, me):
    row_tiles, tiles = cols.shape
    pieces = received.shape[0]
    out = jax.ShapeDtypeStruct((32, 1024), BF)
    return pl.pallas_call(
        agg_one_kernel,
        out_shape=(jax.ShapeDtypeStruct((pieces, 16, 128), BF),) + (out,) * 4,
        grid_spec=pltpu.PrefetchScalarGridSpec(
            num_scalar_prefetch=2,
            grid=(row_tiles // STEP,),
            in_specs=[
                pl.BlockSpec((32, 4096), lambda s, *_: (0, 0)),
                pl.BlockSpec((pieces, 16, 128), lambda s, *_: (0, 0, 0)),
                pl.BlockSpec(idx.shape, lambda s, *_: (0, 0)),
                pl.BlockSpec((STEP, tiles, 128, 128), lambda s, *_: (s, 0, 0, 0)),
            ],
            out_specs=[pl.BlockSpec((pieces, 16, 128), lambda s, *_: (0, 0, 0))]
            + [pl.BlockSpec((32, 1024), lambda s, *_: (0, 0))] * 4,
            scratch_shapes=[VMEM((64, 32, 128), BF), VMEM((512, 256), BF)],
        ),
        compiler_params=params(),
        cost_estimate=cost(2 * 32 * 128 * 128 * 320 * 8, 11 << 20),
        name="agg_one",
    )(cols, me, panel, received, idx, vals)


def dense_kernel(me_ref, *refs):
    own = refs[0:4]
    far = refs[4:8]
    zs = refs[8:12]
    w1t, w2, w2t = refs[12:15]
    ys = refs[15:19]
    gs = refs[19:23]
    mix, zed, hid, gp, yall, gall = refs[23:29]
    me = me_ref[0]
    for d in range(4):
        f = me ^ d
        at = pl.multiple_of(f * 32, 32)
        mix[pl.ds(at, 32), 0:1024] = own[d][...]
        for e in range(8):
            mix[pl.ds(at, 32), 1024 + e * 128 : 1024 + (e + 1) * 128] = unpack_pair(
                far[d][2 * e], far[d][2 * e + 1]
            )
        zed[pl.ds(pl.multiple_of(f * 48, 16), 48), :] = zs[d][...]
    for c in range(8):
        lanes = slice(c * 256, (c + 1) * 256)
        pre = dot(w1t[...], mix[:, lanes])
        gate = 1.0 / (1.0 + jnp.exp(-pre))
        hidden = (pre * gate).astype(BF)
        hid[:, lanes] = hidden
        yall[:, lanes] = dot(w2t[...], hidden).astype(BF)
        gh = dot(w2[...], zed[:, lanes])
        gp[:, lanes] = (gh * gate * (1.0 + pre * (1.0 - gate))).astype(BF)
    p1 = dot(mix[...], gp[...], NT)
    p2 = dot(zed[...], hid[...], NT)
    gall[0:128] = p1[:, :128]
    gall[128:256] = p1[:, 128:]
    gall[256:448] = p2[:, :128]
    gall[448:640] = p2[:, 128:]
    for d in range(4):
        f = me ^ d
        ys[d][...] = yall[pl.ds(pl.multiple_of(f * 48, 16), 48), :]
        gs[d][...] = gall[pl.ds(pl.multiple_of(f * 160, 8), 160), :]


def dense_call(me, own, far, zs, w1t, w2, w2t):
    return pl.pallas_call(
        dense_kernel,
        out_shape=(jax.ShapeDtypeStruct((48, 2048), BF),) * 4
        + (jax.ShapeDtypeStruct((160, 128), F32),) * 4,
        in_specs=[pl.BlockSpec(memory_space=pltpu.SMEM)] + [whole()] * 15,
        out_specs=[whole()] * 8,
        scratch_shapes=[
            VMEM((128, 2048), BF),
            VMEM((192, 2048), BF),
            VMEM((256, 2048), BF),
            VMEM((256, 2048), BF),
            VMEM((192, 2048), BF),
            VMEM((640, 128), F32),
        ],
        compiler_params=params(),
        cost_estimate=cost(2 * 2048 * 256 * 1500, 4 << 20),
        name="dense",
    )(me, *own, *far, *zs, w1t, w2, w2t)


def agg_two_kernel(cols_ref, me_ref, y0, y1, y2, y3, vals_ref, out_ref, ext):
    step = pl.program_id(0)

    @pl.when(step == 0)
    def _():
        me = me_ref[0]
        for d, y in enumerate((y0, y1, y2, y3)):
            chunk = (me ^ d) * 8
            for j in range(8):
                ext[chunk + j] = y[:, j * 128 : (j + 1) * 128]
                ext[32 + chunk + j] = y[:, (8 + j) * 128 : (9 + j) * 128]

    for r in range(STEP):
        total = agg_rows(step, cols_ref, ext, vals_ref, r).astype(BF)
        out_ref[:, r * 128 : (r + 1) * 128] = total[: out_ref.shape[0]]


def agg_two_call(ys, cols, vals, me, classes):
    row_tiles, tiles = cols.shape
    return pl.pallas_call(
        agg_two_kernel,
        out_shape=jax.ShapeDtypeStruct((classes, row_tiles * 128), BF),
        grid_spec=pltpu.PrefetchScalarGridSpec(
            num_scalar_prefetch=2,
            grid=(row_tiles // STEP,),
            in_specs=[pl.BlockSpec((48, 2048), lambda s, *_: (0, 0))] * 4
            + [pl.BlockSpec((STEP, tiles, 128, 128), lambda s, *_: (s, 0, 0, 0))],
            out_specs=pl.BlockSpec((classes, STEP * 128), lambda s, *_: (0, s)),
            scratch_shapes=[VMEM((64, 48, 128), BF)],
        ),
        compiler_params=params(),
        cost_estimate=cost(2 * 48 * 128 * 128 * 320 * 4, 11 << 20),
        name="agg_two",
    )(cols, me, *ys, vals)


def finish_kernel(me_ref, g0, g1, g2, g3, one_ref, two_ref, buf):
    me = me_ref[0]
    for d, g in enumerate((g0, g1, g2, g3)):
        buf[pl.ds(pl.multiple_of((me ^ d) * 160, 8), 160), :] = g[...]
    one_ref[:, :128] = buf[0:128]
    one_ref[:, 128:] = buf[128:256]
    per = two_ref.shape[0] // 4
    for f in range(4):
        two_ref[f * per : (f + 1) * per, :128] = buf[256 + 48 * f : 256 + 48 * f + per]
        two_ref[f * per : (f + 1) * per, 128:] = buf[448 + 48 * f : 448 + 48 * f + per]


def finish_call(me, gs, classes):
    return pl.pallas_call(
        finish_kernel,
        out_shape=(
            jax.ShapeDtypeStruct((128, 256), F32),
            jax.ShapeDtypeStruct((classes, 256), F32),
        ),
        in_specs=[pl.BlockSpec(memory_space=pltpu.SMEM)] + [whole()] * 4,
        out_specs=[whole()] * 2,
        scratch_shapes=[VMEM((640, 128), F32)],
        compiler_params=params(),
        name="finish",
    )(me, *gs)


def swap(x, axis, size, mask):
    return lax.ppermute(x, axis, [(i, i ^ mask) for i in range(size)])


def on_device(
    features, weight_one, weight_two, grad_logits, send_idx, send_count, tile_cols, tile_vals
):
    partitions = lax.axis_size("dom")
    feat = lax.axis_size("feat")
    me = lax.axis_index("feat").astype(jnp.int32)
    me_arr = me.reshape(1)
    bound_rows = send_idx.shape[1]
    class_cols = grad_logits.shape[1]
    hidden = weight_one.shape[1]

    def swap_feat(x, d):
        return swap(x, "feat", feat, d)

    def swap_dom(x, mask):
        return swap(x, "dom", partitions, mask)

    live = jnp.arange(bound_rows, dtype=jnp.int32)[None, :] < send_count[:, None]
    idx = jnp.where(live, send_idx, -1).reshape(-1, 256)
    panel = features.T
    grad = jnp.pad(grad_logits.T, ((0, 48 - class_cols), (0, 0)))
    w2 = jnp.pad(weight_two.reshape(hidden, feat, class_cols), ((0, 0), (0, 0), (0, 48 - class_cols)))
    w2 = w2.reshape(hidden, feat * 48)
    w1t = weight_one.T
    w2t = w2.T

    packed_one = gather_call(panel, idx)
    received_one = lax.all_to_all(packed_one, "dom", split_axis=0, concat_axis=0, tiled=True)
    zs = transpose_agg_call(grad, tile_cols, tile_vals, me_arr)
    zs = [zs[0]] + [swap_feat(zs[d], d) for d in (1, 2, 3)]
    packed_two, *mixed = agg_one_call(panel, received_one, idx, tile_cols, tile_vals, me_arr)
    own = [mixed[0]] + [swap_feat(mixed[d], d) for d in (1, 2, 3)]
    received_two = lax.all_to_all(packed_two, "dom", split_axis=0, concat_axis=0, tiled=True)
    pieces = partitions // feat

    def far_block(d):
        return lax.dynamic_slice_in_dim(received_two, (me ^ d) * pieces, pieces, 0)

    far = [far_block(0)] + [swap_feat(far_block(d), d) for d in (1, 2, 3)]
    outs = dense_call(me_arr, own, far, zs, w1t, w2, w2t)
    ys, gs = outs[:4], outs[4:]
    gs_in = [swap_feat(gs[d], d) for d in (1, 2, 3)]
    ys = [ys[0]] + [swap_feat(ys[d], d) for d in (1, 2, 3)]
    total = (gs[0] + gs_in[0]) + (gs_in[1] + gs_in[2])
    total = total + swap_dom(total, 1)
    near = [swap_dom(total, 16 * d) for d in (1, 2, 3)]
    total = (total + near[0]) + (near[1] + near[2])
    for mask in (2, 4, 8):
        total = total + swap_dom(total, mask)
    parts = [total] + [swap_feat(total, d) for d in (1, 2, 3)]
    grad_one, grad_two = finish_call(me_arr, parts, feat * class_cols)
    logits = agg_two_call(ys, tile_cols, tile_vals, me_arr, class_cols)
    return (logits.T, grad_one, grad_two.T)


def solution(mesh):
    return jax.shard_map(
        on_device,
        mesh=mesh,
        in_specs=(
            P("dom", "feat"),
            P(),
            P(),
            P("dom", "feat"),
            P("dom", None),
            P("dom"),
            P("dom", None),
            P("dom", None, None, None),
        ),
        out_specs=(P("dom", "feat"), P(), P()),
        check_vma=False,
    )
```

time: 471 us -> 146 us (0.31); the launches traced: 462 us -> 145 us
  waiting for transfers between devices: 202 us -> 40.6 us
  local copies, waits for them, and re-layouts: 76.4 us -> 3.07 us
  matrix products: 53.9 us -> 0 us
  blocking collectives: 51.9 us -> 0 us
  Pallas kernels: 0 us -> 43.1 us
  other arithmetic: 43.4 us -> 0.91 us
  starting transfers between devices: 19.9 us -> 56.4 us
  between operations: 14.7 us -> 0.82 us
    psum x1 -> x0, waiting for transfers between devices: 163 us -> none  [on_device(): total_one = lax.psum(part_one, 'dom')]
    dot_general x9 -> x0, matrix products: 53.9 us -> none  [the longest x2 15.7 us: combine(): jnp.einsum('tkij,tkjc->tic', tile_vals, picked, preferred_element_type=jn...]
    gather x7 -> x0, local copies, waits for them, and re-layouts: 44.1 us -> none  [the longest x5 28.4 us: outgoing(): jnp.take(panel_in, send_idx.reshape(-1), axis=0)]
    pallas_call x0 -> x6, Pallas kernels: none -> 43.1 us  [the longest x1 15 us: agg_one_call(): pl.pallas_call(agg_one_kernel, out_shape=(jax.ShapeDtypeStruct((pieces, 1...]
    ppermute x0 -> x25, starting transfers between devices: none -> 37.9 us  [swap(): return lax.ppermute(x, axis, [(i, i ^ mask) for i in range(size)])]
    ppermute x0 -> x25, waiting for transfers between devices: none -> 29.8 us  [swap(): return lax.ppermute(x, axis, [(i, i ^ mask) for i in range(size)])]
    all_to_all x1 -> x0, blocking collectives: 27 us -> none  [on_device(): lax.all_to_all(outgoing(hidden_one), 'dom', split_axis=0, concat_axis=0,...]
    scatter-add x1 -> x0, other arithmetic: 25.4 us -> none  [on_device(): local_grad.at[send_idx.reshape(-1)].add(returned.reshape(-1, grad_cols))]
  transfers between devices with their start and end apart: 6 -> 27, of which waited for: 4 -> 12; matrix products, arithmetic and copies ran while one was open for 22% -> 1% of each run, Pallas kernels for 0% -> 13%
where the time goes in v1:
time: 146 us; the launch traced here: 145 us
  starting transfers between devices  56.4 us (39%)
  Pallas kernels  43.1 us (30%)
  waiting for transfers between devices  40.6 us (28%)
  local copies, waits for them, and re-layouts  3.07 us (2%)
    ppermute x25, starting transfers between devices, swap(): return lax.ppermute(x, axis, [(i, i ^ mask) for i in range(size)])  37.9 us
    ppermute x25, waiting for transfers between devices, swap(): return lax.ppermute(x, axis, [(i, i ^ mask) for i in range(size)])  29.8 us
    pallas_call x1, Pallas kernels, agg_one_call(): pl.pallas_call(agg_one_kernel, out_shape=(jax.ShapeDtypeStruct((pieces, 1...  15 us
    all_to_all x1, starting transfers between devices, on_device(): lax.all_to_all(packed_one, 'dom', split_axis=0, concat_axis=0, tiled=True)  12 us
    all_to_all x1, waiting for transfers between devices, on_device(): lax.all_to_all(packed_one, 'dom', split_axis=0, concat_axis=0, tiled=True)  10.8 us
    pallas_call x1, Pallas kernels, agg_two_call(): pl.pallas_call(agg_two_kernel, out_shape=jax.ShapeDtypeStruct((classes, r...  10 us
    pallas_call x1, Pallas kernels, transpose_agg_call(): pl.pallas_call(transpose_agg_kernel, out_shape=(out,) * 4, grid_spec=pltp...  8.6 us
    all_to_all x1, starting transfers between devices, on_device(): lax.all_to_all(packed_two, 'dom', split_axis=0, concat_axis=0, tiled=True)  6.49 us
  transfers between devices with their start and end apart: 27, of which 12 were waited for; matrix products, arithmetic and copies ran while one was open for 1% of the time, Pallas kernels for 13%

profile of v1, /device:TPU:2, one launch (start us, length us, event | category | flops | bytes accessed | tf_op | source)
XLA Modules:
  0.0 144.9 jit_solution(18249933217310500870)
XLA Ops:
  2.5 5.8 %gather_rows.1 = bf16[64,16,128]{2,1,0:T(8,128)(2,1)} custom-call(bf16[32,4096]{1,0:T(8,128)(2,1)S(1)} %bitcast.13, s32[16,256]{1,0:T(8,128)S(1)} %reshape.20.idx_ref), custom_call_target="tpu_custom_call" | custom-call | flops 1073741824 | bytes 1048576 | tf_op jit(solution)/shard_map/gather_rows/pallas_call | solution.py:83
  8.3 12.0 %all-to-all-start = ((bf16[64,16,128]{2,1,0:T(8,128)(2,1)}), bf16[64,16,128]{2,1,0:T(8,128)(2,1)S(1)}, u32[]{:S(2)}, u32[]{:S(2)}) async-start(bf16[64,16,128]{2,1,0:T(8,128)(2,1)} %gather_rows.1), calls=%async_computation | async-start | bytes 524288 | tf_op jit(solution)/shard_map/all_to_all | solution.py:363
  21.1 10.8 %all-to-all-done.recv_ref = bf16[64,16,128]{2,1,0:T(8,128)(2,1)S(1)} async-done(((bf16[64,16,128]{2,1,0:T(8,128)(2,1)}), bf16[64,16,128]{2,1,0:T(8,128)(2,1)S(1)}, u32[]{:S(2)}, u32[]{:S(2)}) %all-to-all-start) | async-done | bytes 262176 | tf_op jit(solution)/shard_map/all_to_all | solution.py:363
  32.8 15.0 %agg_one.1 = (bf16[64,16,128]{2,1,0:T(8,128)(2,1)}, bf16[32,1024]{1,0:T(8,128)(2,1)S(1)}, bf16[32,1024]{1,0:T(8,128)(2,1)S(1)}, bf16[32,1024]{1,0:T(8,128)(2,1)S(1)}, bf16[32,1024]{1,0:T(8,128)(2,1)S(1)}) custom-call(s32[32,10]{1,0:T(8,128)S(1)} %copy.20.cols_ref, s32[1]{0:T(128)} %bitcast.me_ref, bf16[32,4096]{1,0:T(8,128)(2,1)S(1)} %bitcast.14, ...), custom_call_target="tpu_custom_call" | custom-call | flops 2684354560 | bytes 11534336 | tf_op jit(solution)/shard_map/agg_one/pallas_call | solution.py:187
  47.8 6.5 %all-to-all-start.1 = ((bf16[64,16,128]{2,1,0:T(8,128)(2,1)}), bf16[64,16,128]{2,1,0:T(8,128)(2,1)S(1)}, u32[]{:S(2)}, u32[]{:S(2)}) async-start(bf16[64,16,128]{2,1,0:T(8,128)(2,1)} %get-tuple-element.26), calls=%async_computation.1 | async-start | bytes 524288 | tf_op jit(solution)/shard_map/all_to_all | solution.py:368
  54.3 8.6 %agg_transposed.1 = (bf16[48,2048]{1,0:T(8,128)(2,1)S(1)}, bf16[48,2048]{1,0:T(8,128)(2,1)S(1)}, bf16[48,2048]{1,0:T(8,128)(2,1)S(1)}, bf16[48,2048]{1,0:T(8,128)(2,1)S(1)}) custom-call(s32[32,10]{1,0:T(8,128)S(1)} %copy.20.cols_ref, s32[1]{0:T(128)} %bitcast.me_ref, bf16[48,4096]{1,0:T(8,128)(2,1)S(1)} %pad.8.grad_ref, bf16[32,10,128,128]{3,2,1,0:T(8,128)(2,1)} %vals_ref.5), custom_call_target="tpu_custom_call" | custom-call | flops 2013265920 | bytes 11534336 | tf_op jit(solution)/shard_map/agg_transposed/pallas_call | solution.py:128
  64.6 2.9 %collective-permute-start.7 = (bf16[48,2048]{1,0:T(8,128)(2,1)S(1)}, bf16[48,2048]{1,0:T(8,128)(2,1)S(1)}, u32[]{:S(2)}, u32[]{:S(2)}) collective-permute-start(bf16[48,2048]{1,0:T(8,128)(2,1)S(1)} %get-tuple-element.29), channel_id=1, source_target_pairs={{0,2},{1,3},{2,0},{3,1},{4,6},{5,7},{6,4},{7,5},{8,10},{9,11},{10,... | collective-permute-start | bytes 589832 | tf_op jit(solution)/shard_map/ppermute | solution.py:333
  68.1 4.1 %collective-permute-start.1 = (bf16[32,1024]{1,0:T(8,128)(2,1)S(1)}, bf16[32,1024]{1,0:T(8,128)(2,1)S(1)}, u32[]{:S(2)}, u32[]{:S(2)}) collective-permute-start(bf16[32,1024]{1,0:T(8,128)(2,1)S(1)} %get-tuple-element.24), channel_id=1, source_target_pairs={{0,2},{1,3},{2,0},{3,1},{4,6},{5,7},{6,4},{7,5},{8,10},{9,11},{10,... | collective-permute-start | bytes 196616 | tf_op jit(solution)/shard_map/ppermute | solution.py:333
  73.8 3.7 %collective-permute-done.7.refs_10_ = bf16[48,2048]{1,0:T(8,128)(2,1)S(1)} collective-permute-done((bf16[48,2048]{1,0:T(8,128)(2,1)S(1)}, bf16[48,2048]{1,0:T(8,128)(2,1)S(1)}, u32[]{:S(2)}, u32[]{:S(2)}) %collective-permute-start.7) | collective-permute-done | bytes 196640 | tf_op jit(solution)/shard_map/ppermute | solution.py:333
  77.7 4.1 %collective-permute-done.8.refs_11_ = bf16[48,2048]{1,0:T(8,128)(2,1)S(1)} collective-permute-done((bf16[48,2048]{1,0:T(8,128)(2,1)S(1)}, bf16[48,2048]{1,0:T(8,128)(2,1)S(1)}, u32[]{:S(2)}, u32[]{:S(2)}) %collective-permute-start.8) | collective-permute-done | bytes 196640 | tf_op jit(solution)/shard_map/ppermute | solution.py:333
  83.5 4.1 %collective-permute-done.4.refs_6_ = bf16[16,16,128]{2,1,0:T(8,128)(2,1)S(1)} collective-permute-done((bf16[16,16,128]{2,1,0:T(8,128)(2,1)S(1)}, bf16[16,16,128]{2,1,0:T(8,128)(2,1)S(1)}, u32[]{:S(2)}, u32[]{:S(2)}) %collective-permute-start.4) | collective-permute-done | bytes 65568 | tf_op jit(solution)/shard_map/ppermute | solution.py:333
  87.6 3.0 %dense.1 = (bf16[48,2048]{1,0:T(8,128)(2,1)S(1)}, bf16[48,2048]{1,0:T(8,128)(2,1)S(1)}, bf16[48,2048]{1,0:T(8,128)(2,1)S(1)}, bf16[48,2048]{1,0:T(8,128)(2,1)S(1...) custom-call(s32[1]{0:T(128)} %bitcast.me_ref, ...), custom_call_target="tpu_custom_call" | custom-call | flops 1572864000 | bytes 4194304 | tf_op jit(solution)/shard_map/dense/pallas_call | solution.py:249
  90.7 2.7 %collective-permute-start.13 = (f32[160,128]{1,0:T(8,128)S(1)}, f32[160,128]{1,0:T(8,128)S(1)}, u32[]{:S(2)}, u32[]{:S(2)}) collective-permute-start(f32[160,128]{1,0:T(8,128)S(1)} %get-tuple-element.37), channel_id=1, source_target_pairs={{0,2},{1,3},{2,0},{3,1},{4,6},{5,7},{6,4},{7,5},{8,10},{9,11},{10,... | collective-permute-start | bytes 245768 | tf_op jit(solution)/shard_map/ppermute | solution.py:333
  93.4 2.0 %collective-permute-start.14 = (f32[160,128]{1,0:T(8,128)S(1)}, f32[160,128]{1,0:T(8,128)S(1)}, u32[]{:S(2)}, u32[]{:S(2)}) collective-permute-start(f32[160,128]{1,0:T(8,128)S(1)} %get-tuple-element.38), channel_id=1, source_target_pairs={{0,3},{1,2},{2,1},{3,0},{4,7},{5,6},{6,5},{7,4},{8,11},{9,10},{10,... | collective-permute-start | bytes 245768 | tf_op jit(solution)/shard_map/ppermute | solution.py:333
  96.9 2.2 %collective-permute-done.14 = f32[160,128]{1,0:T(8,128)S(1)} collective-permute-done((f32[160,128]{1,0:T(8,128)S(1)}, f32[160,128]{1,0:T(8,128)S(1)}, u32[]{:S(2)}, u32[]{:S(2)}) %collective-permute-start.14) | collective-permute-done | bytes 81952 | tf_op jit(solution)/shard_map/ppermute | solution.py:333
  105.1 3.8 %collective-permute-done.17 = f32[160,128]{1,0:T(8,128)S(1)} collective-permute-done((f32[160,128]{1,0:T(8,128)S(1)}, f32[160,128]{1,0:T(8,128)S(1)}, u32[]{:S(2)}, u32[]{:S(2)}) %collective-permute-start.17) | collective-permute-done | bytes 81952 | tf_op jit(solution)/shard_map/ppermute | solution.py:333
  110.8 3.0 %collective-permute-start.10 = (bf16[48,2048]{1,0:T(8,128)(2,1)S(1)}, bf16[48,2048]{1,0:T(8,128)(2,1)S(1)}, u32[]{:S(2)}, u32[]{:S(2)}) collective-permute-start(bf16[48,2048]{1,0:T(8,128)(2,1)S(1)} %get-tuple-element.33), channel_id=1, source_target_pairs={{0,2},{1,3},{2,0},{3,1},{4,6},{5,7},{6,4},{7,5},{8,10},{9,11},{10,... | collective-permute-start | bytes 589832 | tf_op jit(solution)/shard_map/ppermute | solution.py:333
  115.1 2.5 %collective-permute-start.20 = (f32[160,128]{1,0:T(8,128)S(1)}, f32[160,128]{1,0:T(8,128)S(1)}, u32[]{:S(2)}, u32[]{:S(2)}) collective-permute-start(f32[160,128]{1,0:T(8,128)S(1)} %add.57), channel_id=1, source_target_pairs={{0,16},{4,20},{8,24},{12,28},{16,0},{20,4},{24,8},{28,12},{32,48},... | collective-permute-start | bytes 245768 | tf_op jit(solution)/shard_map/ppermute | solution.py:333
  117.6 3.8 %collective-permute-done.20 = f32[160,128]{1,0:T(8,128)S(1)} collective-permute-done((f32[160,128]{1,0:T(8,128)S(1)}, f32[160,128]{1,0:T(8,128)S(1)}, u32[]{:S(2)}, u32[]{:S(2)}) %collective-permute-start.20) | collective-permute-done | bytes 81952 | tf_op jit(solution)/shard_map/ppermute | solution.py:333
  121.4 3.8 %collective-permute-start.21 = (f32[160,128]{1,0:T(8,128)S(1)}, f32[160,128]{1,0:T(8,128)S(1)}, u32[]{:S(2)}, u32[]{:S(2)}) collective-permute-start(f32[160,128]{1,0:T(8,128)S(1)} %add.58), channel_id=1, source_target_pairs={{0,32},{4,36},{8,40},{12,44},{16,48},{20,52},{24,56},{28,60},{32,0... | collective-permute-start | bytes 245768 | tf_op jit(solution)/shard_map/ppermute | solution.py:333
  125.3 4.6 %collective-permute-done.21 = f32[160,128]{1,0:T(8,128)S(1)} collective-permute-done((f32[160,128]{1,0:T(8,128)S(1)}, f32[160,128]{1,0:T(8,128)S(1)}, u32[]{:S(2)}, u32[]{:S(2)}) %collective-permute-start.21) | collective-permute-done | bytes 81952 | tf_op jit(solution)/shard_map/ppermute | solution.py:333
  129.9 2.1 %collective-permute-start.24 = (f32[160,128]{1,0:T(8,128)S(1)}, f32[160,128]{1,0:T(8,128)S(1)}, u32[]{:S(2)}, u32[]{:S(2)}) collective-permute-start(f32[160,128]{1,0:T(8,128)S(1)} %add.59.g0), channel_id=1, source_target_pairs={{0,3},{1,2},{2,1},{3,0},{4,7},{5,6},{6,5},{7,4},{8,11},{9,10},{10,... | collective-permute-start | bytes 245768 | tf_op jit(solution)/shard_map/ppermute | solution.py:333
  132.0 2.1 %collective-permute-start.22 = (f32[160,128]{1,0:T(8,128)S(1)}, f32[160,128]{1,0:T(8,128)S(1)}, u32[]{:S(2)}, u32[]{:S(2)}) collective-permute-start(f32[160,128]{1,0:T(8,128)S(1)} %add.59.g0), channel_id=1, source_target_pairs={{0,1},{1,0},{2,3},{3,2},{4,5},{5,4},{6,7},{7,6},{8,9},{9,8},{10,11... | collective-permute-start | bytes 245768 | tf_op jit(solution)/shard_map/ppermute | solution.py:333
  134.1 10.0 %agg_two.1 = bf16[43,4096]{1,0:T(8,128)(2,1)} custom-call(s32[32,10]{1,0:T(8,128)S(1)} %copy.20.cols_ref, s32[1]{0:T(128)} %bitcast.me_ref, bf16[48,2048]{1,0:T(8,128)(2,1)S(1)} %get-tuple-element.31.y0, bf16[48,2048]{1,0:T(8,128)(2,1)S(1)} %collective-permute-done.9.y1, bf16[48,2048]{1,0:T(8,128)(2,1)S(1)} %collective-permute-done.10.y2, ...), custom_call_target="tpu_custom_call" | custom-call | flops 2013265920 | bytes 11534336 | tf_op jit(solution)/shard_map/agg_two/pallas_call | solution.py:288
  (61 shorter events, 21.0 us)
Async XLA Ops:
  8.3 23.6 %all-to-all-start = ((bf16[64,16,128]{2,1,0:T(8,128)(2,1)}), bf16[64,16,128]{2,1,0:T(8,128)(2,1)S(1)}, u32[]{:S(2)}, u32[]{:S(2)}) async-start(bf16[64,16,128]{2,1,0:T(8,128)(2,1)} %gather_rows.1), calls=%async_computation | async-start | bytes 524288 | tf_op jit(solution)/shard_map/all_to_all | solution.py:363
  47.8 24.4 %all-to-all-start.1 = ((bf16[64,16,128]{2,1,0:T(8,128)(2,1)}), bf16[64,16,128]{2,1,0:T(8,128)(2,1)S(1)}, u32[]{:S(2)}, u32[]{:S(2)}) async-start(bf16[64,16,128]{2,1,0:T(8,128)(2,1)} %get-tuple-element.26), calls=%async_computation.1 | async-start | bytes 524288 | tf_op jit(solution)/shard_map/all_to_all | solution.py:368
  62.9 9.3 %collective-permute-start.6 = (bf16[48,2048]{1,0:T(8,128)(2,1)S(1)}, bf16[48,2048]{1,0:T(8,128)(2,1)S(1)}, u32[]{:S(2)}, u32[]{:S(2)}) collective-permute-start(bf16[48,2048]{1,0:T(8,128)(2,1)S(1)} %get-tuple-element.28), channel_id=1, source_target_pairs={{0,1},{1,0},{2,3},{3,2},{4,5},{5,4},{6,7},{7,6},{8,9},{9,8},{10,11... | collective-permute-start | bytes 589832 | tf_op jit(solution)/shard_map/ppermute | solution.py:333
  64.6 12.9 %collective-permute-start.7 = (bf16[48,2048]{1,0:T(8,128)(2,1)S(1)}, bf16[48,2048]{1,0:T(8,128)(2,1)S(1)}, u32[]{:S(2)}, u32[]{:S(2)}) collective-permute-start(bf16[48,2048]{1,0:T(8,128)(2,1)S(1)} %get-tuple-element.29), channel_id=1, source_target_pairs={{0,2},{1,3},{2,0},{3,1},{4,6},{5,7},{6,4},{7,5},{8,10},{9,11},{10,... | collective-permute-start | bytes 589832 | tf_op jit(solution)/shard_map/ppermute | solution.py:333
  67.5 14.3 %collective-permute-start.8 = (bf16[48,2048]{1,0:T(8,128)(2,1)S(1)}, bf16[48,2048]{1,0:T(8,128)(2,1)S(1)}, u32[]{:S(2)}, u32[]{:S(2)}) collective-permute-start(bf16[48,2048]{1,0:T(8,128)(2,1)S(1)} %get-tuple-element.30), channel_id=1, source_target_pairs={{0,3},{1,2},{2,1},{3,0},{4,7},{5,6},{6,5},{7,4},{8,11},{9,10},{10,... | collective-permute-start | bytes 589832 | tf_op jit(solution)/shard_map/ppermute | solution.py:333
  67.7 14.1 %collective-permute-start = (bf16[32,1024]{1,0:T(8,128)(2,1)S(1)}, bf16[32,1024]{1,0:T(8,128)(2,1)S(1)}, u32[]{:S(2)}, u32[]{:S(2)}) collective-permute-start(bf16[32,1024]{1,0:T(8,128)(2,1)S(1)} %get-tuple-element.23), channel_id=1, source_target_pairs={{0,1},{1,0},{2,3},{3,2},{4,5},{5,4},{6,7},{7,6},{8,9},{9,8},{10,11... | collective-permute-start | bytes 196616 | tf_op jit(solution)/shard_map/ppermute | solution.py:333
  68.1 15.1 %collective-permute-start.1 = (bf16[32,1024]{1,0:T(8,128)(2,1)S(1)}, bf16[32,1024]{1,0:T(8,128)(2,1)S(1)}, u32[]{:S(2)}, u32[]{:S(2)}) collective-permute-start(bf16[32,1024]{1,0:T(8,128)(2,1)S(1)} %get-tuple-element.24), channel_id=1, source_target_pairs={{0,2},{1,3},{2,0},{3,1},{4,6},{5,7},{6,4},{7,5},{8,10},{9,11},{10,... | collective-permute-start | bytes 196616 | tf_op jit(solution)/shard_map/ppermute | solution.py:333
  72.2 11.0 %collective-permute-start.2 = (bf16[32,1024]{1,0:T(8,128)(2,1)S(1)}, bf16[32,1024]{1,0:T(8,128)(2,1)S(1)}, u32[]{:S(2)}, u32[]{:S(2)}) collective-permute-start(bf16[32,1024]{1,0:T(8,128)(2,1)S(1)} %get-tuple-element.25), channel_id=1, source_target_pairs={{0,3},{1,2},{2,1},{3,0},{4,7},{5,6},{6,5},{7,4},{8,11},{9,10},{10,... | collective-permute-start | bytes 196616 | tf_op jit(solution)/shard_map/ppermute | solution.py:333
  77.5 6.0 %collective-permute-start.5 = (bf16[16,16,128]{2,1,0:T(8,128)(2,1)S(1)}, bf16[16,16,128]{2,1,0:T(8,128)(2,1)S(1)}, u32[]{:S(2)}, u32[]{:S(2)}) collective-permute-start(bf16[16,16,128]{2,1,0:T(8,128)(2,1)S(1)} %get-tuple-element.41), channel_id=1, source_target_pairs={{0,3},{1,2},{2,1},{3,0},{4,7},{5,6},{6,5},{7,4},{8,11},{9,10},{10,... | collective-permute-start | bytes 196616 | tf_op jit(solution)/shard_map/ppermute | solution.py:333
  81.8 5.8 %collective-permute-start.4 = (bf16[16,16,128]{2,1,0:T(8,128)(2,1)S(1)}, bf16[16,16,128]{2,1,0:T(8,128)(2,1)S(1)}, u32[]{:S(2)}, u32[]{:S(2)}) collective-permute-start(bf16[16,16,128]{2,1,0:T(8,128)(2,1)S(1)} %get-tuple-element.42), channel_id=1, source_target_pairs={{0,2},{1,3},{2,0},{3,1},{4,6},{5,7},{6,4},{7,5},{8,10},{9,11},{10,... | collective-permute-start | bytes 196616 | tf_op jit(solution)/shard_map/ppermute | solution.py:333
  81.8 5.8 %collective-permute-start.3 = (bf16[16,16,128]{2,1,0:T(8,128)(2,1)S(1)}, bf16[16,16,128]{2,1,0:T(8,128)(2,1)S(1)}, u32[]{:S(2)}, u32[]{:S(2)}) collective-permute-start(bf16[16,16,128]{2,1,0:T(8,128)(2,1)S(1)} %get-tuple-element.43), channel_id=1, source_target_pairs={{0,1},{1,0},{2,3},{3,2},{4,5},{5,4},{6,7},{7,6},{8,9},{9,8},{10,11... | collective-permute-start | bytes 196616 | tf_op jit(solution)/shard_map/ppermute | solution.py:333
  90.7 6.2 %collective-permute-start.13 = (f32[160,128]{1,0:T(8,128)S(1)}, f32[160,128]{1,0:T(8,128)S(1)}, u32[]{:S(2)}, u32[]{:S(2)}) collective-permute-start(f32[160,128]{1,0:T(8,128)S(1)} %get-tuple-element.37), channel_id=1, source_target_pairs={{0,2},{1,3},{2,0},{3,1},{4,6},{5,7},{6,4},{7,5},{8,10},{9,11},{10,... | collective-permute-start | bytes 245768 | tf_op jit(solution)/shard_map/ppermute | solution.py:333
  93.4 5.7 %collective-permute-start.14 = (f32[160,128]{1,0:T(8,128)S(1)}, f32[160,128]{1,0:T(8,128)S(1)}, u32[]{:S(2)}, u32[]{:S(2)}) collective-permute-start(f32[160,128]{1,0:T(8,128)S(1)} %get-tuple-element.38), channel_id=1, source_target_pairs={{0,3},{1,2},{2,1},{3,0},{4,7},{5,6},{6,5},{7,4},{8,11},{9,10},{10,... | collective-permute-start | bytes 245768 | tf_op jit(solution)/shard_map/ppermute | solution.py:333
  102.1 6.7 %collective-permute-start.17 = (f32[160,128]{1,0:T(8,128)S(1)}, f32[160,128]{1,0:T(8,128)S(1)}, u32[]{:S(2)}, u32[]{:S(2)}) collective-permute-start(f32[160,128]{1,0:T(8,128)S(1)} %add.53), channel_id=1, source_target_pairs={{0,128},{4,132},{8,136},{12,140},{16,144},{20,148},{24,152},{28,15... | collective-permute-start | bytes 245768 | tf_op jit(solution)/shard_map/ppermute | solution.py:333
  103.0 5.9 %collective-permute-start.16 = (f32[160,128]{1,0:T(8,128)S(1)}, f32[160,128]{1,0:T(8,128)S(1)}, u32[]{:S(2)}, u32[]{:S(2)}) collective-permute-start(f32[160,128]{1,0:T(8,128)S(1)} %add.53), channel_id=1, source_target_pairs={{0,64},{4,68},{8,72},{12,76},{16,80},{20,84},{24,88},{28,92},{32,9... | collective-permute-start | bytes 245768 | tf_op jit(solution)/shard_map/ppermute | solution.py:333
  108.8 6.3 %collective-permute-start.19 = (f32[160,128]{1,0:T(8,128)S(1)}, f32[160,128]{1,0:T(8,128)S(1)}, u32[]{:S(2)}, u32[]{:S(2)}) collective-permute-start(f32[160,128]{1,0:T(8,128)S(1)} %add_add_fusion), channel_id=1, source_target_pairs={{0,8},{4,12},{8,0},{12,4},{16,24},{20,28},{24,16},{28,20},{32,40},... | collective-permute-start | bytes 245768 | tf_op jit(solution)/shard_map/ppermute | solution.py:333
  110.4 21.6 %collective-permute-start.9 = (bf16[48,2048]{1,0:T(8,128)(2,1)S(1)}, bf16[48,2048]{1,0:T(8,128)(2,1)S(1)}, u32[]{:S(2)}, u32[]{:S(2)}) collective-permute-start(bf16[48,2048]{1,0:T(8,128)(2,1)S(1)} %get-tuple-element.32), channel_id=1, source_target_pairs={{0,1},{1,0},{2,3},{3,2},{4,5},{5,4},{6,7},{7,6},{8,9},{9,8},{10,11... | collective-permute-start | bytes 589832 | tf_op jit(solution)/shard_map/ppermute | solution.py:333
  110.8 23.3 %collective-permute-start.10 = (bf16[48,2048]{1,0:T(8,128)(2,1)S(1)}, bf16[48,2048]{1,0:T(8,128)(2,1)S(1)}, u32[]{:S(2)}, u32[]{:S(2)}) collective-permute-start(bf16[48,2048]{1,0:T(8,128)(2,1)S(1)} %get-tuple-element.33), channel_id=1, source_target_pairs={{0,2},{1,3},{2,0},{3,1},{4,6},{5,7},{6,4},{7,5},{8,10},{9,11},{10,... | collective-permute-start | bytes 589832 | tf_op jit(solution)/shard_map/ppermute | solution.py:333
  113.9 20.3 %collective-permute-start.11 = (bf16[48,2048]{1,0:T(8,128)(2,1)S(1)}, bf16[48,2048]{1,0:T(8,128)(2,1)S(1)}, u32[]{:S(2)}, u32[]{:S(2)}) collective-permute-start(bf16[48,2048]{1,0:T(8,128)(2,1)S(1)} %get-tuple-element.34), channel_id=1, source_target_pairs={{0,3},{1,2},{2,1},{3,0},{4,7},{5,6},{6,5},{7,4},{8,11},{9,10},{10,... | collective-permute-start | bytes 589832 | tf_op jit(solution)/shard_map/ppermute | solution.py:333
  115.1 6.3 %collective-permute-start.20 = (f32[160,128]{1,0:T(8,128)S(1)}, f32[160,128]{1,0:T(8,128)S(1)}, u32[]{:S(2)}, u32[]{:S(2)}) collective-permute-start(f32[160,128]{1,0:T(8,128)S(1)} %add.57), channel_id=1, source_target_pairs={{0,16},{4,20},{8,24},{12,28},{16,0},{20,4},{24,8},{28,12},{32,48},... | collective-permute-start | bytes 245768 | tf_op jit(solution)/shard_map/ppermute | solution.py:333
  121.4 8.5 %collective-permute-start.21 = (f32[160,128]{1,0:T(8,128)S(1)}, f32[160,128]{1,0:T(8,128)S(1)}, u32[]{:S(2)}, u32[]{:S(2)}) collective-permute-start(f32[160,128]{1,0:T(8,128)S(1)} %add.58), channel_id=1, source_target_pairs={{0,32},{4,36},{8,40},{12,44},{16,48},{20,52},{24,56},{28,60},{32,0... | collective-permute-start | bytes 245768 | tf_op jit(solution)/shard_map/ppermute | solution.py:333
  129.9 14.2 %collective-permute-start.24 = (f32[160,128]{1,0:T(8,128)S(1)}, f32[160,128]{1,0:T(8,128)S(1)}, u32[]{:S(2)}, u32[]{:S(2)}) collective-permute-start(f32[160,128]{1,0:T(8,128)S(1)} %add.59.g0), channel_id=1, source_target_pairs={{0,3},{1,2},{2,1},{3,0},{4,7},{5,6},{6,5},{7,4},{8,11},{9,10},{10,... | collective-permute-start | bytes 245768 | tf_op jit(solution)/shard_map/ppermute | solution.py:333
  132.0 12.2 %collective-permute-start.23 = (f32[160,128]{1,0:T(8,128)S(1)}, f32[160,128]{1,0:T(8,128)S(1)}, u32[]{:S(2)}, u32[]{:S(2)}) collective-permute-start(f32[160,128]{1,0:T(8,128)S(1)} %add.59.g0), channel_id=1, source_target_pairs={{0,2},{1,3},{2,0},{3,1},{4,6},{5,7},{6,4},{7,5},{8,10},{9,11},{10,... | collective-permute-start | bytes 245768 | tf_op jit(solution)/shard_map/ppermute | solution.py:333
  132.0 12.2 %collective-permute-start.22 = (f32[160,128]{1,0:T(8,128)S(1)}, f32[160,128]{1,0:T(8,128)S(1)}, u32[]{:S(2)}, u32[]{:S(2)}) collective-permute-start(f32[160,128]{1,0:T(8,128)S(1)} %add.59.g0), channel_id=1, source_target_pairs={{0,1},{1,0},{2,3},{3,2},{4,5},{5,4},{6,7},{7,6},{8,9},{9,8},{10,11... | collective-permute-start | bytes 245768 | tf_op jit(solution)/shard_map/ppermute | solution.py:333
  (8 other events, 164.8 us)

commit v2 on v1

v2 whole, which is shorter than its diff:
```python
import functools

import jax
import jax.numpy as jnp
from jax import lax
from jax.experimental import pallas as pl
from jax.experimental.pallas import tpu as pltpu
from jax.sharding import PartitionSpec as P

BF = jnp.bfloat16
F32 = jnp.float32
VMEM = pltpu.VMEM
LIMIT = 24 * 1024 * 1024
LARGE = 48 * 1024 * 1024
NT = (((1,), (1,)), ((), ()))
NN = (((1,), (0,)), ((), ()))


def dot(a, b, dims=NN):
    return lax.dot_general(a, b, dims, preferred_element_type=F32)


def params(limit=LIMIT):
    return pltpu.CompilerParams(vmem_limit_bytes=limit)


def cost(flops, nbytes):
    return pl.CostEstimate(flops=flops, bytes_accessed=nbytes, transcendentals=0)


def whole():
    return pl.BlockSpec(memory_space=VMEM)


def gather_packed(stack_ref, idx_ref, out_ref, cols):
    chunks = stack_ref.shape[0] // cols
    lanes = stack_ref.shape[1]
    row_ids = lax.broadcasted_iota(jnp.int32, (lanes, 256), 0)
    low = lax.broadcasted_iota(jnp.int32, (16, 128), 1) < 64

    def step(j, carry):
        idx = idx_ref[pl.ds(j, 1), :]
        hot = (row_ids == (idx & (lanes - 1))).astype(BF)
        part = idx >> (lanes.bit_length() - 1)
        got = jnp.zeros((cols, 256), F32)
        wide = dot(stack_ref[...], hot)
        for c in range(chunks):
            got = jnp.where(part == c, wide[c * cols : (c + 1) * cols], got)
        for pair in range(2):
            top = got[:16, pair * 128 : (pair + 1) * 128]
            bottom = got[16:, pair * 128 : (pair + 1) * 128]
            first = jnp.where(low, top, pltpu.roll(bottom, 64, 1))
            second = jnp.where(low, pltpu.roll(top, 64, 1), bottom)
            out_ref[j * 4 + pair * 2] = first.astype(BF)
            out_ref[j * 4 + pair * 2 + 1] = second.astype(BF)
        return carry

    lax.fori_loop(0, idx_ref.shape[0], step, 0, unroll=8)


def unpack_pair(first, second):
    low = lax.broadcasted_iota(jnp.int32, (16, 128), 1) < 64
    first, second = first.astype(F32), second.astype(F32)
    top = jnp.where(low, first, pltpu.roll(second, 64, 1))
    bottom = jnp.where(low, pltpu.roll(first, 64, 1), second)
    return jnp.concatenate([top, bottom], axis=0).astype(BF)


def fill_stack(stack_ref, panel_ref):
    cols, rows = panel_ref.shape
    for c in range(rows // 256):
        stack_ref[c * cols : (c + 1) * cols, :] = panel_ref[:, c * 256 : (c + 1) * 256]


def gather_kernel(panel_ref, idx_ref, out_ref, stack_ref):
    fill_stack(stack_ref, panel_ref)
    gather_packed(stack_ref, idx_ref, out_ref, panel_ref.shape[0])


def gather_call(panel, idx):
    cols, rows = panel.shape
    pieces = idx.size // 64
    return pl.pallas_call(
        gather_kernel,
        out_shape=jax.ShapeDtypeStruct((pieces, 16, 128), BF),
        in_specs=[whole(), whole()],
        out_specs=whole(),
        scratch_shapes=[VMEM((rows // 256 * cols, 256), BF)],
        compiler_params=params(),
        cost_estimate=cost(2 * 512 * 256 * 4096, 1 << 20),
        name="gather_rows",
    )(panel, idx)


def smem():
    return pl.BlockSpec(memory_space=pltpu.SMEM)


UNROLL = 8


def anywhere():
    return pl.BlockSpec(memory_space=pl.ANY)


def held_scratch(vals, group):
    return [VMEM(vals.shape, vals.dtype), pltpu.SemaphoreType.DMA((vals.shape[0] // group,))]


def fetch(vals_ref, held, sems, s, group, first=0):
    return pltpu.make_async_copy(
        vals_ref.at[pl.ds(first + s * group, group)], held.at[pl.ds(s * group, group)], sems.at[s]
    )


def transpose_agg_kernel(cols_ref, me_ref, grad_ref, vals_ref, o0, o1, o2, o3, acc, held, sems):
    row_tiles, tiles = vals_ref.shape[:2]
    classes = grad_ref.shape[0]
    for s in range(row_tiles // UNROLL):
        fetch(vals_ref, held, sems, s, UNROLL).start()
    acc[...] = jnp.zeros_like(acc)

    def body(s, carry):
        fetch(vals_ref, held, sems, s, UNROLL).wait()
        for r in range(UNROLL):
            t = s * UNROLL + r
            slab = grad_ref[:, pl.ds(pl.multiple_of(t * 128, 128), 128)]
            side = jnp.concatenate([held[t, k] for k in range(tiles)], axis=1)
            part = dot(slab, side)
            for k in range(tiles):
                acc[cols_ref[k, t], :classes] += part[:, k * 128 : (k + 1) * 128]
        return carry

    lax.fori_loop(0, row_tiles // UNROLL, body, 0)
    me = me_ref[0]
    for d, out in enumerate((o0, o1, o2, o3)):
        chunk = (me ^ d) * 8
        for j in range(8):
            out[:, j * 128 : (j + 1) * 128] = acc[chunk + j].astype(BF)
            out[:, (8 + j) * 128 : (9 + j) * 128] = acc[32 + chunk + j].astype(BF)


def transpose_agg_call(grad, cols, vals, me):
    width = 48
    return pl.pallas_call(
        transpose_agg_kernel,
        out_shape=(jax.ShapeDtypeStruct((width, 2048), BF),) * 4,
        in_specs=[smem(), smem(), whole(), anywhere()],
        out_specs=[whole()] * 4,
        scratch_shapes=[VMEM((64, width, 128), F32)] + held_scratch(vals, UNROLL),
        compiler_params=params(LARGE),
        cost_estimate=cost(2 * 48 * 128 * 128 * 320 * 4, 11 << 20),
        name="agg_transposed",
    )(cols, me, grad, vals)


def agg_tile(t, place, cols_ref, ext, held):
    tiles = held.shape[1]
    left = jnp.concatenate([held[place, k] for k in range(tiles)], axis=1)
    right = jnp.concatenate([ext[cols_ref[k, t]] for k in range(tiles)], axis=1)
    return dot(left, right, NT).T.astype(BF)


def agg_one_kernel(
    cols_ref, me_ref, panel_ref, recv_ref, idx_ref, vals_ref, packed_ref, o0, o1, o2, o3, ext, stack, held, sems
):
    row_tiles = vals_ref.shape[0]
    for s in range(row_tiles // UNROLL):
        fetch(vals_ref, held, sems, s, UNROLL).start()
    for e in range(32):
        ext[e] = panel_ref[:, e * 128 : (e + 1) * 128]
        ext[32 + e] = unpack_pair(recv_ref[2 * e], recv_ref[2 * e + 1])

    def body(s, carry):
        fetch(vals_ref, held, sems, s, UNROLL).wait()
        for r in range(UNROLL):
            place = pl.multiple_of((s * (UNROLL // 2) + r // 2) * 32, 32)
            total = agg_tile(s * UNROLL + r, s * UNROLL + r, cols_ref, ext, held)
            stack[pl.ds(place, 32), (r % 2) * 128 : (r % 2 + 1) * 128] = total
        return carry

    lax.fori_loop(0, row_tiles // UNROLL, body, 0)
    gather_packed(stack, idx_ref, packed_ref, 32)
    me = me_ref[0]
    for d, out in enumerate((o0, o1, o2, o3)):
        for j in range(4):
            place = pl.multiple_of(((me ^ d) * 4 + j) * 32, 32)
            out[:, j * 256 : (j + 1) * 256] = stack[pl.ds(place, 32), :]


def agg_one_call(panel, received, idx, cols, vals, me):
    pieces = received.shape[0]
    out = jax.ShapeDtypeStruct((32, 1024), BF)
    return pl.pallas_call(
        agg_one_kernel,
        out_shape=(jax.ShapeDtypeStruct((pieces, 16, 128), BF),) + (out,) * 4,
        in_specs=[smem(), smem(), whole(), whole(), whole(), anywhere()],
        out_specs=[whole()] * 5,
        scratch_shapes=[VMEM((64, 32, 128), BF), VMEM((512, 256), BF)] + held_scratch(vals, UNROLL),
        compiler_params=params(LARGE),
        cost_estimate=cost(2 * 32 * 128 * 128 * 320 * 8, 11 << 20),
        name="agg_one",
    )(cols, me, panel, received, idx, vals)


def dense_body(mix, zed, w1t, w2, w2t, hid, gp, yall):
    rows = mix.shape[1]
    for c in range(rows // 256):
        lanes = slice(c * 256, (c + 1) * 256)
        pre = dot(w1t[...], mix[:, lanes])
        gate = 1.0 / (1.0 + jnp.exp(-pre))
        hidden = (pre * gate).astype(BF)
        hid[:, lanes] = hidden
        yall[:, lanes] = dot(w2t[...], hidden).astype(BF)
        gh = dot(w2[...], zed[:, lanes])
        gp[:, lanes] = (gh * gate * (1.0 + pre * (1.0 - gate))).astype(BF)
    return dot(mix[...], gp[...], NT), dot(zed[...], hid[...], NT)


def dense_own_kernel(me_ref, *refs):
    own, zs = refs[0:4], refs[4:8]
    w1t, w2, w2t = refs[8:11]
    yall, p1_ref, p2_ref = refs[11:14]
    mix, zed, hid, gp = refs[14:18]
    me = me_ref[0]
    for d in range(4):
        f = me ^ d
        mix[pl.ds(pl.multiple_of(f * 32, 32), 32), :] = own[d][...]
        zed[pl.ds(pl.multiple_of(f * 48, 16), 48), :] = zs[d][:, :1024]
    p1, p2 = dense_body(mix, zed, w1t, w2, w2t, hid, gp, yall)
    p1_ref[...] = p1
    p2_ref[...] = p2


def dense_far_kernel(me_ref, *refs):
    far, zs = refs[0:4], refs[4:8]
    w1t, w2, w2t, y_own, p1_ref, p2_ref = refs[8:14]
    ys, gs = refs[14:18], refs[18:22]
    mix, zed, hid, gp, yall, gall = refs[22:28]
    me = me_ref[0]
    for d in range(4):
        f = me ^ d
        at = pl.multiple_of(f * 32, 32)
        for e in range(8):
            mix[pl.ds(at, 32), e * 128 : (e + 1) * 128] = unpack_pair(far[d][2 * e], far[d][2 * e + 1])
        zed[pl.ds(pl.multiple_of(f * 48, 16), 48), :] = zs[d][:, 1024:]
    p1, p2 = dense_body(mix, zed, w1t, w2, w2t, hid, gp, yall)
    for d in range(4):
        place = pl.ds(pl.multiple_of((me ^ d) * 48, 16), 48)
        ys[d][:, :1024] = y_own[place, :]
        ys[d][:, 1024:] = yall[place, :]
    p1 = p1 + p1_ref[...]
    p2 = p2 + p2_ref[...]
    gall[0:128] = p1[:, :128]
    gall[128:256] = p1[:, 128:]
    gall[256:448] = p2[:, :128]
    gall[448:640] = p2[:, 128:]
    for d in range(4):
        gs[d][...] = gall[pl.ds(pl.multiple_of((me ^ d) * 160, 8), 160), :]


def dense_scratch():
    return [
        VMEM((128, 1024), BF),
        VMEM((192, 1024), BF),
        VMEM((256, 1024), BF),
        VMEM((256, 1024), BF),
    ]


def dense_own_call(me, own, zs, w1t, w2, w2t):
    return pl.pallas_call(
        dense_own_kernel,
        out_shape=(
            jax.ShapeDtypeStruct((192, 1024), BF),
            jax.ShapeDtypeStruct((128, 256), F32),
            jax.ShapeDtypeStruct((192, 256), F32),
        ),
        in_specs=[smem()] + [whole()] * 11,
        out_specs=[whole()] * 3,
        scratch_shapes=dense_scratch(),
        compiler_params=params(),
        cost_estimate=cost(2 * 1024 * 256 * 1500, 4 << 20),
        name="dense_own",
    )(me, *own, *zs, w1t, w2, w2t)


def dense_far_call(me, far, zs, w1t, w2, w2t, y_own, p1, p2):
    return pl.pallas_call(
        dense_far_kernel,
        out_shape=(jax.ShapeDtypeStruct((48, 2048), BF),) * 4
        + (jax.ShapeDtypeStruct((160, 128), F32),) * 4,
        in_specs=[smem()] + [whole()] * 14,
        out_specs=[whole()] * 8,
        scratch_shapes=dense_scratch() + [VMEM((192, 1024), BF), VMEM((640, 128), F32)],
        compiler_params=params(),
        cost_estimate=cost(2 * 1024 * 256 * 1500, 4 << 20),
        name="dense_far",
    )(me, *far, *zs, w1t, w2, w2t, y_own, p1, p2)


def spread_kernel(me_ref, *refs):
    ext = refs[4]
    me = me_ref[0]
    for d in range(4):
        chunk = (me ^ d) * 8
        for j in range(8):
            ext[chunk + j] = refs[d][:, j * 128 : (j + 1) * 128]
            ext[32 + chunk + j] = refs[d][:, (8 + j) * 128 : (9 + j) * 128]


def spread_call(me, ys):
    return pl.pallas_call(
        spread_kernel,
        out_shape=jax.ShapeDtypeStruct((64, 48, 128), BF),
        in_specs=[smem()] + [whole()] * 4,
        out_specs=whole(),
        compiler_params=params(),
        cost_estimate=cost(0, 100 << 20),
        name="spread",
    )(me, *ys)


def agg_two_call(first, count, ext, cols, vals, classes):
    def kernel(cols_ref, ext_ref, vals_ref, out_ref):
        for r in range(count):
            total = agg_tile(first + r, first + r, cols_ref, ext_ref, vals_ref)
            out_ref[:, r * 128 : (r + 1) * 128] = total[:classes]

    return pl.pallas_call(
        kernel,
        out_shape=jax.ShapeDtypeStruct((classes, count * 128), BF),
        in_specs=[smem(), whole(), whole()],
        out_specs=whole(),
        compiler_params=params(),
        cost_estimate=cost(2 * 48 * 128 * 128 * 10 * count * 4, count * 330000),
        name="agg_two",
    )(cols, ext, vals)


def finish_kernel(me_ref, g0, g1, g2, g3, one_ref, two_ref, buf):
    me = me_ref[0]
    for d, g in enumerate((g0, g1, g2, g3)):
        buf[pl.ds(pl.multiple_of((me ^ d) * 160, 8), 160), :] = g[...]
    one_ref[:, :128] = buf[0:128]
    one_ref[:, 128:] = buf[128:256]
    per = two_ref.shape[0] // 4
    for f in range(4):
        two_ref[f * per : (f + 1) * per, :128] = buf[256 + 48 * f : 256 + 48 * f + per]
        two_ref[f * per : (f + 1) * per, 128:] = buf[448 + 48 * f : 448 + 48 * f + per]


def finish_call(me, gs, classes):
    return pl.pallas_call(
        finish_kernel,
        out_shape=(
            jax.ShapeDtypeStruct((128, 256), F32),
            jax.ShapeDtypeStruct((classes, 256), F32),
        ),
        in_specs=[pl.BlockSpec(memory_space=pltpu.SMEM)] + [whole()] * 4,
        out_specs=[whole()] * 2,
        scratch_shapes=[VMEM((640, 128), F32)],
        compiler_params=params(),
        name="finish",
    )(me, *gs)


def swap(x, axis, size, mask):
    return lax.ppermute(x, axis, [(i, i ^ mask) for i in range(size)])


def after(x, *others):
    return lax.optimization_barrier((x, *others))[0]


def swap_sum(blocks, move):
    moved = [move(blocks[d], d) for d in (1, 2, 3)]
    return (blocks[0] + moved[0]) + (moved[1] + moved[2])


def on_device(
    features, weight_one, weight_two, grad_logits, send_idx, send_count, tile_cols, tile_vals
):
    partitions = lax.axis_size("dom")
    feat = lax.axis_size("feat")
    me = lax.axis_index("feat").astype(jnp.int32)
    me_arr = me.reshape(1)
    bound_rows = send_idx.shape[1]
    class_cols = grad_logits.shape[1]
    hidden = weight_one.shape[1]

    def swap_feat(x, d):
        return swap(x, "feat", feat, d)

    def swap_dom(x, mask):
        return swap(x, "dom", partitions, mask)

    live = jnp.arange(bound_rows, dtype=jnp.int32)[None, :] < send_count[:, None]
    idx = jnp.where(live, send_idx, -1).reshape(-1, 256)
    panel = features.T
    grad = grad_logits.T
    cols = tile_cols.T
    w2 = jnp.pad(weight_two.reshape(hidden, feat, class_cols), ((0, 0), (0, 0), (0, 48 - class_cols)))
    w2 = w2.reshape(hidden, feat * 48)
    w1t = weight_one.T
    w2t = w2.T

    packed_one = gather_call(panel, idx)
    received_one = lax.all_to_all(packed_one, "dom", split_axis=0, concat_axis=0, tiled=True)
    zs = transpose_agg_call(grad, cols, tile_vals, me_arr)
    received_one = after(received_one, zs[0])
    zs = [zs[0]] + [swap_feat(zs[d], d) for d in (1, 2, 3)]
    packed_two, *mixed = agg_one_call(panel, received_one, idx, cols, tile_vals, me_arr)
    packed_two = after(packed_two, *zs)
    received_two = lax.all_to_all(packed_two, "dom", split_axis=0, concat_axis=0, tiled=True)
    own = [mixed[0]] + [swap_feat(mixed[d], d) for d in (1, 2, 3)]
    pieces = partitions // feat

    def far_block(d):
        return lax.dynamic_slice_in_dim(received_two, (me ^ d) * pieces, pieces, 0)

    near = far_block(0)
    far = [near] + [swap_feat(far_block(d), d) for d in (1, 2, 3)]
    own[0] = after(own[0], near)
    y_own, p1, p2 = dense_own_call(me_arr, own, zs, w1t, w2, w2t)
    outs = dense_far_call(me_arr, far, zs, w1t, w2, w2t, y_own, p1, p2)
    ys, gs = outs[:4], outs[4:]
    total = swap_sum(gs, swap_feat)
    ys = [ys[0]] + [swap_feat(ys[d], d) for d in (1, 2, 3)]
    total = total + swap_dom(total, 1)
    total = swap_sum([total] * 4, lambda x, d: swap_dom(x, 16 * d))
    ext = spread_call(me_arr, ys)
    out = []
    row_tiles = tile_cols.shape[0]
    cuts = [0, row_tiles // 8, row_tiles * 9 // 16, row_tiles]

    def beside(moved):
        first, last = cuts[len(out) : len(out) + 2]
        out.append(agg_two_call(first, last - first, ext, cols, tile_vals, class_cols))
        *moved, out[-1] = lax.optimization_barrier((*moved, out[-1]))
        return moved

    ext, total = lax.optimization_barrier((ext, total))
    (moved,) = beside([swap_dom(total, 8)])
    total = total + moved
    ext, total = lax.optimization_barrier((ext, total))
    moved = beside([swap_dom(total, d) for d in (2, 4, 6)])
    total = (total + moved[0]) + (moved[1] + moved[2])
    ext, total = lax.optimization_barrier((ext, total))
    moved = beside([swap_feat(total, d) for d in (1, 2, 3)])
    logits = jnp.concatenate(out, axis=1)
    logits, *moved = lax.optimization_barrier((logits, *moved))
    grad_one, grad_two = finish_call(me_arr, [total] + moved, feat * class_cols)
    return (logits.T, grad_one, grad_two.T)


def solution(mesh):
    return jax.shard_map(
        on_device,
        mesh=mesh,
        in_specs=(
            P("dom", "feat"),
            P(),
            P(),
            P("dom", "feat"),
            P("dom", None),
            P("dom"),
            P("dom", None),
            P("dom", None, None, None),
        ),
        out_specs=(P("dom", "feat"), P(), P()),
        check_vma=False,
    )
```

time: 146 us -> 119 us (0.82)
  waiting for transfers between devices: 40.6 us -> 22.3 us
  Pallas kernels: 43.1 us -> 25.7 us
  starting transfers between devices: 56.4 us -> 60.8 us
  local copies, waits for them, and re-layouts: 3.07 us -> 6.98 us
    ppermute x25 -> x26, waiting for transfers between devices: 29.8 us -> 15.9 us  [swap(): return lax.ppermute(x, axis, [(i, i ^ mask) for i in range(size)])]
    all_to_all x1, waiting for transfers between devices: 10.8 us -> 0.01 us  [on_device(): lax.all_to_all(packed_one, 'dom', split_axis=0, concat_axis=0, tiled=True)]
    pallas_call x3 -> x7, Pallas kernels: 21.6 us -> 14.1 us  [the longest x1 5.53 us: transpose_agg_call(): pl.pallas_call(transpose_agg_kernel, out_shape=(jax.ShapeDtypeStruct((wid...]
    pallas_call x1, Pallas kernels: 15 us -> 8.39 us  [agg_one_call(): pl.pallas_call(agg_one_kernel, out_shape=(jax.ShapeDtypeStruct((pieces, 1...]
    all_to_all x1, waiting for transfers between devices: 0.01 us -> 6.42 us  [on_device(): lax.all_to_all(packed_two, 'dom', split_axis=0, concat_axis=0, tiled=True)]
    unnamed x12 -> x17, local copies, waits for them, and re-layouts: 2.8 us -> 6.75 us
    all_to_all x1, starting transfers between devices: 6.49 us -> 10.3 us  [on_device(): lax.all_to_all(packed_two, 'dom', split_axis=0, concat_axis=0, tiled=True)]
    pallas_call x1, Pallas kernels: 5.76 us -> 2.43 us  [gather_call(): pl.pallas_call(gather_kernel, out_shape=jax.ShapeDtypeStruct((pieces, 16,...]
  transfers between devices with their start and end apart: 27 -> 28, of which waited for: 12 -> 15; matrix products, arithmetic and copies ran while one was open for 1% -> 0% of each run, Pallas kernels for 13% -> 18%
where the time goes in v2:
time: 119 us; the launch traced here: 118 us
  starting transfers between devices  60.8 us (51%)
  Pallas kernels  25.7 us (22%)
  waiting for transfers between devices  22.3 us (19%)
  local copies, waits for them, and re-layouts  6.98 us (6%)
  other arithmetic  1.7 us (1%)
    ppermute x26, starting transfers between devices, swap(): return lax.ppermute(x, axis, [(i, i ^ mask) for i in range(size)])  38.5 us
    ppermute x26, waiting for transfers between devices, swap(): return lax.ppermute(x, axis, [(i, i ^ mask) for i in range(size)])  15.9 us
    all_to_all x1, starting transfers between devices, on_device(): lax.all_to_all(packed_one, 'dom', split_axis=0, concat_axis=0, tiled=True)  12 us
    all_to_all x1, starting transfers between devices, on_device(): lax.all_to_all(packed_two, 'dom', split_axis=0, concat_axis=0, tiled=True)  10.3 us
    pallas_call x1, Pallas kernels, agg_one_call(): pl.pallas_call(agg_one_kernel, out_shape=(jax.ShapeDtypeStruct((pieces, 1...  8.39 us
    unnamed x17, local copies, waits for them, and re-layouts  6.75 us
    all_to_all x1, waiting for transfers between devices, on_device(): lax.all_to_all(packed_two, 'dom', split_axis=0, concat_axis=0, tiled=True)  6.42 us
    pallas_call x1, Pallas kernels, transpose_agg_call(): pl.pallas_call(transpose_agg_kernel, out_shape=(jax.ShapeDtypeStruct((wid...  5.53 us
  transfers between devices with their start and end apart: 28, of which 15 were waited for; matrix products, arithmetic and copies ran while one was open for 0% of the time, Pallas kernels for 18%

profile of v2, /device:TPU:2, one launch (start us, length us, event | category | flops | bytes accessed | tf_op | source)
XLA Modules:
  0.0 118.3 jit_solution(11112962518162661128)
XLA Ops:
  2.5 2.4 %gather_rows.1 = bf16[64,16,128]{2,1,0:T(8,128)(2,1)} custom-call(bf16[32,4096]{1,0:T(8,128)(2,1)S(1)} %bitcast.16, s32[16,256]{1,0:T(8,128)S(1)} %reshape.20.idx_ref), custom_call_target="tpu_custom_call" | custom-call | flops 1073741824 | bytes 1048576 | tf_op jit(solution)/shard_map/gather_rows/pallas_call | solution.py:83
  4.9 12.0 %all-to-all-start = ((bf16[64,16,128]{2,1,0:T(8,128)(2,1)}), bf16[64,16,128]{2,1,0:T(8,128)(2,1)S(1)}, u32[]{:S(2)}, u32[]{:S(2)}) async-start(bf16[64,16,128]{2,1,0:T(8,128)(2,1)} %gather_rows.1), calls=%async_computation | async-start | bytes 524288 | tf_op jit(solution)/shard_map/all_to_all | solution.py:409
  18.7 5.5 %agg_transposed.1 = (bf16[48,2048]{1,0:T(8,128)(2,1)S(1)}, bf16[48,2048]{1,0:T(8,128)(2,1)S(1)}, bf16[48,2048]{1,0:T(8,128)(2,1)S(1)}, bf16[48,2048]{1,0:T(8,128)(2,1)S(1)}) custom-call(s32[10,32]{1,0:T(8,128)S(1)} %bitcast.18, s32[1]{0:T(128)} %bitcast.me_ref, bf16[43,4096]{1,0:T(8,128)(2,1)S(1)} %bitcast.12, bf16[32,10,128,128]{3,2,1,0:T(8,128)(2,1)} %vals_ref.9), custom_call_target="tpu_custom_call" | custom-call | flops 2013265920 | bytes 11534336 | tf_op jit(solution)/shard_map/agg_transposed/pallas_call | solution.py:145
  25.9 2.9 %collective-permute-start.1 = (bf16[48,2048]{1,0:T(8,128)(2,1)S(1)}, bf16[48,2048]{1,0:T(8,128)(2,1)S(1)}, u32[]{:S(2)}, u32[]{:S(2)}) collective-permute-start(bf16[48,2048]{1,0:T(8,128)(2,1)S(1)} %get-tuple-element.52), channel_id=1, source_target_pairs={{0,2},{1,3},{2,0},{3,1},{4,6},{5,7},{6,4},{7,5},{8,10},{9,11},{10,... | collective-permute-start | bytes 589832 | tf_op jit(solution)/shard_map/ppermute | solution.py:369
  29.0 8.4 %agg_one.1 = (bf16[64,16,128]{2,1,0:T(8,128)(2,1)}, bf16[32,1024]{1,0:T(8,128)(2,1)S(1)}, bf16[32,1024]{1,0:T(8,128)(2,1)S(1)}, bf16[32,1024]{1,0:T(8,128)(2,1)S(1)}, bf16[32,1024]{1,0:T(8,128)(2,1)S(1)}) custom-call(s32[10,32]{1,0:T(8,128)S(1)} %bitcast.19, s32[1]{0:T(128)} %bitcast.me_ref, bf16[32,4096]{1,0:T(8,128)(2,1)S(1)} %bitcast.17, ...), custom_call_target="tpu_custom_call" | custom-call | flops 2684354560 | bytes 11534336 | tf_op jit(solution)/shard_map/agg_one/pallas_call | solution.py:194
  38.0 2.6 %collective-permute-done.2.refs_7_ = bf16[48,2048]{1,0:T(8,128)(2,1)S(1)} collective-permute-done((bf16[48,2048]{1,0:T(8,128)(2,1)S(1)}, bf16[48,2048]{1,0:T(8,128)(2,1)S(1)}, u32[]{:S(2)}, u32[]{:S(2)}) %collective-permute-start.2) | collective-permute-done | bytes 196640 | tf_op jit(solution)/shard_map/ppermute | solution.py:369
  40.6 10.3 %all-to-all-start.1 = ((bf16[64,16,128]{2,1,0:T(8,128)(2,1)}), bf16[64,16,128]{2,1,0:T(8,128)(2,1)S(1)}, u32[]{:S(2)}, u32[]{:S(2)}) async-start(bf16[64,16,128]{2,1,0:T(8,128)(2,1)} %get-tuple-element.54), calls=%async_computation.1 | async-start | bytes 524288 | tf_op jit(solution)/shard_map/all_to_all | solution.py:415
  51.4 1.7 %collective-permute-start.7 = (bf16[32,1024]{1,0:T(8,128)(2,1)S(1)}, bf16[32,1024]{1,0:T(8,128)(2,1)S(1)}, u32[]{:S(2)}, u32[]{:S(2)}) collective-permute-start(bf16[32,1024]{1,0:T(8,128)(2,1)S(1)} %get-tuple-element.58), channel_id=1, source_target_pairs={{0,2},{1,3},{2,0},{3,1},{4,6},{5,7},{6,4},{7,5},{8,10},{9,11},{10,... | collective-permute-start | bytes 196616 | tf_op jit(solution)/shard_map/ppermute | solution.py:369
  53.1 3.0 %collective-permute-start.8 = (bf16[32,1024]{1,0:T(8,128)(2,1)S(1)}, bf16[32,1024]{1,0:T(8,128)(2,1)S(1)}, u32[]{:S(2)}, u32[]{:S(2)}) collective-permute-start(bf16[32,1024]{1,0:T(8,128)(2,1)S(1)} %get-tuple-element.59), channel_id=1, source_target_pairs={{0,3},{1,2},{2,1},{3,0},{4,7},{5,6},{6,5},{7,4},{8,11},{9,10},{10,... | collective-permute-start | bytes 196616 | tf_op jit(solution)/shard_map/ppermute | solution.py:369
  56.1 6.4 %all-to-all-done.1 = bf16[64,16,128]{2,1,0:T(8,128)(2,1)S(1)} async-done(((bf16[64,16,128]{2,1,0:T(8,128)(2,1)}), bf16[64,16,128]{2,1,0:T(8,128)(2,1)S(1)}, u32[]{:S(2)}, u32[]{:S(2)}) %all-to-all-start.1) | async-done | bytes 262176 | tf_op jit(solution)/shard_map/all_to_all | solution.py:415
  63.6 3.1 %collective-permute-start.3 = (bf16[16,16,128]{2,1,0:T(8,128)(2,1)S(1)}, bf16[16,16,128]{2,1,0:T(8,128)(2,1)S(1)}, u32[]{:S(2)}, u32[]{:S(2)}) collective-permute-start(bf16[16,16,128]{2,1,0:T(8,128)(2,1)S(1)} %get-tuple-element.95), channel_id=1, source_target_pairs={{0,1},{1,0},{2,3},{3,2},{4,5},{5,4},{6,7},{7,6},{8,9},{9,8},{10,11... | collective-permute-start | bytes 196616 | tf_op jit(solution)/shard_map/ppermute | solution.py:369
  72.7 2.4 %collective-permute-start.13 = (f32[160,128]{1,0:T(8,128)S(1)}, f32[160,128]{1,0:T(8,128)S(1)}, u32[]{:S(2)}, u32[]{:S(2)}) collective-permute-start(f32[160,128]{1,0:T(8,128)S(1)} %get-tuple-element.69), channel_id=1, source_target_pairs={{0,2},{1,3},{2,0},{3,1},{4,6},{5,7},{6,4},{7,5},{8,10},{9,11},{10,... | collective-permute-start | bytes 245768 | tf_op jit(solution)/shard_map/ppermute | solution.py:369
  76.4 3.4 %collective-permute-start.10 = (bf16[48,2048]{1,0:T(8,128)(2,1)S(1)}, bf16[48,2048]{1,0:T(8,128)(2,1)S(1)}, u32[]{:S(2)}, u32[]{:S(2)}) collective-permute-start(bf16[48,2048]{1,0:T(8,128)(2,1)S(1)} %get-tuple-element.65), channel_id=1, source_target_pairs={{0,2},{1,3},{2,0},{3,1},{4,6},{5,7},{6,4},{7,5},{8,10},{9,11},{10,... | collective-permute-start | bytes 589832 | tf_op jit(solution)/shard_map/ppermute | solution.py:369
  85.6 1.8 %collective-permute-start.16 = (f32[160,128]{1,0:T(8,128)S(1)}, f32[160,128]{1,0:T(8,128)S(1)}, u32[]{:S(2)}, u32[]{:S(2)}) collective-permute-start(f32[160,128]{1,0:T(8,128)S(1)} %add.54), channel_id=1, source_target_pairs={{0,64},{4,68},{8,72},{12,76},{16,80},{20,84},{24,88},{28,92},{32,9... | collective-permute-start | bytes 245768 | tf_op jit(solution)/shard_map/ppermute | solution.py:369
  87.3 1.9 %collective-permute-done.11.refs_3_ = bf16[48,2048]{1,0:T(8,128)(2,1)S(1)} collective-permute-done((bf16[48,2048]{1,0:T(8,128)(2,1)S(1)}, bf16[48,2048]{1,0:T(8,128)(2,1)S(1)}, u32[]{:S(2)}, u32[]{:S(2)}) %collective-permute-start.11) | collective-permute-done | bytes 196640 | tf_op jit(solution)/shard_map/ppermute | solution.py:369
  89.3 2.2 %collective-permute-done.17 = f32[160,128]{1,0:T(8,128)S(1)} collective-permute-done((f32[160,128]{1,0:T(8,128)S(1)}, f32[160,128]{1,0:T(8,128)S(1)}, u32[]{:S(2)}, u32[]{:S(2)}) %collective-permute-start.17) | collective-permute-done | bytes 81952 | tf_op jit(solution)/shard_map/ppermute | solution.py:369
  91.5 2.3 %collective-permute-start.19 = (f32[160,128]{1,0:T(8,128)S(1)}, f32[160,128]{1,0:T(8,128)S(1)}, u32[]{:S(2)}, u32[]{:S(2)}) collective-permute-start(f32[160,128]{1,0:T(8,128)S(1)} %add_add_fusion.1), channel_id=1, source_target_pairs={{0,32},{4,36},{8,40},{12,44},{16,48},{20,52},{24,56},{28,60},{32,0... | collective-permute-start | bytes 245768 | tf_op jit(solution)/shard_map/ppermute | solution.py:369
  93.8 4.0 %copy-done = bf16[32,10,128,128]{3,2,1,0:T(8,128)(2,1)S(1)} copy-done((bf16[32,10,128,128]{3,2,1,0:T(8,128)(2,1)S(1)}, bf16[32,10,128,128]{3,2,1,0:T(8,128)(2,1)}, u32[]{:S(2)}) %copy-start) | copy-done | bytes 10485784
  100.0 2.3 %collective-permute-start.22 = (f32[160,128]{1,0:T(8,128)S(1)}, f32[160,128]{1,0:T(8,128)S(1)}, u32[]{:S(2)}, u32[]{:S(2)}) collective-permute-start(f32[160,128]{1,0:T(8,128)S(1)} %add.58), channel_id=1, source_target_pairs={{0,24},{4,28},{8,16},{12,20},{16,8},{20,12},{24,0},{28,4},{32,56},... | collective-permute-start | bytes 245768 | tf_op jit(solution)/shard_map/ppermute | solution.py:369
  102.3 1.7 %collective-permute-start.21 = (f32[160,128]{1,0:T(8,128)S(1)}, f32[160,128]{1,0:T(8,128)S(1)}, u32[]{:S(2)}, u32[]{:S(2)}) collective-permute-start(f32[160,128]{1,0:T(8,128)S(1)} %add.58), channel_id=1, source_target_pairs={{0,16},{4,20},{8,24},{12,28},{16,0},{20,4},{24,8},{28,12},{32,48},... | collective-permute-start | bytes 245768 | tf_op jit(solution)/shard_map/ppermute | solution.py:369
  104.5 2.1 %agg_two.4 = bf16[43,1792]{1,0:T(8,128)(2,1)S(1)} custom-call(s32[10,32]{1,0:T(8,128)S(1)} %bitcast.21, bf16[64,48,128]{2,1,0:T(8,128)(2,1)S(1)} %spread.1.ext_ref, bf16[32,10,128,128]{3,2,1,0:T(8,128)(2,1)S(1)} %copy-done), custom_call_target="tpu_custom_call" | custom-call | flops 880803840 | bytes 4620000 | tf_op jit(solution)/shard_map/agg_two/pallas_call | solution.py:330
  107.0 2.1 %collective-permute-done.21 = f32[160,128]{1,0:T(8,128)S(1)} collective-permute-done((f32[160,128]{1,0:T(8,128)S(1)}, f32[160,128]{1,0:T(8,128)S(1)}, u32[]{:S(2)}, u32[]{:S(2)}) %collective-permute-start.21) | collective-permute-done | bytes 81952 | tf_op jit(solution)/shard_map/ppermute | solution.py:369
  110.6 3.0 %collective-permute-start.23 = (f32[160,128]{1,0:T(8,128)S(1)}, f32[160,128]{1,0:T(8,128)S(1)}, u32[]{:S(2)}, u32[]{:S(2)}) collective-permute-start(f32[160,128]{1,0:T(8,128)S(1)} %add_add_fusion.g0), channel_id=1, source_target_pairs={{0,1},{1,0},{2,3},{3,2},{4,5},{5,4},{6,7},{7,6},{8,9},{9,8},{10,11... | collective-permute-start | bytes 245768 | tf_op jit(solution)/shard_map/ppermute | solution.py:369
  113.5 2.1 %agg_two.5 = bf16[43,1792]{1,0:T(8,128)(2,1)S(1)} custom-call(s32[10,32]{1,0:T(8,128)S(1)} %bitcast.22, bf16[64,48,128]{2,1,0:T(8,128)(2,1)S(1)} %spread.1.ext_ref, bf16[32,10,128,128]{3,2,1,0:T(8,128)(2,1)S(1)} %copy-done), custom_call_target="tpu_custom_call" | custom-call | flops 880803840 | bytes 4620000 | tf_op jit(solution)/shard_map/agg_two/pallas_call | solution.py:330
  (71 shorter events, 28.0 us)
Async XLA Ops:
  4.9 24.1 %all-to-all-start = ((bf16[64,16,128]{2,1,0:T(8,128)(2,1)}), bf16[64,16,128]{2,1,0:T(8,128)(2,1)S(1)}, u32[]{:S(2)}, u32[]{:S(2)}) async-start(bf16[64,16,128]{2,1,0:T(8,128)(2,1)} %gather_rows.1), calls=%async_computation | async-start | bytes 524288 | tf_op jit(solution)/shard_map/all_to_all | solution.py:409
  24.2 13.2 %collective-permute-start = (bf16[48,2048]{1,0:T(8,128)(2,1)S(1)}, bf16[48,2048]{1,0:T(8,128)(2,1)S(1)}, u32[]{:S(2)}, u32[]{:S(2)}) collective-permute-start(bf16[48,2048]{1,0:T(8,128)(2,1)S(1)} %get-tuple-element.51), channel_id=1, source_target_pairs={{0,1},{1,0},{2,3},{3,2},{4,5},{5,4},{6,7},{7,6},{8,9},{9,8},{10,11... | collective-permute-start | bytes 589832 | tf_op jit(solution)/shard_map/ppermute | solution.py:369
  25.9 12.1 %collective-permute-start.1 = (bf16[48,2048]{1,0:T(8,128)(2,1)S(1)}, bf16[48,2048]{1,0:T(8,128)(2,1)S(1)}, u32[]{:S(2)}, u32[]{:S(2)}) collective-permute-start(bf16[48,2048]{1,0:T(8,128)(2,1)S(1)} %get-tuple-element.52), channel_id=1, source_target_pairs={{0,2},{1,3},{2,0},{3,1},{4,6},{5,7},{6,4},{7,5},{8,10},{9,11},{10,... | collective-permute-start | bytes 589832 | tf_op jit(solution)/shard_map/ppermute | solution.py:369
  28.8 11.8 %collective-permute-start.2 = (bf16[48,2048]{1,0:T(8,128)(2,1)S(1)}, bf16[48,2048]{1,0:T(8,128)(2,1)S(1)}, u32[]{:S(2)}, u32[]{:S(2)}) collective-permute-start(bf16[48,2048]{1,0:T(8,128)(2,1)S(1)} %get-tuple-element.53), channel_id=1, source_target_pairs={{0,3},{1,2},{2,1},{3,0},{4,7},{5,6},{6,5},{7,4},{8,11},{9,10},{10,... | collective-permute-start | bytes 589832 | tf_op jit(solution)/shard_map/ppermute | solution.py:369
  40.6 21.9 %all-to-all-start.1 = ((bf16[64,16,128]{2,1,0:T(8,128)(2,1)}), bf16[64,16,128]{2,1,0:T(8,128)(2,1)S(1)}, u32[]{:S(2)}, u32[]{:S(2)}) async-start(bf16[64,16,128]{2,1,0:T(8,128)(2,1)} %get-tuple-element.54), calls=%async_computation.1 | async-start | bytes 524288 | tf_op jit(solution)/shard_map/all_to_all | solution.py:415
  51.3 12.3 %collective-permute-start.6 = (bf16[32,1024]{1,0:T(8,128)(2,1)S(1)}, bf16[32,1024]{1,0:T(8,128)(2,1)S(1)}, u32[]{:S(2)}, u32[]{:S(2)}) collective-permute-start(bf16[32,1024]{1,0:T(8,128)(2,1)S(1)} %get-tuple-element.57), channel_id=1, source_target_pairs={{0,1},{1,0},{2,3},{3,2},{4,5},{5,4},{6,7},{7,6},{8,9},{9,8},{10,11... | collective-permute-start | bytes 196616 | tf_op jit(solution)/shard_map/ppermute | solution.py:369
  51.4 15.3 %collective-permute-start.7 = (bf16[32,1024]{1,0:T(8,128)(2,1)S(1)}, bf16[32,1024]{1,0:T(8,128)(2,1)S(1)}, u32[]{:S(2)}, u32[]{:S(2)}) collective-permute-start(bf16[32,1024]{1,0:T(8,128)(2,1)S(1)} %get-tuple-element.58), channel_id=1, source_target_pairs={{0,2},{1,3},{2,0},{3,1},{4,6},{5,7},{6,4},{7,5},{8,10},{9,11},{10,... | collective-permute-start | bytes 196616 | tf_op jit(solution)/shard_map/ppermute | solution.py:369
  53.1 13.6 %collective-permute-start.8 = (bf16[32,1024]{1,0:T(8,128)(2,1)S(1)}, bf16[32,1024]{1,0:T(8,128)(2,1)S(1)}, u32[]{:S(2)}, u32[]{:S(2)}) collective-permute-start(bf16[32,1024]{1,0:T(8,128)(2,1)S(1)} %get-tuple-element.59), channel_id=1, source_target_pairs={{0,3},{1,2},{2,1},{3,0},{4,7},{5,6},{6,5},{7,4},{8,11},{9,10},{10,... | collective-permute-start | bytes 196616 | tf_op jit(solution)/shard_map/ppermute | solution.py:369
  62.5 6.8 %collective-permute-start.5 = (bf16[16,16,128]{2,1,0:T(8,128)(2,1)S(1)}, bf16[16,16,128]{2,1,0:T(8,128)(2,1)S(1)}, u32[]{:S(2)}, u32[]{:S(2)}) collective-permute-start(bf16[16,16,128]{2,1,0:T(8,128)(2,1)S(1)} %get-tuple-element.93), channel_id=1, source_target_pairs={{0,3},{1,2},{2,1},{3,0},{4,7},{5,6},{6,5},{7,4},{8,11},{9,10},{10,... | collective-permute-start | bytes 196616 | tf_op jit(solution)/shard_map/ppermute | solution.py:369
  62.9 6.5 %collective-permute-start.4 = (bf16[16,16,128]{2,1,0:T(8,128)(2,1)S(1)}, bf16[16,16,128]{2,1,0:T(8,128)(2,1)S(1)}, u32[]{:S(2)}, u32[]{:S(2)}) collective-permute-start(bf16[16,16,128]{2,1,0:T(8,128)(2,1)S(1)} %get-tuple-element.94), channel_id=1, source_target_pairs={{0,2},{1,3},{2,0},{3,1},{4,6},{5,7},{6,4},{7,5},{8,10},{9,11},{10,... | collective-permute-start | bytes 196616 | tf_op jit(solution)/shard_map/ppermute | solution.py:369
  63.6 6.3 %collective-permute-start.3 = (bf16[16,16,128]{2,1,0:T(8,128)(2,1)S(1)}, bf16[16,16,128]{2,1,0:T(8,128)(2,1)S(1)}, u32[]{:S(2)}, u32[]{:S(2)}) collective-permute-start(bf16[16,16,128]{2,1,0:T(8,128)(2,1)S(1)} %get-tuple-element.95), channel_id=1, source_target_pairs={{0,1},{1,0},{2,3},{3,2},{4,5},{5,4},{6,7},{7,6},{8,9},{9,8},{10,11... | collective-permute-start | bytes 196616 | tf_op jit(solution)/shard_map/ppermute | solution.py:369
  71.6 8.2 %collective-permute-start.12 = (f32[160,128]{1,0:T(8,128)S(1)}, f32[160,128]{1,0:T(8,128)S(1)}, u32[]{:S(2)}, u32[]{:S(2)}) collective-permute-start(f32[160,128]{1,0:T(8,128)S(1)} %get-tuple-element.68), channel_id=1, source_target_pairs={{0,1},{1,0},{2,3},{3,2},{4,5},{5,4},{6,7},{7,6},{8,9},{9,8},{10,11... | collective-permute-start | bytes 245768 | tf_op jit(solution)/shard_map/ppermute | solution.py:369
  72.7 8.4 %collective-permute-start.13 = (f32[160,128]{1,0:T(8,128)S(1)}, f32[160,128]{1,0:T(8,128)S(1)}, u32[]{:S(2)}, u32[]{:S(2)}) collective-permute-start(f32[160,128]{1,0:T(8,128)S(1)} %get-tuple-element.69), channel_id=1, source_target_pairs={{0,2},{1,3},{2,0},{3,1},{4,6},{5,7},{6,4},{7,5},{8,10},{9,11},{10,... | collective-permute-start | bytes 245768 | tf_op jit(solution)/shard_map/ppermute | solution.py:369
  75.1 6.6 %collective-permute-start.14 = (f32[160,128]{1,0:T(8,128)S(1)}, f32[160,128]{1,0:T(8,128)S(1)}, u32[]{:S(2)}, u32[]{:S(2)}) collective-permute-start(f32[160,128]{1,0:T(8,128)S(1)} %get-tuple-element.70), channel_id=1, source_target_pairs={{0,3},{1,2},{2,1},{3,0},{4,7},{5,6},{6,5},{7,4},{8,11},{9,10},{10,... | collective-permute-start | bytes 245768 | tf_op jit(solution)/shard_map/ppermute | solution.py:369
  76.4 9.2 %collective-permute-start.9 = (bf16[48,2048]{1,0:T(8,128)(2,1)S(1)}, bf16[48,2048]{1,0:T(8,128)(2,1)S(1)}, u32[]{:S(2)}, u32[]{:S(2)}) collective-permute-start(bf16[48,2048]{1,0:T(8,128)(2,1)S(1)} %get-tuple-element.64), channel_id=1, source_target_pairs={{0,1},{1,0},{2,3},{3,2},{4,5},{5,4},{6,7},{7,6},{8,9},{9,8},{10,11... | collective-permute-start | bytes 589832 | tf_op jit(solution)/shard_map/ppermute | solution.py:369
  76.4 11.0 %collective-permute-start.10 = (bf16[48,2048]{1,0:T(8,128)(2,1)S(1)}, bf16[48,2048]{1,0:T(8,128)(2,1)S(1)}, u32[]{:S(2)}, u32[]{:S(2)}) collective-permute-start(bf16[48,2048]{1,0:T(8,128)(2,1)S(1)} %get-tuple-element.65), channel_id=1, source_target_pairs={{0,2},{1,3},{2,0},{3,1},{4,6},{5,7},{6,4},{7,5},{8,10},{9,11},{10,... | collective-permute-start | bytes 589832 | tf_op jit(solution)/shard_map/ppermute | solution.py:369
  79.8 9.4 %collective-permute-start.11 = (bf16[48,2048]{1,0:T(8,128)(2,1)S(1)}, bf16[48,2048]{1,0:T(8,128)(2,1)S(1)}, u32[]{:S(2)}, u32[]{:S(2)}) collective-permute-start(bf16[48,2048]{1,0:T(8,128)(2,1)S(1)} %get-tuple-element.66), channel_id=1, source_target_pairs={{0,3},{1,2},{2,1},{3,0},{4,7},{5,6},{6,5},{7,4},{8,11},{9,10},{10,... | collective-permute-start | bytes 589832 | tf_op jit(solution)/shard_map/ppermute | solution.py:369
  83.1 6.2 %collective-permute-start.18 = (f32[160,128]{1,0:T(8,128)S(1)}, f32[160,128]{1,0:T(8,128)S(1)}, u32[]{:S(2)}, u32[]{:S(2)}) collective-permute-start(f32[160,128]{1,0:T(8,128)S(1)} %add.54), channel_id=1, source_target_pairs={{0,192},{4,196},{8,200},{12,204},{16,208},{20,212},{24,216},{28,22... | collective-permute-start | bytes 245768 | tf_op jit(solution)/shard_map/ppermute | solution.py:369
  84.7 6.7 %collective-permute-start.17 = (f32[160,128]{1,0:T(8,128)S(1)}, f32[160,128]{1,0:T(8,128)S(1)}, u32[]{:S(2)}, u32[]{:S(2)}) collective-permute-start(f32[160,128]{1,0:T(8,128)S(1)} %add.54), channel_id=1, source_target_pairs={{0,128},{4,132},{8,136},{12,140},{16,144},{20,148},{24,152},{28,15... | collective-permute-start | bytes 245768 | tf_op jit(solution)/shard_map/ppermute | solution.py:369
  91.5 8.5 %collective-permute-start.19 = (f32[160,128]{1,0:T(8,128)S(1)}, f32[160,128]{1,0:T(8,128)S(1)}, u32[]{:S(2)}, u32[]{:S(2)}) collective-permute-start(f32[160,128]{1,0:T(8,128)S(1)} %add_add_fusion.1), channel_id=1, source_target_pairs={{0,32},{4,36},{8,40},{12,44},{16,48},{20,52},{24,56},{28,60},{32,0... | collective-permute-start | bytes 245768 | tf_op jit(solution)/shard_map/ppermute | solution.py:369
  100.0 7.0 %collective-permute-start.22 = (f32[160,128]{1,0:T(8,128)S(1)}, f32[160,128]{1,0:T(8,128)S(1)}, u32[]{:S(2)}, u32[]{:S(2)}) collective-permute-start(f32[160,128]{1,0:T(8,128)S(1)} %add.58), channel_id=1, source_target_pairs={{0,24},{4,28},{8,16},{12,20},{16,8},{20,12},{24,0},{28,4},{32,56},... | collective-permute-start | bytes 245768 | tf_op jit(solution)/shard_map/ppermute | solution.py:369
  102.3 6.8 %collective-permute-start.21 = (f32[160,128]{1,0:T(8,128)S(1)}, f32[160,128]{1,0:T(8,128)S(1)}, u32[]{:S(2)}, u32[]{:S(2)}) collective-permute-start(f32[160,128]{1,0:T(8,128)S(1)} %add.58), channel_id=1, source_target_pairs={{0,16},{4,20},{8,24},{12,28},{16,0},{20,4},{24,8},{28,12},{32,48},... | collective-permute-start | bytes 245768 | tf_op jit(solution)/shard_map/ppermute | solution.py:369
  109.3 6.2 %collective-permute-start.25 = (f32[160,128]{1,0:T(8,128)S(1)}, f32[160,128]{1,0:T(8,128)S(1)}, u32[]{:S(2)}, u32[]{:S(2)}) collective-permute-start(f32[160,128]{1,0:T(8,128)S(1)} %add_add_fusion.g0), channel_id=1, source_target_pairs={{0,3},{1,2},{2,1},{3,0},{4,7},{5,6},{6,5},{7,4},{8,11},{9,10},{10,... | collective-permute-start | bytes 245768 | tf_op jit(solution)/shard_map/ppermute | solution.py:369
  110.6 6.3 %collective-permute-start.23 = (f32[160,128]{1,0:T(8,128)S(1)}, f32[160,128]{1,0:T(8,128)S(1)}, u32[]{:S(2)}, u32[]{:S(2)}) collective-permute-start(f32[160,128]{1,0:T(8,128)S(1)} %add_add_fusion.g0), channel_id=1, source_target_pairs={{0,1},{1,0},{2,3},{3,2},{4,5},{5,4},{6,7},{7,6},{8,9},{9,8},{10,11... | collective-permute-start | bytes 245768 | tf_op jit(solution)/shard_map/ppermute | solution.py:369
  (12 other events, 144.7 us)

commit v3 on v2

--- a/solution.py
+++ b/solution.py
@@ -66,30 +66,57 @@
     return jnp.concatenate([top, bottom], axis=0).astype(BF)
 
 
-def fill_stack(stack_ref, panel_ref):
-    cols, rows = panel_ref.shape
-    for c in range(rows // 256):
-        stack_ref[c * cols : (c + 1) * cols, :] = panel_ref[:, c * 256 : (c + 1) * 256]
-
-
-def gather_kernel(panel_ref, idx_ref, out_ref, stack_ref):
-    fill_stack(stack_ref, panel_ref)
-    gather_packed(stack_ref, idx_ref, out_ref, panel_ref.shape[0])
-
-
-def gather_call(panel, idx):
+def gather_kernel(live_ref, panel_ref, send_ref, out_ref, idx_ref, stack_ref, lists, count_ref, sems):
+    cols = panel_ref.shape[0]
+    lanes = stack_ref.shape[1]
+    chunks = panel_ref.shape[1] // lanes
+    copies = [
+        pltpu.make_async_copy(live_ref, count_ref, sems.at[chunks + 1]),
+        pltpu.make_async_copy(send_ref, lists, sems.at[chunks]),
+    ] + [
+        pltpu.make_async_copy(
+            panel_ref.at[:, pl.ds(c * lanes, lanes)], stack_ref.at[pl.ds(c * cols, cols), :], sems.at[c]
+        )
+        for c in range(chunks)
+    ]
+    for copy in copies:
+        copy.start()
+    copies[0].wait()
+    copies[1].wait()
+    bound = lists.shape[1]
+    slot = lax.broadcasted_iota(jnp.int32, (1, bound), 1)
+    per = lanes // bound
+    for j in range(idx_ref.shape[0]):
+        rows = [
+            jnp.where(slot < count_ref[q], lists[q : q + 1, :], -1) for q in range(j * per, (j + 1) * per)
+        ]
+        idx_ref[j : j + 1, :] = jnp.concatenate(rows, axis=1)
+    for copy in copies[2:]:
+        copy.wait()
+    gather_packed(stack_ref, idx_ref, out_ref, cols)
+
+
+def gather_call(panel, send_idx, send_count):
     cols, rows = panel.shape
-    pieces = idx.size // 64
+    pieces, bound = send_idx.shape
     return pl.pallas_call(
         gather_kernel,
-        out_shape=jax.ShapeDtypeStruct((pieces, 16, 128), BF),
-        in_specs=[whole(), whole()],
-        out_specs=whole(),
-        scratch_shapes=[VMEM((rows // 256 * cols, 256), BF)],
-        compiler_params=params(),
+        out_shape=(
+            jax.ShapeDtypeStruct((pieces, 16, 128), BF),
+            jax.ShapeDtypeStruct((pieces * bound // 256, 256), jnp.int32),
+        ),
+        in_specs=[anywhere()] * 3,
+        out_specs=[whole(), whole()],
+        scratch_shapes=[
+            VMEM((rows // 256 * cols, 256), BF),
+            VMEM((pieces, bound), jnp.int32),
+            pltpu.SMEM((pieces,), jnp.int32),
+            pltpu.SemaphoreType.DMA((rows // 256 + 2,)),
+        ],
+        compiler_params=params(60 * 1024 * 1024),
         cost_estimate=cost(2 * 512 * 256 * 4096, 1 << 20),
         name="gather_rows",
-    )(panel, idx)
+    )(send_count, panel, send_idx)
 
 
 def smem():
@@ -321,21 +348,28 @@
     )(me, *ys)
 
 
-def agg_two_call(first, count, ext, cols, vals, classes):
-    def kernel(cols_ref, ext_ref, vals_ref, out_ref):
+def agg_two_call(first, count, ext, cols, vals, classes, done):
+    lead = sum(part.shape[1] for part in done)
+
+    def kernel(cols_ref, ext_ref, vals_ref, *refs):
+        out_ref = refs[-1]
+        at = 0
+        for part in refs[:-1]:
+            out_ref[:, at : at + part.shape[1]] = part[...]
+            at += part.shape[1]
         for r in range(count):
             total = agg_tile(first + r, first + r, cols_ref, ext_ref, vals_ref)
-            out_ref[:, r * 128 : (r + 1) * 128] = total[:classes]
+            out_ref[:, at + r * 128 : at + (r + 1) * 128] = total[:classes]
 
     return pl.pallas_call(
         kernel,
-        out_shape=jax.ShapeDtypeStruct((classes, count * 128), BF),
-        in_specs=[smem(), whole(), whole()],
+        out_shape=jax.ShapeDtypeStruct((classes, lead + count * 128), BF),
+        in_specs=[smem()] + [whole()] * (2 + len(done)),
         out_specs=whole(),
         compiler_params=params(),
         cost_estimate=cost(2 * 48 * 128 * 128 * 10 * count * 4, count * 330000),
         name="agg_two",
-    )(cols, ext, vals)
+    )(cols, ext, vals, *done)
 
 
 def finish_kernel(me_ref, g0, g1, g2, g3, one_ref, two_ref, buf):
@@ -385,7 +419,6 @@
     feat = lax.axis_size("feat")
     me = lax.axis_index("feat").astype(jnp.int32)
     me_arr = me.reshape(1)
-    bound_rows = send_idx.shape[1]
     class_cols = grad_logits.shape[1]
     hidden = weight_one.shape[1]
 
@@ -395,8 +428,6 @@
     def swap_dom(x, mask):
         return swap(x, "dom", partitions, mask)
 
-    live = jnp.arange(bound_rows, dtype=jnp.int32)[None, :] < send_count[:, None]
-    idx = jnp.where(live, send_idx, -1).reshape(-1, 256)
     panel = features.T
     grad = grad_logits.T
     cols = tile_cols.T
@@ -405,13 +436,13 @@
     w1t = weight_one.T
     w2t = w2.T
 
-    packed_one = gather_call(panel, idx)
+    packed_one, idx = gather_call(panel, send_idx, send_count)
     received_one = lax.all_to_all(packed_one, "dom", split_axis=0, concat_axis=0, tiled=True)
     zs = transpose_agg_call(grad, cols, tile_vals, me_arr)
     received_one = after(received_one, zs[0])
     zs = [zs[0]] + [swap_feat(zs[d], d) for d in (1, 2, 3)]
     packed_two, *mixed = agg_one_call(panel, received_one, idx, cols, tile_vals, me_arr)
-    packed_two = after(packed_two, *zs)
+    packed_two = after(packed_two, zs[1], zs[3])
     received_two = lax.all_to_all(packed_two, "dom", split_axis=0, concat_axis=0, tiled=True)
     own = [mixed[0]] + [swap_feat(mixed[d], d) for d in (1, 2, 3)]
     pieces = partitions // feat
@@ -436,7 +467,8 @@
 
     def beside(moved):
         first, last = cuts[len(out) : len(out) + 2]
-        out.append(agg_two_call(first, last - first, ext, cols, tile_vals, class_cols))
+        done = out if last == row_tiles else []
+        out.append(agg_two_call(first, last - first, ext, cols, tile_vals, class_cols, done))
         *moved, out[-1] = lax.optimization_barrier((*moved, out[-1]))
         return moved
 
@@ -448,8 +480,7 @@
     total = (total + moved[0]) + (moved[1] + moved[2])
     ext, total = lax.optimization_barrier((ext, total))
     moved = beside([swap_feat(total, d) for d in (1, 2, 3)])
-    logits = jnp.concatenate(out, axis=1)
-    logits, *moved = lax.optimization_barrier((logits, *moved))
+    logits = out[-1]
     grad_one, grad_two = finish_call(me_arr, [total] + moved, feat * class_cols)
     return (logits.T, grad_one, grad_two.T)
 

time: 119 us -> 113 us (0.950)
  waiting for transfers between devices: 22.3 us -> 17.2 us
  Pallas kernels: 25.7 us -> 27.5 us
  other arithmetic: 1.7 us -> 0.08 us
    ppermute x26, waiting for transfers between devices: 15.9 us -> 11.1 us  [swap(): return lax.ppermute(x, axis, [(i, i ^ mask) for i in range(size)])]
    pallas_call x4, Pallas kernels: 7.74 us -> 9.56 us  [the longest x3 6.06 us: agg_two_call(): pl.pallas_call(kernel, out_shape=jax.ShapeDtypeStruct((classes, lead + co...]
  transfers between devices with their start and end apart: 28 -> 28, of which waited for: 15 -> 14; matrix products, arithmetic and copies ran while one was open for 0% -> 0% of each run, Pallas kernels for 18% -> 19%
where the time goes in v3:
time: 113 us
  starting transfers between devices  61.2 us (54%)
  Pallas kernels  27.5 us (24%)
  waiting for transfers between devices  17.2 us (15%)
  local copies, waits for them, and re-layouts  5.96 us (5%)
    ppermute x26, starting transfers between devices, swap(): return lax.ppermute(x, axis, [(i, i ^ mask) for i in range(size)])  39.2 us
    all_to_all x1, starting transfers between devices, on_device(): lax.all_to_all(packed_one, 'dom', split_axis=0, concat_axis=0, tiled=True)  12 us
    ppermute x26, waiting for transfers between devices, swap(): return lax.ppermute(x, axis, [(i, i ^ mask) for i in range(size)])  11.1 us
    all_to_all x1, starting transfers between devices, on_device(): lax.all_to_all(packed_two, 'dom', split_axis=0, concat_axis=0, tiled=True)  9.89 us
    pallas_call x1, Pallas kernels, agg_one_call(): pl.pallas_call(agg_one_kernel, out_shape=(jax.ShapeDtypeStruct((pieces, 1...  8.39 us
    pallas_call x3, Pallas kernels, agg_two_call(): pl.pallas_call(kernel, out_shape=jax.ShapeDtypeStruct((classes, lead + co...  6.06 us
    unnamed x17, local copies, waits for them, and re-layouts  5.8 us
    all_to_all x1, waiting for transfers between devices, on_device(): lax.all_to_all(packed_two, 'dom', split_axis=0, concat_axis=0, tiled=True)  5.62 us
  transfers between devices with their start and end apart: 28, of which 14 were waited for; matrix products, arithmetic and copies ran while one was open for 0% of the time, Pallas kernels for 19%

profile of v3, /device:TPU:2, one launch (start us, length us, event | category | flops | bytes accessed | tf_op | source)
XLA Modules:
  0.0 112.8 jit_solution(8307800563594587570)
XLA Ops:
  0.7 3.5 %gather_rows.1 = (bf16[64,16,128]{2,1,0:T(8,128)(2,1)}, s32[16,256]{1,0:T(8,128)}) custom-call(s32[64]{0:T(128)} %live_ref.1, bf16[32,4096]{1,0:T(8,128)(2,1)} %bitcast.16, s32[64,64]{1,0:T(8,128)} %send_ref.1), custom_call_target="tpu_custom_call" | custom-call | flops 1073741824 | bytes 1048576 | tf_op jit(solution)/shard_map/gather_rows/pallas_call | solution.py:102
  4.2 12.0 %all-to-all-start = ((bf16[64,16,128]{2,1,0:T(8,128)(2,1)}), bf16[64,16,128]{2,1,0:T(8,128)(2,1)S(1)}, u32[]{:S(2)}, u32[]{:S(2)}) async-start(bf16[64,16,128]{2,1,0:T(8,128)(2,1)} %get-tuple-element.46), calls=%async_computation | async-start | bytes 524288 | tf_op jit(solution)/shard_map/all_to_all | solution.py:440
  17.9 5.5 %agg_transposed.1 = (bf16[48,2048]{1,0:T(8,128)(2,1)S(1)}, bf16[48,2048]{1,0:T(8,128)(2,1)S(1)}, bf16[48,2048]{1,0:T(8,128)(2,1)S(1)}, bf16[48,2048]{1,0:T(8,128)(2,1)S(1)}) custom-call(s32[10,32]{1,0:T(8,128)S(1)} %bitcast.18, s32[1]{0:T(128)} %bitcast.me_ref, bf16[43,4096]{1,0:T(8,128)(2,1)S(1)} %bitcast.12, bf16[32,10,128,128]{3,2,1,0:T(8,128)(2,1)} %vals_ref.9), custom_call_target="tpu_custom_call" | custom-call | flops 2013265920 | bytes 11534336 | tf_op jit(solution)/shard_map/agg_transposed/pallas_call | solution.py:172
  23.5 1.7 %collective-permute-start = (bf16[48,2048]{1,0:T(8,128)(2,1)S(1)}, bf16[48,2048]{1,0:T(8,128)(2,1)S(1)}, u32[]{:S(2)}, u32[]{:S(2)}) collective-permute-start(bf16[48,2048]{1,0:T(8,128)(2,1)S(1)} %get-tuple-element.51), channel_id=1, source_target_pairs={{0,1},{1,0},{2,3},{3,2},{4,5},{5,4},{6,7},{7,6},{8,9},{9,8},{10,11... | collective-permute-start | bytes 589832 | tf_op jit(solution)/shard_map/ppermute | solution.py:403
  25.1 2.2 %collective-permute-start.1 = (bf16[48,2048]{1,0:T(8,128)(2,1)S(1)}, bf16[48,2048]{1,0:T(8,128)(2,1)S(1)}, u32[]{:S(2)}, u32[]{:S(2)}) collective-permute-start(bf16[48,2048]{1,0:T(8,128)(2,1)S(1)} %get-tuple-element.52), channel_id=1, source_target_pairs={{0,3},{1,2},{2,1},{3,0},{4,7},{5,6},{6,5},{7,4},{8,11},{9,10},{10,... | collective-permute-start | bytes 589832 | tf_op jit(solution)/shard_map/ppermute | solution.py:403
  27.8 8.4 %agg_one.1 = (bf16[64,16,128]{2,1,0:T(8,128)(2,1)}, bf16[32,1024]{1,0:T(8,128)(2,1)S(1)}, bf16[32,1024]{1,0:T(8,128)(2,1)S(1)}, bf16[32,1024]{1,0:T(8,128)(2,1)S(1)}, bf16[32,1024]{1,0:T(8,128)(2,1)S(1)}) custom-call(s32[10,32]{1,0:T(8,128)S(1)} %bitcast.19, s32[1]{0:T(128)} %bitcast.me_ref, bf16[32,4096]{1,0:T(8,128)(2,1)S(1)} %bitcast.17, ...), custom_call_target="tpu_custom_call" | custom-call | flops 2684354560 | bytes 11534336 | tf_op jit(solution)/shard_map/agg_one/pallas_call | solution.py:221
  36.2 9.9 %all-to-all-start.1 = ((bf16[64,16,128]{2,1,0:T(8,128)(2,1)}), bf16[64,16,128]{2,1,0:T(8,128)(2,1)S(1)}, u32[]{:S(2)}, u32[]{:S(2)}) async-start(bf16[64,16,128]{2,1,0:T(8,128)(2,1)} %get-tuple-element.53), calls=%async_computation.1 | async-start | bytes 524288 | tf_op jit(solution)/shard_map/all_to_all | solution.py:446
  48.5 2.9 %collective-permute-start.7 = (bf16[32,1024]{1,0:T(8,128)(2,1)S(1)}, bf16[32,1024]{1,0:T(8,128)(2,1)S(1)}, u32[]{:S(2)}, u32[]{:S(2)}) collective-permute-start(bf16[32,1024]{1,0:T(8,128)(2,1)S(1)} %get-tuple-element.58), channel_id=1, source_target_pairs={{0,2},{1,3},{2,0},{3,1},{4,6},{5,7},{6,4},{7,5},{8,10},{9,11},{10,... | collective-permute-start | bytes 196616 | tf_op jit(solution)/shard_map/ppermute | solution.py:403
  52.0 5.6 %all-to-all-done.1 = bf16[64,16,128]{2,1,0:T(8,128)(2,1)S(1)} async-done(((bf16[64,16,128]{2,1,0:T(8,128)(2,1)}), bf16[64,16,128]{2,1,0:T(8,128)(2,1)S(1)}, u32[]{:S(2)}, u32[]{:S(2)}) %all-to-all-start.1) | async-done | bytes 262176 | tf_op jit(solution)/shard_map/all_to_all | solution.py:446
  58.8 1.7 %collective-permute-start.3 = (bf16[16,16,128]{2,1,0:T(8,128)(2,1)S(1)}, bf16[16,16,128]{2,1,0:T(8,128)(2,1)S(1)}, u32[]{:S(2)}, u32[]{:S(2)}) collective-permute-start(bf16[16,16,128]{2,1,0:T(8,128)(2,1)S(1)} %get-tuple-element.90), channel_id=1, source_target_pairs={{0,2},{1,3},{2,0},{3,1},{4,6},{5,7},{6,4},{7,5},{8,10},{9,11},{10,... | collective-permute-start | bytes 196616 | tf_op jit(solution)/shard_map/ppermute | solution.py:403
  65.1 1.7 %dense_far.1 = (bf16[48,2048]{1,0:T(8,128)(2,1)S(1)}, bf16[48,2048]{1,0:T(8,128)(2,1)S(1)}, bf16[48,2048]{1,0:T(8,128)(2,1)S(1)}, bf16[48,2048]{1,0:T(8,128)(2,1...) custom-call(s32[1]{0:T(128)} %bitcast.me_ref, ...), custom_call_target="tpu_custom_call" | custom-call | flops 786432000 | bytes 4194304 | tf_op jit(solution)/shard_map/dense_far/pallas_call | solution.py:316
  67.9 2.4 %collective-permute-start.13 = (f32[160,128]{1,0:T(8,128)S(1)}, f32[160,128]{1,0:T(8,128)S(1)}, u32[]{:S(2)}, u32[]{:S(2)}) collective-permute-start(f32[160,128]{1,0:T(8,128)S(1)} %get-tuple-element.69), channel_id=1, source_target_pairs={{0,2},{1,3},{2,0},{3,1},{4,6},{5,7},{6,4},{7,5},{8,10},{9,11},{10,... | collective-permute-start | bytes 245768 | tf_op jit(solution)/shard_map/ppermute | solution.py:403
  71.5 3.4 %collective-permute-start.10 = (bf16[48,2048]{1,0:T(8,128)(2,1)S(1)}, bf16[48,2048]{1,0:T(8,128)(2,1)S(1)}, u32[]{:S(2)}, u32[]{:S(2)}) collective-permute-start(bf16[48,2048]{1,0:T(8,128)(2,1)S(1)} %get-tuple-element.65), channel_id=1, source_target_pairs={{0,2},{1,3},{2,0},{3,1},{4,6},{5,7},{6,4},{7,5},{8,10},{9,11},{10,... | collective-permute-start | bytes 589832 | tf_op jit(solution)/shard_map/ppermute | solution.py:403
  80.7 1.7 %collective-permute-start.16 = (f32[160,128]{1,0:T(8,128)S(1)}, f32[160,128]{1,0:T(8,128)S(1)}, u32[]{:S(2)}, u32[]{:S(2)}) collective-permute-start(f32[160,128]{1,0:T(8,128)S(1)} %add.54), channel_id=1, source_target_pairs={{0,64},{4,68},{8,72},{12,76},{16,80},{20,84},{24,88},{28,92},{32,9... | collective-permute-start | bytes 245768 | tf_op jit(solution)/shard_map/ppermute | solution.py:403
  82.5 1.9 %collective-permute-done.11.refs_3_ = bf16[48,2048]{1,0:T(8,128)(2,1)S(1)} collective-permute-done((bf16[48,2048]{1,0:T(8,128)(2,1)S(1)}, bf16[48,2048]{1,0:T(8,128)(2,1)S(1)}, u32[]{:S(2)}, u32[]{:S(2)}) %collective-permute-start.11) | collective-permute-done | bytes 196640 | tf_op jit(solution)/shard_map/ppermute | solution.py:403
  84.5 2.1 %collective-permute-done.17 = f32[160,128]{1,0:T(8,128)S(1)} collective-permute-done((f32[160,128]{1,0:T(8,128)S(1)}, f32[160,128]{1,0:T(8,128)S(1)}, u32[]{:S(2)}, u32[]{:S(2)}) %collective-permute-start.17) | collective-permute-done | bytes 81952 | tf_op jit(solution)/shard_map/ppermute | solution.py:403
  86.7 3.2 %collective-permute-start.19 = (f32[160,128]{1,0:T(8,128)S(1)}, f32[160,128]{1,0:T(8,128)S(1)}, u32[]{:S(2)}, u32[]{:S(2)}) collective-permute-start(f32[160,128]{1,0:T(8,128)S(1)} %add_add_fusion.1), channel_id=1, source_target_pairs={{0,32},{4,36},{8,40},{12,44},{16,48},{20,52},{24,56},{28,60},{32,0... | collective-permute-start | bytes 245768 | tf_op jit(solution)/shard_map/ppermute | solution.py:403
  89.9 4.0 %copy-done = bf16[32,10,128,128]{3,2,1,0:T(8,128)(2,1)S(1)} copy-done((bf16[32,10,128,128]{3,2,1,0:T(8,128)(2,1)S(1)}, bf16[32,10,128,128]{3,2,1,0:T(8,128)(2,1)}, u32[]{:S(2)}) %copy-start) | copy-done | bytes 10485784
  95.1 2.2 %collective-permute-start.22 = (f32[160,128]{1,0:T(8,128)S(1)}, f32[160,128]{1,0:T(8,128)S(1)}, u32[]{:S(2)}, u32[]{:S(2)}) collective-permute-start(f32[160,128]{1,0:T(8,128)S(1)} %add.58), channel_id=1, source_target_pairs={{0,24},{4,28},{8,16},{12,20},{16,8},{20,12},{24,0},{28,4},{32,56},... | collective-permute-start | bytes 245768 | tf_op jit(solution)/shard_map/ppermute | solution.py:403
  97.4 1.7 %collective-permute-start.21 = (f32[160,128]{1,0:T(8,128)S(1)}, f32[160,128]{1,0:T(8,128)S(1)}, u32[]{:S(2)}, u32[]{:S(2)}) collective-permute-start(f32[160,128]{1,0:T(8,128)S(1)} %add.58), channel_id=1, source_target_pairs={{0,16},{4,20},{8,24},{12,28},{16,0},{20,4},{24,8},{28,12},{32,48},... | collective-permute-start | bytes 245768 | tf_op jit(solution)/shard_map/ppermute | solution.py:403
  99.6 2.1 %agg_two.4.refs_1_ = bf16[43,1792]{1,0:T(8,128)(2,1)S(1)} custom-call(s32[10,32]{1,0:T(8,128)S(1)} %bitcast.21, bf16[64,48,128]{2,1,0:T(8,128)(2,1)S(1)} %spread.1.ext_ref, bf16[32,10,128,128]{3,2,1,0:T(8,128)(2,1)S(1)} %copy-done), custom_call_target="tpu_custom_call" | custom-call | flops 880803840 | bytes 4620000 | tf_op jit(solution)/shard_map/agg_two/pallas_call | solution.py:364
  102.2 2.4 %collective-permute-done.21 = f32[160,128]{1,0:T(8,128)S(1)} collective-permute-done((f32[160,128]{1,0:T(8,128)S(1)}, f32[160,128]{1,0:T(8,128)S(1)}, u32[]{:S(2)}, u32[]{:S(2)}) %collective-permute-start.21) | collective-permute-done | bytes 81952 | tf_op jit(solution)/shard_map/ppermute | solution.py:403
  105.8 3.0 %collective-permute-start.23 = (f32[160,128]{1,0:T(8,128)S(1)}, f32[160,128]{1,0:T(8,128)S(1)}, u32[]{:S(2)}, u32[]{:S(2)}) collective-permute-start(f32[160,128]{1,0:T(8,128)S(1)} %add_add_fusion.g0), channel_id=1, source_target_pairs={{0,1},{1,0},{2,3},{3,2},{4,5},{5,4},{6,7},{7,6},{8,9},{9,8},{10,11... | collective-permute-start | bytes 245768 | tf_op jit(solution)/shard_map/ppermute | solution.py:403
  108.8 2.8 %agg_two.5 = bf16[43,4096]{1,0:T(8,128)(2,1)} custom-call(s32[10,32]{1,0:T(8,128)S(1)} %bitcast.22, bf16[64,48,128]{2,1,0:T(8,128)(2,1)S(1)} %spread.1.ext_ref, bf16[32,10,128,128]{3,2,1,0:T(8,128)(2,1)S(1)} %copy-done, bf16[43,512]{1,0:T(8,128)(2,1)S(1)} %agg_two.3.refs_0_, bf16[43,1792]{1,0:T(8,128)(2,1)S(1)} %agg_two.4.refs_1_), custom_call_target="tpu_custom_call" | custom-call | flops 880803840 | bytes 4620000 | tf_op jit(solution)/shard_map/agg_two/pallas_call | solution.py:364
  (68 shorter events, 24.0 us)
Async XLA Ops:
  4.2 23.6 %all-to-all-start = ((bf16[64,16,128]{2,1,0:T(8,128)(2,1)}), bf16[64,16,128]{2,1,0:T(8,128)(2,1)S(1)}, u32[]{:S(2)}, u32[]{:S(2)}) async-start(bf16[64,16,128]{2,1,0:T(8,128)(2,1)} %get-tuple-element.46), calls=%async_computation | async-start | bytes 524288 | tf_op jit(solution)/shard_map/all_to_all | solution.py:440
  23.5 12.7 %collective-permute-start = (bf16[48,2048]{1,0:T(8,128)(2,1)S(1)}, bf16[48,2048]{1,0:T(8,128)(2,1)S(1)}, u32[]{:S(2)}, u32[]{:S(2)}) collective-permute-start(bf16[48,2048]{1,0:T(8,128)(2,1)S(1)} %get-tuple-element.51), channel_id=1, source_target_pairs={{0,1},{1,0},{2,3},{3,2},{4,5},{5,4},{6,7},{7,6},{8,9},{9,8},{10,11... | collective-permute-start | bytes 589832 | tf_op jit(solution)/shard_map/ppermute | solution.py:403
  25.1 11.1 %collective-permute-start.1 = (bf16[48,2048]{1,0:T(8,128)(2,1)S(1)}, bf16[48,2048]{1,0:T(8,128)(2,1)S(1)}, u32[]{:S(2)}, u32[]{:S(2)}) collective-permute-start(bf16[48,2048]{1,0:T(8,128)(2,1)S(1)} %get-tuple-element.52), channel_id=1, source_target_pairs={{0,3},{1,2},{2,1},{3,0},{4,7},{5,6},{6,5},{7,4},{8,11},{9,10},{10,... | collective-permute-start | bytes 589832 | tf_op jit(solution)/shard_map/ppermute | solution.py:403
  36.2 21.4 %all-to-all-start.1 = ((bf16[64,16,128]{2,1,0:T(8,128)(2,1)}), bf16[64,16,128]{2,1,0:T(8,128)(2,1)S(1)}, u32[]{:S(2)}, u32[]{:S(2)}) async-start(bf16[64,16,128]{2,1,0:T(8,128)(2,1)} %get-tuple-element.53), calls=%async_computation.1 | async-start | bytes 524288 | tf_op jit(solution)/shard_map/all_to_all | solution.py:446
  46.1 12.7 %collective-permute-start.5 = (bf16[48,2048]{1,0:T(8,128)(2,1)S(1)}, bf16[48,2048]{1,0:T(8,128)(2,1)S(1)}, u32[]{:S(2)}, u32[]{:S(2)}) collective-permute-start(bf16[48,2048]{1,0:T(8,128)(2,1)S(1)} %get-tuple-element.54), channel_id=1, source_target_pairs={{0,2},{1,3},{2,0},{3,1},{4,6},{5,7},{6,4},{7,5},{8,10},{9,11},{10,... | collective-permute-start | bytes 589832 | tf_op jit(solution)/shard_map/ppermute | solution.py:403
  47.2 13.3 %collective-permute-start.6 = (bf16[32,1024]{1,0:T(8,128)(2,1)S(1)}, bf16[32,1024]{1,0:T(8,128)(2,1)S(1)}, u32[]{:S(2)}, u32[]{:S(2)}) collective-permute-start(bf16[32,1024]{1,0:T(8,128)(2,1)S(1)} %get-tuple-element.57), channel_id=1, source_target_pairs={{0,1},{1,0},{2,3},{3,2},{4,5},{5,4},{6,7},{7,6},{8,9},{9,8},{10,11... | collective-permute-start | bytes 196616 | tf_op jit(solution)/shard_map/ppermute | solution.py:403
  48.5 13.4 %collective-permute-start.7 = (bf16[32,1024]{1,0:T(8,128)(2,1)S(1)}, bf16[32,1024]{1,0:T(8,128)(2,1)S(1)}, u32[]{:S(2)}, u32[]{:S(2)}) collective-permute-start(bf16[32,1024]{1,0:T(8,128)(2,1)S(1)} %get-tuple-element.58), channel_id=1, source_target_pairs={{0,2},{1,3},{2,0},{3,1},{4,6},{5,7},{6,4},{7,5},{8,10},{9,11},{10,... | collective-permute-start | bytes 196616 | tf_op jit(solution)/shard_map/ppermute | solution.py:403
  51.4 10.5 %collective-permute-start.8 = (bf16[32,1024]{1,0:T(8,128)(2,1)S(1)}, bf16[32,1024]{1,0:T(8,128)(2,1)S(1)}, u32[]{:S(2)}, u32[]{:S(2)}) collective-permute-start(bf16[32,1024]{1,0:T(8,128)(2,1)S(1)} %get-tuple-element.59), channel_id=1, source_target_pairs={{0,3},{1,2},{2,1},{3,0},{4,7},{5,6},{6,5},{7,4},{8,11},{9,10},{10,... | collective-permute-start | bytes 196616 | tf_op jit(solution)/shard_map/ppermute | solution.py:403
  57.7 6.3 %collective-permute-start.4 = (bf16[16,16,128]{2,1,0:T(8,128)(2,1)S(1)}, bf16[16,16,128]{2,1,0:T(8,128)(2,1)S(1)}, u32[]{:S(2)}, u32[]{:S(2)}) collective-permute-start(bf16[16,16,128]{2,1,0:T(8,128)(2,1)S(1)} %get-tuple-element.89), channel_id=1, source_target_pairs={{0,3},{1,2},{2,1},{3,0},{4,7},{5,6},{6,5},{7,4},{8,11},{9,10},{10,... | collective-permute-start | bytes 196616 | tf_op jit(solution)/shard_map/ppermute | solution.py:403
  58.8 6.1 %collective-permute-start.3 = (bf16[16,16,128]{2,1,0:T(8,128)(2,1)S(1)}, bf16[16,16,128]{2,1,0:T(8,128)(2,1)S(1)}, u32[]{:S(2)}, u32[]{:S(2)}) collective-permute-start(bf16[16,16,128]{2,1,0:T(8,128)(2,1)S(1)} %get-tuple-element.90), channel_id=1, source_target_pairs={{0,2},{1,3},{2,0},{3,1},{4,6},{5,7},{6,4},{7,5},{8,10},{9,11},{10,... | collective-permute-start | bytes 196616 | tf_op jit(solution)/shard_map/ppermute | solution.py:403
  66.7 8.2 %collective-permute-start.12 = (f32[160,128]{1,0:T(8,128)S(1)}, f32[160,128]{1,0:T(8,128)S(1)}, u32[]{:S(2)}, u32[]{:S(2)}) collective-permute-start(f32[160,128]{1,0:T(8,128)S(1)} %get-tuple-element.68), channel_id=1, source_target_pairs={{0,1},{1,0},{2,3},{3,2},{4,5},{5,4},{6,7},{7,6},{8,9},{9,8},{10,11... | collective-permute-start | bytes 245768 | tf_op jit(solution)/shard_map/ppermute | solution.py:403
  67.9 8.4 %collective-permute-start.13 = (f32[160,128]{1,0:T(8,128)S(1)}, f32[160,128]{1,0:T(8,128)S(1)}, u32[]{:S(2)}, u32[]{:S(2)}) collective-permute-start(f32[160,128]{1,0:T(8,128)S(1)} %get-tuple-element.69), channel_id=1, source_target_pairs={{0,2},{1,3},{2,0},{3,1},{4,6},{5,7},{6,4},{7,5},{8,10},{9,11},{10,... | collective-permute-start | bytes 245768 | tf_op jit(solution)/shard_map/ppermute | solution.py:403
  70.3 6.6 %collective-permute-start.14 = (f32[160,128]{1,0:T(8,128)S(1)}, f32[160,128]{1,0:T(8,128)S(1)}, u32[]{:S(2)}, u32[]{:S(2)}) collective-permute-start(f32[160,128]{1,0:T(8,128)S(1)} %get-tuple-element.70), channel_id=1, source_target_pairs={{0,3},{1,2},{2,1},{3,0},{4,7},{5,6},{6,5},{7,4},{8,11},{9,10},{10,... | collective-permute-start | bytes 245768 | tf_op jit(solution)/shard_map/ppermute | solution.py:403
  71.5 9.2 %collective-permute-start.9 = (bf16[48,2048]{1,0:T(8,128)(2,1)S(1)}, bf16[48,2048]{1,0:T(8,128)(2,1)S(1)}, u32[]{:S(2)}, u32[]{:S(2)}) collective-permute-start(bf16[48,2048]{1,0:T(8,128)(2,1)S(1)} %get-tuple-element.64), channel_id=1, source_target_pairs={{0,1},{1,0},{2,3},{3,2},{4,5},{5,4},{6,7},{7,6},{8,9},{9,8},{10,11... | collective-permute-start | bytes 589832 | tf_op jit(solution)/shard_map/ppermute | solution.py:403
  71.5 10.9 %collective-permute-start.10 = (bf16[48,2048]{1,0:T(8,128)(2,1)S(1)}, bf16[48,2048]{1,0:T(8,128)(2,1)S(1)}, u32[]{:S(2)}, u32[]{:S(2)}) collective-permute-start(bf16[48,2048]{1,0:T(8,128)(2,1)S(1)} %get-tuple-element.65), channel_id=1, source_target_pairs={{0,2},{1,3},{2,0},{3,1},{4,6},{5,7},{6,4},{7,5},{8,10},{9,11},{10,... | collective-permute-start | bytes 589832 | tf_op jit(solution)/shard_map/ppermute | solution.py:403
  75.0 9.4 %collective-permute-start.11 = (bf16[48,2048]{1,0:T(8,128)(2,1)S(1)}, bf16[48,2048]{1,0:T(8,128)(2,1)S(1)}, u32[]{:S(2)}, u32[]{:S(2)}) collective-permute-start(bf16[48,2048]{1,0:T(8,128)(2,1)S(1)} %get-tuple-element.66), channel_id=1, source_target_pairs={{0,3},{1,2},{2,1},{3,0},{4,7},{5,6},{6,5},{7,4},{8,11},{9,10},{10,... | collective-permute-start | bytes 589832 | tf_op jit(solution)/shard_map/ppermute | solution.py:403
  78.3 6.2 %collective-permute-start.18 = (f32[160,128]{1,0:T(8,128)S(1)}, f32[160,128]{1,0:T(8,128)S(1)}, u32[]{:S(2)}, u32[]{:S(2)}) collective-permute-start(f32[160,128]{1,0:T(8,128)S(1)} %add.54), channel_id=1, source_target_pairs={{0,192},{4,196},{8,200},{12,204},{16,208},{20,212},{24,216},{28,22... | collective-permute-start | bytes 245768 | tf_op jit(solution)/shard_map/ppermute | solution.py:403
  79.9 6.7 %collective-permute-start.17 = (f32[160,128]{1,0:T(8,128)S(1)}, f32[160,128]{1,0:T(8,128)S(1)}, u32[]{:S(2)}, u32[]{:S(2)}) collective-permute-start(f32[160,128]{1,0:T(8,128)S(1)} %add.54), channel_id=1, source_target_pairs={{0,128},{4,132},{8,136},{12,140},{16,144},{20,148},{24,152},{28,15... | collective-permute-start | bytes 245768 | tf_op jit(solution)/shard_map/ppermute | solution.py:403
  86.7 8.4 %collective-permute-start.19 = (f32[160,128]{1,0:T(8,128)S(1)}, f32[160,128]{1,0:T(8,128)S(1)}, u32[]{:S(2)}, u32[]{:S(2)}) collective-permute-start(f32[160,128]{1,0:T(8,128)S(1)} %add_add_fusion.1), channel_id=1, source_target_pairs={{0,32},{4,36},{8,40},{12,44},{16,48},{20,52},{24,56},{28,60},{32,0... | collective-permute-start | bytes 245768 | tf_op jit(solution)/shard_map/ppermute | solution.py:403
  95.1 7.1 %collective-permute-start.22 = (f32[160,128]{1,0:T(8,128)S(1)}, f32[160,128]{1,0:T(8,128)S(1)}, u32[]{:S(2)}, u32[]{:S(2)}) collective-permute-start(f32[160,128]{1,0:T(8,128)S(1)} %add.58), channel_id=1, source_target_pairs={{0,24},{4,28},{8,16},{12,20},{16,8},{20,12},{24,0},{28,4},{32,56},... | collective-permute-start | bytes 245768 | tf_op jit(solution)/shard_map/ppermute | solution.py:403
  97.4 7.2 %collective-permute-start.21 = (f32[160,128]{1,0:T(8,128)S(1)}, f32[160,128]{1,0:T(8,128)S(1)}, u32[]{:S(2)}, u32[]{:S(2)}) collective-permute-start(f32[160,128]{1,0:T(8,128)S(1)} %add.58), channel_id=1, source_target_pairs={{0,16},{4,20},{8,24},{12,28},{16,0},{20,4},{24,8},{28,12},{32,48},... | collective-permute-start | bytes 245768 | tf_op jit(solution)/shard_map/ppermute | solution.py:403
  104.6 7.0 %collective-permute-start.25 = (f32[160,128]{1,0:T(8,128)S(1)}, f32[160,128]{1,0:T(8,128)S(1)}, u32[]{:S(2)}, u32[]{:S(2)}) collective-permute-start(f32[160,128]{1,0:T(8,128)S(1)} %add_add_fusion.g0), channel_id=1, source_target_pairs={{0,3},{1,2},{2,1},{3,0},{4,7},{5,6},{6,5},{7,4},{8,11},{9,10},{10,... | collective-permute-start | bytes 245768 | tf_op jit(solution)/shard_map/ppermute | solution.py:403
  105.8 5.9 %collective-permute-start.24 = (f32[160,128]{1,0:T(8,128)S(1)}, f32[160,128]{1,0:T(8,128)S(1)}, u32[]{:S(2)}, u32[]{:S(2)}) collective-permute-start(f32[160,128]{1,0:T(8,128)S(1)} %add_add_fusion.g0), channel_id=1, source_target_pairs={{0,2},{1,3},{2,0},{3,1},{4,6},{5,7},{6,4},{7,5},{8,10},{9,11},{10,... | collective-permute-start | bytes 245768 | tf_op jit(solution)/shard_map/ppermute | solution.py:403
  105.8 6.3 %collective-permute-start.23 = (f32[160,128]{1,0:T(8,128)S(1)}, f32[160,128]{1,0:T(8,128)S(1)}, u32[]{:S(2)}, u32[]{:S(2)}) collective-permute-start(f32[160,128]{1,0:T(8,128)S(1)} %add_add_fusion.g0), channel_id=1, source_target_pairs={{0,1},{1,0},{2,3},{3,2},{4,5},{5,4},{6,7},{7,6},{8,9},{9,8},{10,11... | collective-permute-start | bytes 245768 | tf_op jit(solution)/shard_map/ppermute | solution.py:403
  (12 other events, 159.1 us)

commit v4 on v3

--- a/solution.py
+++ b/solution.py
@@ -12,6 +12,7 @@
 VMEM = pltpu.VMEM
 LIMIT = 24 * 1024 * 1024
 LARGE = 48 * 1024 * 1024
+PARTNERS = (0, 1, 3, 2)
 NT = (((1,), (1,)), ((), ()))
 NN = (((1,), (0,)), ((), ()))
 
@@ -134,18 +135,25 @@
     return [VMEM(vals.shape, vals.dtype), pltpu.SemaphoreType.DMA((vals.shape[0] // group,))]
 
 
+def list_scratch(cols):
+    return [pltpu.SMEM(cols.shape, cols.dtype), pltpu.SemaphoreType.DMA]
+
+
 def fetch(vals_ref, held, sems, s, group, first=0):
     return pltpu.make_async_copy(
         vals_ref.at[pl.ds(first + s * group, group)], held.at[pl.ds(s * group, group)], sems.at[s]
     )
 
 
-def transpose_agg_kernel(cols_ref, me_ref, grad_ref, vals_ref, o0, o1, o2, o3, acc, held, sems):
+def transpose_agg_kernel(list_ref, me_ref, grad_ref, vals_ref, o0, o1, o2, o3, acc, cols_ref, col_sem, held, sems):
     row_tiles, tiles = vals_ref.shape[:2]
     classes = grad_ref.shape[0]
+    lists = pltpu.make_async_copy(list_ref, cols_ref, col_sem)
+    lists.start()
     for s in range(row_tiles // UNROLL):
         fetch(vals_ref, held, sems, s, UNROLL).start()
     acc[...] = jnp.zeros_like(acc)
+    lists.wait()
 
     def body(s, carry):
         fetch(vals_ref, held, sems, s, UNROLL).wait()
@@ -172,9 +180,9 @@
     return pl.pallas_call(
         transpose_agg_kernel,
         out_shape=(jax.ShapeDtypeStruct((width, 2048), BF),) * 4,
-        in_specs=[smem(), smem(), whole(), anywhere()],
+        in_specs=[anywhere(), smem(), whole(), anywhere()],
         out_specs=[whole()] * 4,
-        scratch_shapes=[VMEM((64, width, 128), F32)] + held_scratch(vals, UNROLL),
+        scratch_shapes=[VMEM((64, width, 128), F32)] + list_scratch(cols) + held_scratch(vals, UNROLL),
         compiler_params=params(LARGE),
         cost_estimate=cost(2 * 48 * 128 * 128 * 320 * 4, 11 << 20),
         name="agg_transposed",
@@ -189,14 +197,33 @@
 
 
 def agg_one_kernel(
-    cols_ref, me_ref, panel_ref, recv_ref, idx_ref, vals_ref, packed_ref, o0, o1, o2, o3, ext, stack, held, sems
+    list_ref,
+    me_ref,
+    panel_ref,
+    recv_ref,
+    idx_ref,
+    vals_ref,
+    packed_ref,
+    o0,
+    o1,
+    o2,
+    o3,
+    ext,
+    stack,
+    cols_ref,
+    col_sem,
+    held,
+    sems,
 ):
     row_tiles = vals_ref.shape[0]
+    lists = pltpu.make_async_copy(list_ref, cols_ref, col_sem)
+    lists.start()
     for s in range(row_tiles // UNROLL):
         fetch(vals_ref, held, sems, s, UNROLL).start()
     for e in range(32):
         ext[e] = panel_ref[:, e * 128 : (e + 1) * 128]
         ext[32 + e] = unpack_pair(recv_ref[2 * e], recv_ref[2 * e + 1])
+    lists.wait()
 
     def body(s, carry):
         fetch(vals_ref, held, sems, s, UNROLL).wait()
@@ -221,9 +248,11 @@
     return pl.pallas_call(
         agg_one_kernel,
         out_shape=(jax.ShapeDtypeStruct((pieces, 16, 128), BF),) + (out,) * 4,
-        in_specs=[smem(), smem(), whole(), whole(), whole(), anywhere()],
+        in_specs=[anywhere(), smem(), whole(), whole(), whole(), anywhere()],
         out_specs=[whole()] * 5,
-        scratch_shapes=[VMEM((64, 32, 128), BF), VMEM((512, 256), BF)] + held_scratch(vals, UNROLL),
+        scratch_shapes=[VMEM((64, 32, 128), BF), VMEM((512, 256), BF)]
+        + list_scratch(cols)
+        + held_scratch(vals, UNROLL),
         compiler_params=params(LARGE),
         cost_estimate=cost(2 * 32 * 128 * 128 * 320 * 8, 11 << 20),
         name="agg_one",
@@ -269,7 +298,8 @@
         f = me ^ d
         at = pl.multiple_of(f * 32, 32)
         for e in range(8):
-            mix[pl.ds(at, 32), e * 128 : (e + 1) * 128] = unpack_pair(far[d][2 * e], far[d][2 * e + 1])
+            pair = far[PARTNERS.index(d)]
+            mix[pl.ds(at, 32), e * 128 : (e + 1) * 128] = unpack_pair(pair[2 * e], pair[2 * e + 1])
         zed[pl.ds(pl.multiple_of(f * 48, 16), 48), :] = zs[d][:, 1024:]
     p1, p2 = dense_body(mix, zed, w1t, w2, w2t, hid, gp, yall)
     for d in range(4):
@@ -374,7 +404,7 @@
 
 def finish_kernel(me_ref, g0, g1, g2, g3, one_ref, two_ref, buf):
     me = me_ref[0]
-    for d, g in enumerate((g0, g1, g2, g3)):
+    for d, g in zip(PARTNERS, (g0, g1, g2, g3)):
         buf[pl.ds(pl.multiple_of((me ^ d) * 160, 8), 160), :] = g[...]
     one_ref[:, :128] = buf[0:128]
     one_ref[:, 128:] = buf[128:256]
@@ -407,11 +437,6 @@
     return lax.optimization_barrier((x, *others))[0]
 
 
-def swap_sum(blocks, move):
-    moved = [move(blocks[d], d) for d in (1, 2, 3)]
-    return (blocks[0] + moved[0]) + (moved[1] + moved[2])
-
-
 def on_device(
     features, weight_one, weight_two, grad_logits, send_idx, send_count, tile_cols, tile_vals
 ):
@@ -451,19 +476,21 @@
         return lax.dynamic_slice_in_dim(received_two, (me ^ d) * pieces, pieces, 0)
 
     near = far_block(0)
-    far = [near] + [swap_feat(far_block(d), d) for d in (1, 2, 3)]
+    far = [near] + [swap_feat(far_block(d), d) for d in PARTNERS[1:]]
     own[0] = after(own[0], near)
     y_own, p1, p2 = dense_own_call(me_arr, own, zs, w1t, w2, w2t)
     outs = dense_far_call(me_arr, far, zs, w1t, w2, w2t, y_own, p1, p2)
     ys, gs = outs[:4], outs[4:]
-    total = swap_sum(gs, swap_feat)
+    moved = [swap_feat(gs[d], d) for d in (1, 2, 3)]
+    total = (moved[1] + moved[2]) + (gs[0] + moved[0])
     ys = [ys[0]] + [swap_feat(ys[d], d) for d in (1, 2, 3)]
     total = total + swap_dom(total, 1)
-    total = swap_sum([total] * 4, lambda x, d: swap_dom(x, 16 * d))
+    moved = [swap_dom(total, 16 * d) for d in (1, 2, 3)]
+    total = (total + moved[0]) + (moved[2] + moved[1])
     ext = spread_call(me_arr, ys)
     out = []
     row_tiles = tile_cols.shape[0]
-    cuts = [0, row_tiles // 8, row_tiles * 9 // 16, row_tiles]
+    cuts = [0, row_tiles // 16, row_tiles * 21 // 32, row_tiles]
 
     def beside(moved):
         first, last = cuts[len(out) : len(out) + 2]
@@ -477,9 +504,9 @@
     total = total + moved
     ext, total = lax.optimization_barrier((ext, total))
     moved = beside([swap_dom(total, d) for d in (2, 4, 6)])
-    total = (total + moved[0]) + (moved[1] + moved[2])
+    total = (total + moved[0]) + (moved[2] + moved[1])
     ext, total = lax.optimization_barrier((ext, total))
-    moved = beside([swap_feat(total, d) for d in (1, 2, 3)])
+    moved = beside([swap_feat(total, d) for d in PARTNERS[1:]])
     logits = out[-1]
     grad_one, grad_two = finish_call(me_arr, [total] + moved, feat * class_cols)
     return (logits.T, grad_one, grad_two.T)

time: 113 us -> 112 us (level)
  waiting for transfers between devices: 17.2 us -> 21.7 us
  starting transfers between devices: 61.2 us -> 57 us
  Pallas kernels: 27.5 us -> 26.2 us
    ppermute x26, waiting for transfers between devices: 11.1 us -> 15 us  [swap(): return lax.ppermute(x, axis, [(i, i ^ mask) for i in range(size)])]
    ppermute x26, starting transfers between devices: 39.2 us -> 35.7 us  [swap(): return lax.ppermute(x, axis, [(i, i ^ mask) for i in range(size)])]
  transfers between devices with their start and end apart: 28 -> 28, of which waited for: 14 -> 15; matrix products, arithmetic and copies ran while one was open for 0% -> 0% of each run, Pallas kernels for 19% -> 18%
where the time goes in v4:
time: 112 us
  starting transfers between devices  57 us (51%)
  Pallas kernels  26.2 us (23%)
  waiting for transfers between devices  21.7 us (19%)
  local copies, waits for them, and re-layouts  5.96 us (5%)
    ppermute x26, starting transfers between devices, swap(): return lax.ppermute(x, axis, [(i, i ^ mask) for i in range(size)])  35.7 us
    ppermute x26, waiting for transfers between devices, swap(): return lax.ppermute(x, axis, [(i, i ^ mask) for i in range(size)])  15 us
    all_to_all x1, starting transfers between devices, on_device(): lax.all_to_all(packed_one, 'dom', split_axis=0, concat_axis=0, tiled=True)  12 us
    all_to_all x1, starting transfers between devices, on_device(): lax.all_to_all(packed_two, 'dom', split_axis=0, concat_axis=0, tiled=True)  9.26 us
    pallas_call x1, Pallas kernels, agg_one_call(): pl.pallas_call(agg_one_kernel, out_shape=(jax.ShapeDtypeStruct((pieces, 1...  7.73 us
    pallas_call x3, Pallas kernels, agg_two_call(): pl.pallas_call(kernel, out_shape=jax.ShapeDtypeStruct((classes, lead + co...  6.06 us
    unnamed x17, local copies, waits for them, and re-layouts  5.8 us
    all_to_all x1, waiting for transfers between devices, on_device(): lax.all_to_all(packed_two, 'dom', split_axis=0, concat_axis=0, tiled=True)  5.63 us
  transfers between devices with their start and end apart: 28, of which 15 were waited for; matrix products, arithmetic and copies ran while one was open for 0% of the time, Pallas kernels for 18%

profile of v4, /device:TPU:2, one launch (start us, length us, event | category | flops | bytes accessed | tf_op | source)
XLA Modules:
  0.0 111.8 jit_solution(14506443554763400051)
XLA Ops:
  0.7 3.5 %gather_rows.1 = (bf16[64,16,128]{2,1,0:T(8,128)(2,1)}, s32[16,256]{1,0:T(8,128)}) custom-call(s32[64]{0:T(128)} %live_ref.1, bf16[32,4096]{1,0:T(8,128)(2,1)} %bitcast.16, s32[64,64]{1,0:T(8,128)} %send_ref.1), custom_call_target="tpu_custom_call" | custom-call | flops 1073741824 | bytes 1048576 | tf_op jit(solution)/shard_map/gather_rows/pallas_call | solution.py:103
  4.2 12.0 %all-to-all-start = ((bf16[64,16,128]{2,1,0:T(8,128)(2,1)}), bf16[64,16,128]{2,1,0:T(8,128)(2,1)S(1)}, u32[]{:S(2)}, u32[]{:S(2)}) async-start(bf16[64,16,128]{2,1,0:T(8,128)(2,1)} %get-tuple-element.46), calls=%async_computation | async-start | bytes 524288 | tf_op jit(solution)/shard_map/all_to_all | solution.py:465
  17.9 4.9 %agg_transposed.1 = (bf16[48,2048]{1,0:T(8,128)(2,1)S(1)}, bf16[48,2048]{1,0:T(8,128)(2,1)S(1)}, bf16[48,2048]{1,0:T(8,128)(2,1)S(1)}, bf16[48,2048]{1,0:T(8,128)(2,1)S(1)}) custom-call(s32[10,32]{1,0:T(8,128)S(1)} %bitcast.18, s32[1]{0:T(128)} %bitcast.me_ref, bf16[43,4096]{1,0:T(8,128)(2,1)S(1)} %bitcast.12, bf16[32,10,128,128]{3,2,1,0:T(8,128)(2,1)} %vals_ref.9), custom_call_target="tpu_custom_call" | custom-call | flops 2013265920 | bytes 11534336 | tf_op jit(solution)/shard_map/agg_transposed/pallas_call | solution.py:180
  22.8 1.7 %collective-permute-start = (bf16[48,2048]{1,0:T(8,128)(2,1)S(1)}, bf16[48,2048]{1,0:T(8,128)(2,1)S(1)}, u32[]{:S(2)}, u32[]{:S(2)}) collective-permute-start(bf16[48,2048]{1,0:T(8,128)(2,1)S(1)} %get-tuple-element.51), channel_id=1, source_target_pairs={{0,1},{1,0},{2,3},{3,2},{4,5},{5,4},{6,7},{7,6},{8,9},{9,8},{10,11... | collective-permute-start | bytes 589832 | tf_op jit(solution)/shard_map/ppermute | solution.py:433
  24.5 2.2 %collective-permute-start.1 = (bf16[48,2048]{1,0:T(8,128)(2,1)S(1)}, bf16[48,2048]{1,0:T(8,128)(2,1)S(1)}, u32[]{:S(2)}, u32[]{:S(2)}) collective-permute-start(bf16[48,2048]{1,0:T(8,128)(2,1)S(1)} %get-tuple-element.52), channel_id=1, source_target_pairs={{0,3},{1,2},{2,1},{3,0},{4,7},{5,6},{6,5},{7,4},{8,11},{9,10},{10,... | collective-permute-start | bytes 589832 | tf_op jit(solution)/shard_map/ppermute | solution.py:433
  27.8 7.7 %agg_one.1 = (bf16[64,16,128]{2,1,0:T(8,128)(2,1)}, bf16[32,1024]{1,0:T(8,128)(2,1)S(1)}, bf16[32,1024]{1,0:T(8,128)(2,1)S(1)}, bf16[32,1024]{1,0:T(8,128)(2,1)S(1)}, bf16[32,1024]{1,0:T(8,128)(2,1)S(1)}) custom-call(s32[10,32]{1,0:T(8,128)S(1)} %bitcast.19, s32[1]{0:T(128)} %bitcast.me_ref, bf16[32,4096]{1,0:T(8,128)(2,1)S(1)} %bitcast.17, ...), custom_call_target="tpu_custom_call" | custom-call | flops 2684354560 | bytes 11534336 | tf_op jit(solution)/shard_map/agg_one/pallas_call | solution.py:248
  35.5 9.3 %all-to-all-start.1 = ((bf16[64,16,128]{2,1,0:T(8,128)(2,1)}), bf16[64,16,128]{2,1,0:T(8,128)(2,1)S(1)}, u32[]{:S(2)}, u32[]{:S(2)}) async-start(bf16[64,16,128]{2,1,0:T(8,128)(2,1)} %get-tuple-element.53), calls=%async_computation.1 | async-start | bytes 524288 | tf_op jit(solution)/shard_map/all_to_all | solution.py:471
  47.2 2.9 %collective-permute-start.7 = (bf16[32,1024]{1,0:T(8,128)(2,1)S(1)}, bf16[32,1024]{1,0:T(8,128)(2,1)S(1)}, u32[]{:S(2)}, u32[]{:S(2)}) collective-permute-start(bf16[32,1024]{1,0:T(8,128)(2,1)S(1)} %get-tuple-element.58), channel_id=1, source_target_pairs={{0,2},{1,3},{2,0},{3,1},{4,6},{5,7},{6,4},{7,5},{8,10},{9,11},{10,... | collective-permute-start | bytes 196616 | tf_op jit(solution)/shard_map/ppermute | solution.py:433
  50.7 5.6 %all-to-all-done.1 = bf16[64,16,128]{2,1,0:T(8,128)(2,1)S(1)} async-done(((bf16[64,16,128]{2,1,0:T(8,128)(2,1)}), bf16[64,16,128]{2,1,0:T(8,128)(2,1)S(1)}, u32[]{:S(2)}, u32[]{:S(2)}) %all-to-all-start.1) | async-done | bytes 262176 | tf_op jit(solution)/shard_map/all_to_all | solution.py:471
  57.2 2.6 %collective-permute-start.3 = (bf16[16,16,128]{2,1,0:T(8,128)(2,1)S(1)}, bf16[16,16,128]{2,1,0:T(8,128)(2,1)S(1)}, u32[]{:S(2)}, u32[]{:S(2)}) collective-permute-start(bf16[16,16,128]{2,1,0:T(8,128)(2,1)S(1)} %get-tuple-element.90), channel_id=1, source_target_pairs={{0,3},{1,2},{2,1},{3,0},{4,7},{5,6},{6,5},{7,4},{8,11},{9,10},{10,... | collective-permute-start | bytes 196616 | tf_op jit(solution)/shard_map/ppermute | solution.py:433
  64.1 1.7 %dense_far.1 = (bf16[48,2048]{1,0:T(8,128)(2,1)S(1)}, bf16[48,2048]{1,0:T(8,128)(2,1)S(1)}, bf16[48,2048]{1,0:T(8,128)(2,1)S(1)}, bf16[48,2048]{1,0:T(8,128)(2,1...) custom-call(s32[1]{0:T(128)} %bitcast.me_ref, ...), custom_call_target="tpu_custom_call" | custom-call | flops 786432000 | bytes 4194304 | tf_op jit(solution)/shard_map/dense_far/pallas_call | solution.py:346
  66.6 2.1 %collective-permute-start.13 = (f32[160,128]{1,0:T(8,128)S(1)}, f32[160,128]{1,0:T(8,128)S(1)}, u32[]{:S(2)}, u32[]{:S(2)}) collective-permute-start(f32[160,128]{1,0:T(8,128)S(1)} %get-tuple-element.68), channel_id=1, source_target_pairs={{0,3},{1,2},{2,1},{3,0},{4,7},{5,6},{6,5},{7,4},{8,11},{9,10},{10,... | collective-permute-start | bytes 245768 | tf_op jit(solution)/shard_map/ppermute | solution.py:433
  75.4 2.4 %collective-permute-start.18 = (f32[160,128]{1,0:T(8,128)S(1)}, f32[160,128]{1,0:T(8,128)S(1)}, u32[]{:S(2)}, u32[]{:S(2)}) collective-permute-start(f32[160,128]{1,0:T(8,128)S(1)} %add.54), channel_id=1, source_target_pairs={{0,128},{4,132},{8,136},{12,140},{16,144},{20,148},{24,152},{28,15... | collective-permute-start | bytes 245768 | tf_op jit(solution)/shard_map/ppermute | solution.py:433
  78.2 2.0 %collective-permute-start.16 = (f32[160,128]{1,0:T(8,128)S(1)}, f32[160,128]{1,0:T(8,128)S(1)}, u32[]{:S(2)}, u32[]{:S(2)}) collective-permute-start(f32[160,128]{1,0:T(8,128)S(1)} %add.54), channel_id=1, source_target_pairs={{0,64},{4,68},{8,72},{12,76},{16,80},{20,84},{24,88},{28,92},{32,9... | collective-permute-start | bytes 245768 | tf_op jit(solution)/shard_map/ppermute | solution.py:433
  80.2 1.5 %collective-permute-done.10.refs_2_ = bf16[48,2048]{1,0:T(8,128)(2,1)S(1)} collective-permute-done((bf16[48,2048]{1,0:T(8,128)(2,1)S(1)}, bf16[48,2048]{1,0:T(8,128)(2,1)S(1)}, u32[]{:S(2)}, u32[]{:S(2)}) %collective-permute-start.10) | collective-permute-done | bytes 196640 | tf_op jit(solution)/shard_map/ppermute | solution.py:433
  83.5 2.5 %collective-permute-start.19 = (f32[160,128]{1,0:T(8,128)S(1)}, f32[160,128]{1,0:T(8,128)S(1)}, u32[]{:S(2)}, u32[]{:S(2)}) collective-permute-start(f32[160,128]{1,0:T(8,128)S(1)} %add_add_fusion.1), channel_id=1, source_target_pairs={{0,32},{4,36},{8,40},{12,44},{16,48},{20,52},{24,56},{28,60},{32,0... | collective-permute-start | bytes 245768 | tf_op jit(solution)/shard_map/ppermute | solution.py:433
  85.9 4.0 %copy-done = bf16[32,10,128,128]{3,2,1,0:T(8,128)(2,1)S(1)} copy-done((bf16[32,10,128,128]{3,2,1,0:T(8,128)(2,1)S(1)}, bf16[32,10,128,128]{3,2,1,0:T(8,128)(2,1)}, u32[]{:S(2)}) %copy-start) | copy-done | bytes 10485784
  90.9 2.4 %collective-permute-done.19 = f32[160,128]{1,0:T(8,128)S(1)} collective-permute-done((f32[160,128]{1,0:T(8,128)S(1)}, f32[160,128]{1,0:T(8,128)S(1)}, u32[]{:S(2)}, u32[]{:S(2)}) %collective-permute-start.19) | collective-permute-done | bytes 81952 | tf_op jit(solution)/shard_map/ppermute | solution.py:433
  94.1 2.0 %collective-permute-start.21 = (f32[160,128]{1,0:T(8,128)S(1)}, f32[160,128]{1,0:T(8,128)S(1)}, u32[]{:S(2)}, u32[]{:S(2)}) collective-permute-start(f32[160,128]{1,0:T(8,128)S(1)} %add.58), channel_id=1, source_target_pairs={{0,16},{4,20},{8,24},{12,28},{16,0},{20,4},{24,8},{28,12},{32,48},... | collective-permute-start | bytes 245768 | tf_op jit(solution)/shard_map/ppermute | solution.py:433
  96.1 1.8 %collective-permute-start.20 = (f32[160,128]{1,0:T(8,128)S(1)}, f32[160,128]{1,0:T(8,128)S(1)}, u32[]{:S(2)}, u32[]{:S(2)}) collective-permute-start(f32[160,128]{1,0:T(8,128)S(1)} %add.58), channel_id=1, source_target_pairs={{0,8},{4,12},{8,0},{12,4},{16,24},{20,28},{24,16},{28,20},{32,40},... | collective-permute-start | bytes 245768 | tf_op jit(solution)/shard_map/ppermute | solution.py:433
  97.8 2.5 %agg_two.4.refs_1_ = bf16[43,2432]{1,0:T(8,128)(2,1)S(1)} custom-call(s32[10,32]{1,0:T(8,128)S(1)} %bitcast.21, bf16[64,48,128]{2,1,0:T(8,128)(2,1)S(1)} %spread.1.ext_ref, bf16[32,10,128,128]{3,2,1,0:T(8,128)(2,1)S(1)} %copy-done), custom_call_target="tpu_custom_call" | custom-call | flops 1195376640 | bytes 6270000 | tf_op jit(solution)/shard_map/agg_two/pallas_call | solution.py:394
  100.4 3.0 %collective-permute-done.21 = f32[160,128]{1,0:T(8,128)S(1)} collective-permute-done((f32[160,128]{1,0:T(8,128)S(1)}, f32[160,128]{1,0:T(8,128)S(1)}, u32[]{:S(2)}, u32[]{:S(2)}) %collective-permute-start.21) | collective-permute-done | bytes 81952 | tf_op jit(solution)/shard_map/ppermute | solution.py:433
  103.4 1.6 %collective-permute-start.25 = (f32[160,128]{1,0:T(8,128)S(1)}, f32[160,128]{1,0:T(8,128)S(1)}, u32[]{:S(2)}, u32[]{:S(2)}) collective-permute-start(f32[160,128]{1,0:T(8,128)S(1)} %add_add_fusion.g0), channel_id=1, source_target_pairs={{0,2},{1,3},{2,0},{3,1},{4,6},{5,7},{6,4},{7,5},{8,10},{9,11},{10,... | collective-permute-start | bytes 245768 | tf_op jit(solution)/shard_map/ppermute | solution.py:433
  107.0 2.5 %agg_two.5 = bf16[43,4096]{1,0:T(8,128)(2,1)} custom-call(s32[10,32]{1,0:T(8,128)S(1)} %bitcast.22, bf16[64,48,128]{2,1,0:T(8,128)(2,1)S(1)} %spread.1.ext_ref, bf16[32,10,128,128]{3,2,1,0:T(8,128)(2,1)S(1)} %copy-done, bf16[43,256]{1,0:T(8,128)(2,1)S(1)} %agg_two.3.refs_0_, bf16[43,2432]{1,0:T(8,128)(2,1)S(1)} %agg_two.4.refs_1_), custom_call_target="tpu_custom_call" | custom-call | flops 692060160 | bytes 3630000 | tf_op jit(solution)/shard_map/agg_two/pallas_call | solution.py:394
  (68 shorter events, 26.6 us)
Async XLA Ops:
  4.2 23.6 %all-to-all-start = ((bf16[64,16,128]{2,1,0:T(8,128)(2,1)}), bf16[64,16,128]{2,1,0:T(8,128)(2,1)S(1)}, u32[]{:S(2)}, u32[]{:S(2)}) async-start(bf16[64,16,128]{2,1,0:T(8,128)(2,1)} %get-tuple-element.46), calls=%async_computation | async-start | bytes 524288 | tf_op jit(solution)/shard_map/all_to_all | solution.py:465
  22.8 12.7 %collective-permute-start = (bf16[48,2048]{1,0:T(8,128)(2,1)S(1)}, bf16[48,2048]{1,0:T(8,128)(2,1)S(1)}, u32[]{:S(2)}, u32[]{:S(2)}) collective-permute-start(bf16[48,2048]{1,0:T(8,128)(2,1)S(1)} %get-tuple-element.51), channel_id=1, source_target_pairs={{0,1},{1,0},{2,3},{3,2},{4,5},{5,4},{6,7},{7,6},{8,9},{9,8},{10,11... | collective-permute-start | bytes 589832 | tf_op jit(solution)/shard_map/ppermute | solution.py:433
  24.5 11.0 %collective-permute-start.1 = (bf16[48,2048]{1,0:T(8,128)(2,1)S(1)}, bf16[48,2048]{1,0:T(8,128)(2,1)S(1)}, u32[]{:S(2)}, u32[]{:S(2)}) collective-permute-start(bf16[48,2048]{1,0:T(8,128)(2,1)S(1)} %get-tuple-element.52), channel_id=1, source_target_pairs={{0,3},{1,2},{2,1},{3,0},{4,7},{5,6},{6,5},{7,4},{8,11},{9,10},{10,... | collective-permute-start | bytes 589832 | tf_op jit(solution)/shard_map/ppermute | solution.py:433
  35.5 20.8 %all-to-all-start.1 = ((bf16[64,16,128]{2,1,0:T(8,128)(2,1)}), bf16[64,16,128]{2,1,0:T(8,128)(2,1)S(1)}, u32[]{:S(2)}, u32[]{:S(2)}) async-start(bf16[64,16,128]{2,1,0:T(8,128)(2,1)} %get-tuple-element.53), calls=%async_computation.1 | async-start | bytes 524288 | tf_op jit(solution)/shard_map/all_to_all | solution.py:471
  44.8 12.4 %collective-permute-start.5 = (bf16[48,2048]{1,0:T(8,128)(2,1)S(1)}, bf16[48,2048]{1,0:T(8,128)(2,1)S(1)}, u32[]{:S(2)}, u32[]{:S(2)}) collective-permute-start(bf16[48,2048]{1,0:T(8,128)(2,1)S(1)} %get-tuple-element.54), channel_id=1, source_target_pairs={{0,2},{1,3},{2,0},{3,1},{4,6},{5,7},{6,4},{7,5},{8,10},{9,11},{10,... | collective-permute-start | bytes 589832 | tf_op jit(solution)/shard_map/ppermute | solution.py:433
  45.9 13.9 %collective-permute-start.6 = (bf16[32,1024]{1,0:T(8,128)(2,1)S(1)}, bf16[32,1024]{1,0:T(8,128)(2,1)S(1)}, u32[]{:S(2)}, u32[]{:S(2)}) collective-permute-start(bf16[32,1024]{1,0:T(8,128)(2,1)S(1)} %get-tuple-element.57), channel_id=1, source_target_pairs={{0,1},{1,0},{2,3},{3,2},{4,5},{5,4},{6,7},{7,6},{8,9},{9,8},{10,11... | collective-permute-start | bytes 196616 | tf_op jit(solution)/shard_map/ppermute | solution.py:433
  47.2 12.8 %collective-permute-start.7 = (bf16[32,1024]{1,0:T(8,128)(2,1)S(1)}, bf16[32,1024]{1,0:T(8,128)(2,1)S(1)}, u32[]{:S(2)}, u32[]{:S(2)}) collective-permute-start(bf16[32,1024]{1,0:T(8,128)(2,1)S(1)} %get-tuple-element.58), channel_id=1, source_target_pairs={{0,2},{1,3},{2,0},{3,1},{4,6},{5,7},{6,4},{7,5},{8,10},{9,11},{10,... | collective-permute-start | bytes 196616 | tf_op jit(solution)/shard_map/ppermute | solution.py:433
  50.1 9.8 %collective-permute-start.8 = (bf16[32,1024]{1,0:T(8,128)(2,1)S(1)}, bf16[32,1024]{1,0:T(8,128)(2,1)S(1)}, u32[]{:S(2)}, u32[]{:S(2)}) collective-permute-start(bf16[32,1024]{1,0:T(8,128)(2,1)S(1)} %get-tuple-element.59), channel_id=1, source_target_pairs={{0,3},{1,2},{2,1},{3,0},{4,7},{5,6},{6,5},{7,4},{8,11},{9,10},{10,... | collective-permute-start | bytes 196616 | tf_op jit(solution)/shard_map/ppermute | solution.py:433
  56.4 6.1 %collective-permute-start.4 = (bf16[16,16,128]{2,1,0:T(8,128)(2,1)S(1)}, bf16[16,16,128]{2,1,0:T(8,128)(2,1)S(1)}, u32[]{:S(2)}, u32[]{:S(2)}) collective-permute-start(bf16[16,16,128]{2,1,0:T(8,128)(2,1)S(1)} %get-tuple-element.89), channel_id=1, source_target_pairs={{0,2},{1,3},{2,0},{3,1},{4,6},{5,7},{6,4},{7,5},{8,10},{9,11},{10,... | collective-permute-start | bytes 196616 | tf_op jit(solution)/shard_map/ppermute | solution.py:433
  57.2 6.3 %collective-permute-start.3 = (bf16[16,16,128]{2,1,0:T(8,128)(2,1)S(1)}, bf16[16,16,128]{2,1,0:T(8,128)(2,1)S(1)}, u32[]{:S(2)}, u32[]{:S(2)}) collective-permute-start(bf16[16,16,128]{2,1,0:T(8,128)(2,1)S(1)} %get-tuple-element.90), channel_id=1, source_target_pairs={{0,3},{1,2},{2,1},{3,0},{4,7},{5,6},{6,5},{7,4},{8,11},{9,10},{10,... | collective-permute-start | bytes 196616 | tf_op jit(solution)/shard_map/ppermute | solution.py:433
  65.8 6.9 %collective-permute-start.12 = (f32[160,128]{1,0:T(8,128)S(1)}, f32[160,128]{1,0:T(8,128)S(1)}, u32[]{:S(2)}, u32[]{:S(2)}) collective-permute-start(f32[160,128]{1,0:T(8,128)S(1)} %get-tuple-element.67), channel_id=1, source_target_pairs={{0,2},{1,3},{2,0},{3,1},{4,6},{5,7},{6,4},{7,5},{8,10},{9,11},{10,... | collective-permute-start | bytes 245768 | tf_op jit(solution)/shard_map/ppermute | solution.py:433
  66.6 7.5 %collective-permute-start.13 = (f32[160,128]{1,0:T(8,128)S(1)}, f32[160,128]{1,0:T(8,128)S(1)}, u32[]{:S(2)}, u32[]{:S(2)}) collective-permute-start(f32[160,128]{1,0:T(8,128)S(1)} %get-tuple-element.68), channel_id=1, source_target_pairs={{0,3},{1,2},{2,1},{3,0},{4,7},{5,6},{6,5},{7,4},{8,11},{9,10},{10,... | collective-permute-start | bytes 245768 | tf_op jit(solution)/shard_map/ppermute | solution.py:433
  68.6 5.4 %collective-permute-start.14 = (f32[160,128]{1,0:T(8,128)S(1)}, f32[160,128]{1,0:T(8,128)S(1)}, u32[]{:S(2)}, u32[]{:S(2)}) collective-permute-start(f32[160,128]{1,0:T(8,128)S(1)} %get-tuple-element.70), channel_id=1, source_target_pairs={{0,1},{1,0},{2,3},{3,2},{4,5},{5,4},{6,7},{7,6},{8,9},{9,8},{10,11... | collective-permute-start | bytes 245768 | tf_op jit(solution)/shard_map/ppermute | solution.py:433
  69.3 8.9 %collective-permute-start.9 = (bf16[48,2048]{1,0:T(8,128)(2,1)S(1)}, bf16[48,2048]{1,0:T(8,128)(2,1)S(1)}, u32[]{:S(2)}, u32[]{:S(2)}) collective-permute-start(bf16[48,2048]{1,0:T(8,128)(2,1)S(1)} %get-tuple-element.64), channel_id=1, source_target_pairs={{0,1},{1,0},{2,3},{3,2},{4,5},{5,4},{6,7},{7,6},{8,9},{9,8},{10,11... | collective-permute-start | bytes 589832 | tf_op jit(solution)/shard_map/ppermute | solution.py:433
  70.7 11.1 %collective-permute-start.10 = (bf16[48,2048]{1,0:T(8,128)(2,1)S(1)}, bf16[48,2048]{1,0:T(8,128)(2,1)S(1)}, u32[]{:S(2)}, u32[]{:S(2)}) collective-permute-start(bf16[48,2048]{1,0:T(8,128)(2,1)S(1)} %get-tuple-element.65), channel_id=1, source_target_pairs={{0,2},{1,3},{2,0},{3,1},{4,6},{5,7},{6,4},{7,5},{8,10},{9,11},{10,... | collective-permute-start | bytes 589832 | tf_op jit(solution)/shard_map/ppermute | solution.py:433
  72.7 10.4 %collective-permute-start.11 = (bf16[48,2048]{1,0:T(8,128)(2,1)S(1)}, bf16[48,2048]{1,0:T(8,128)(2,1)S(1)}, u32[]{:S(2)}, u32[]{:S(2)}) collective-permute-start(bf16[48,2048]{1,0:T(8,128)(2,1)S(1)} %get-tuple-element.66), channel_id=1, source_target_pairs={{0,3},{1,2},{2,1},{3,0},{4,7},{5,6},{6,5},{7,4},{8,11},{9,10},{10,... | collective-permute-start | bytes 589832 | tf_op jit(solution)/shard_map/ppermute | solution.py:433
  75.4 7.8 %collective-permute-start.18 = (f32[160,128]{1,0:T(8,128)S(1)}, f32[160,128]{1,0:T(8,128)S(1)}, u32[]{:S(2)}, u32[]{:S(2)}) collective-permute-start(f32[160,128]{1,0:T(8,128)S(1)} %add.54), channel_id=1, source_target_pairs={{0,128},{4,132},{8,136},{12,140},{16,144},{20,148},{24,152},{28,15... | collective-permute-start | bytes 245768 | tf_op jit(solution)/shard_map/ppermute | solution.py:433
  77.8 5.5 %collective-permute-start.17 = (f32[160,128]{1,0:T(8,128)S(1)}, f32[160,128]{1,0:T(8,128)S(1)}, u32[]{:S(2)}, u32[]{:S(2)}) collective-permute-start(f32[160,128]{1,0:T(8,128)S(1)} %add.54), channel_id=1, source_target_pairs={{0,192},{4,196},{8,200},{12,204},{16,208},{20,212},{24,216},{28,22... | collective-permute-start | bytes 245768 | tf_op jit(solution)/shard_map/ppermute | solution.py:433
  83.5 9.9 %collective-permute-start.19 = (f32[160,128]{1,0:T(8,128)S(1)}, f32[160,128]{1,0:T(8,128)S(1)}, u32[]{:S(2)}, u32[]{:S(2)}) collective-permute-start(f32[160,128]{1,0:T(8,128)S(1)} %add_add_fusion.1), channel_id=1, source_target_pairs={{0,32},{4,36},{8,40},{12,44},{16,48},{20,52},{24,56},{28,60},{32,0... | collective-permute-start | bytes 245768 | tf_op jit(solution)/shard_map/ppermute | solution.py:433
  93.4 7.0 %collective-permute-start.22 = (f32[160,128]{1,0:T(8,128)S(1)}, f32[160,128]{1,0:T(8,128)S(1)}, u32[]{:S(2)}, u32[]{:S(2)}) collective-permute-start(f32[160,128]{1,0:T(8,128)S(1)} %add.58), channel_id=1, source_target_pairs={{0,24},{4,28},{8,16},{12,20},{16,8},{20,12},{24,0},{28,4},{32,56},... | collective-permute-start | bytes 245768 | tf_op jit(solution)/shard_map/ppermute | solution.py:433
  94.1 9.3 %collective-permute-start.21 = (f32[160,128]{1,0:T(8,128)S(1)}, f32[160,128]{1,0:T(8,128)S(1)}, u32[]{:S(2)}, u32[]{:S(2)}) collective-permute-start(f32[160,128]{1,0:T(8,128)S(1)} %add.58), channel_id=1, source_target_pairs={{0,16},{4,20},{8,24},{12,28},{16,0},{20,4},{24,8},{28,12},{32,48},... | collective-permute-start | bytes 245768 | tf_op jit(solution)/shard_map/ppermute | solution.py:433
  96.1 7.3 %collective-permute-start.20 = (f32[160,128]{1,0:T(8,128)S(1)}, f32[160,128]{1,0:T(8,128)S(1)}, u32[]{:S(2)}, u32[]{:S(2)}) collective-permute-start(f32[160,128]{1,0:T(8,128)S(1)} %add.58), channel_id=1, source_target_pairs={{0,8},{4,12},{8,0},{12,4},{16,24},{20,28},{24,16},{28,20},{32,40},... | collective-permute-start | bytes 245768 | tf_op jit(solution)/shard_map/ppermute | solution.py:433
  103.4 6.1 %collective-permute-start.25 = (f32[160,128]{1,0:T(8,128)S(1)}, f32[160,128]{1,0:T(8,128)S(1)}, u32[]{:S(2)}, u32[]{:S(2)}) collective-permute-start(f32[160,128]{1,0:T(8,128)S(1)} %add_add_fusion.g0), channel_id=1, source_target_pairs={{0,2},{1,3},{2,0},{3,1},{4,6},{5,7},{6,4},{7,5},{8,10},{9,11},{10,... | collective-permute-start | bytes 245768 | tf_op jit(solution)/shard_map/ppermute | solution.py:433
  105.0 6.1 %collective-permute-start.24 = (f32[160,128]{1,0:T(8,128)S(1)}, f32[160,128]{1,0:T(8,128)S(1)}, u32[]{:S(2)}, u32[]{:S(2)}) collective-permute-start(f32[160,128]{1,0:T(8,128)S(1)} %add_add_fusion.g0), channel_id=1, source_target_pairs={{0,3},{1,2},{2,1},{3,0},{4,7},{5,6},{6,5},{7,4},{8,11},{9,10},{10,... | collective-permute-start | bytes 245768 | tf_op jit(solution)/shard_map/ppermute | solution.py:433
  (12 other events, 154.9 us)

commit v5 on v4

--- a/solution.py
+++ b/solution.py
@@ -56,7 +56,7 @@
             out_ref[j * 4 + pair * 2 + 1] = second.astype(BF)
         return carry
 
-    lax.fori_loop(0, idx_ref.shape[0], step, 0, unroll=8)
+    lax.fori_loop(0, idx_ref.shape[0], step, 0, unroll=16)
 
 
 def unpack_pair(first, second):
@@ -490,7 +490,7 @@
     ext = spread_call(me_arr, ys)
     out = []
     row_tiles = tile_cols.shape[0]
-    cuts = [0, row_tiles // 16, row_tiles * 21 // 32, row_tiles]
+    cuts = [0, row_tiles // 16, row_tiles * 23 // 32, row_tiles]
 
     def beside(moved):
         first, last = cuts[len(out) : len(out) + 2]

time: 112 us -> 112 us (level)
  transfers between devices with their start and end apart: 28 -> 28, of which waited for: 15 -> 16; matrix products, arithmetic and copies ran while one was open for 0% -> 0% of each run, Pallas kernels for 18% -> 18%
where the time goes in v5:
time: 112 us
  starting transfers between devices  57 us (51%)
  Pallas kernels  26 us (23%)
  waiting for transfers between devices  21.7 us (19%)
  local copies, waits for them, and re-layouts  5.96 us (5%)
    ppermute x26, starting transfers between devices, swap(): return lax.ppermute(x, axis, [(i, i ^ mask) for i in range(size)])  35.7 us
    ppermute x26, waiting for transfers between devices, swap(): return lax.ppermute(x, axis, [(i, i ^ mask) for i in range(size)])  15 us
    all_to_all x1, starting transfers between devices, on_device(): lax.all_to_all(packed_one, 'dom', split_axis=0, concat_axis=0, tiled=True)  12 us
    all_to_all x1, starting transfers between devices, on_device(): lax.all_to_all(packed_two, 'dom', split_axis=0, concat_axis=0, tiled=True)  9.28 us
    pallas_call x1, Pallas kernels, agg_one_call(): pl.pallas_call(agg_one_kernel, out_shape=(jax.ShapeDtypeStruct((pieces, 1...  7.62 us
    pallas_call x3, Pallas kernels, agg_two_call(): pl.pallas_call(kernel, out_shape=jax.ShapeDtypeStruct((classes, lead + co...  6.06 us
    unnamed x17, local copies, waits for them, and re-layouts  5.8 us
    all_to_all x1, waiting for transfers between devices, on_device(): lax.all_to_all(packed_two, 'dom', split_axis=0, concat_axis=0, tiled=True)  5.63 us
  transfers between devices with their start and end apart: 28, of which 16 were waited for; matrix products, arithmetic and copies ran while one was open for 0% of the time, Pallas kernels for 18%

profile of v5, /device:TPU:2, one launch (start us, length us, event | category | flops | bytes accessed | tf_op | source)
XLA Modules:
  0.0 111.7 jit_solution(508424958456352747)
XLA Ops:
  0.7 3.4 %gather_rows.1 = (bf16[64,16,128]{2,1,0:T(8,128)(2,1)}, s32[16,256]{1,0:T(8,128)}) custom-call(s32[64]{0:T(128)} %live_ref.1, bf16[32,4096]{1,0:T(8,128)(2,1)} %bitcast.16, s32[64,64]{1,0:T(8,128)} %send_ref.1), custom_call_target="tpu_custom_call" | custom-call | flops 1073741824 | bytes 1048576 | tf_op jit(solution)/shard_map/gather_rows/pallas_call | solution.py:103
  4.1 12.0 %all-to-all-start = ((bf16[64,16,128]{2,1,0:T(8,128)(2,1)}), bf16[64,16,128]{2,1,0:T(8,128)(2,1)S(1)}, u32[]{:S(2)}, u32[]{:S(2)}) async-start(bf16[64,16,128]{2,1,0:T(8,128)(2,1)} %get-tuple-element.46), calls=%async_computation | async-start | bytes 524288 | tf_op jit(solution)/shard_map/all_to_all | solution.py:465
  17.8 4.9 %agg_transposed.1 = (bf16[48,2048]{1,0:T(8,128)(2,1)S(1)}, bf16[48,2048]{1,0:T(8,128)(2,1)S(1)}, bf16[48,2048]{1,0:T(8,128)(2,1)S(1)}, bf16[48,2048]{1,0:T(8,128)(2,1)S(1)}) custom-call(s32[10,32]{1,0:T(8,128)S(1)} %bitcast.18, s32[1]{0:T(128)} %bitcast.me_ref, bf16[43,4096]{1,0:T(8,128)(2,1)S(1)} %bitcast.12, bf16[32,10,128,128]{3,2,1,0:T(8,128)(2,1)} %vals_ref.9), custom_call_target="tpu_custom_call" | custom-call | flops 2013265920 | bytes 11534336 | tf_op jit(solution)/shard_map/agg_transposed/pallas_call | solution.py:180
  22.8 1.7 %collective-permute-start = (bf16[48,2048]{1,0:T(8,128)(2,1)S(1)}, bf16[48,2048]{1,0:T(8,128)(2,1)S(1)}, u32[]{:S(2)}, u32[]{:S(2)}) collective-permute-start(bf16[48,2048]{1,0:T(8,128)(2,1)S(1)} %get-tuple-element.51), channel_id=1, source_target_pairs={{0,1},{1,0},{2,3},{3,2},{4,5},{5,4},{6,7},{7,6},{8,9},{9,8},{10,11... | collective-permute-start | bytes 589832 | tf_op jit(solution)/shard_map/ppermute | solution.py:433
  24.4 2.2 %collective-permute-start.1 = (bf16[48,2048]{1,0:T(8,128)(2,1)S(1)}, bf16[48,2048]{1,0:T(8,128)(2,1)S(1)}, u32[]{:S(2)}, u32[]{:S(2)}) collective-permute-start(bf16[48,2048]{1,0:T(8,128)(2,1)S(1)} %get-tuple-element.52), channel_id=1, source_target_pairs={{0,3},{1,2},{2,1},{3,0},{4,7},{5,6},{6,5},{7,4},{8,11},{9,10},{10,... | collective-permute-start | bytes 589832 | tf_op jit(solution)/shard_map/ppermute | solution.py:433
  27.7 7.6 %agg_one.1 = (bf16[64,16,128]{2,1,0:T(8,128)(2,1)}, bf16[32,1024]{1,0:T(8,128)(2,1)S(1)}, bf16[32,1024]{1,0:T(8,128)(2,1)S(1)}, bf16[32,1024]{1,0:T(8,128)(2,1)S(1)}, bf16[32,1024]{1,0:T(8,128)(2,1)S(1)}) custom-call(s32[10,32]{1,0:T(8,128)S(1)} %bitcast.19, s32[1]{0:T(128)} %bitcast.me_ref, bf16[32,4096]{1,0:T(8,128)(2,1)S(1)} %bitcast.17, ...), custom_call_target="tpu_custom_call" | custom-call | flops 2684354560 | bytes 11534336 | tf_op jit(solution)/shard_map/agg_one/pallas_call | solution.py:248
  35.3 9.3 %all-to-all-start.1 = ((bf16[64,16,128]{2,1,0:T(8,128)(2,1)}), bf16[64,16,128]{2,1,0:T(8,128)(2,1)S(1)}, u32[]{:S(2)}, u32[]{:S(2)}) async-start(bf16[64,16,128]{2,1,0:T(8,128)(2,1)} %get-tuple-element.53), calls=%async_computation.1 | async-start | bytes 524288 | tf_op jit(solution)/shard_map/all_to_all | solution.py:471
  47.0 2.9 %collective-permute-start.7 = (bf16[32,1024]{1,0:T(8,128)(2,1)S(1)}, bf16[32,1024]{1,0:T(8,128)(2,1)S(1)}, u32[]{:S(2)}, u32[]{:S(2)}) collective-permute-start(bf16[32,1024]{1,0:T(8,128)(2,1)S(1)} %get-tuple-element.58), channel_id=1, source_target_pairs={{0,2},{1,3},{2,0},{3,1},{4,6},{5,7},{6,4},{7,5},{8,10},{9,11},{10,... | collective-permute-start | bytes 196616 | tf_op jit(solution)/shard_map/ppermute | solution.py:433
  50.5 5.6 %all-to-all-done.1 = bf16[64,16,128]{2,1,0:T(8,128)(2,1)S(1)} async-done(((bf16[64,16,128]{2,1,0:T(8,128)(2,1)}), bf16[64,16,128]{2,1,0:T(8,128)(2,1)S(1)}, u32[]{:S(2)}, u32[]{:S(2)}) %all-to-all-start.1) | async-done | bytes 262176 | tf_op jit(solution)/shard_map/all_to_all | solution.py:471
  57.0 2.6 %collective-permute-start.3 = (bf16[16,16,128]{2,1,0:T(8,128)(2,1)S(1)}, bf16[16,16,128]{2,1,0:T(8,128)(2,1)S(1)}, u32[]{:S(2)}, u32[]{:S(2)}) collective-permute-start(bf16[16,16,128]{2,1,0:T(8,128)(2,1)S(1)} %get-tuple-element.90), channel_id=1, source_target_pairs={{0,3},{1,2},{2,1},{3,0},{4,7},{5,6},{6,5},{7,4},{8,11},{9,10},{10,... | collective-permute-start | bytes 196616 | tf_op jit(solution)/shard_map/ppermute | solution.py:433
  63.9 1.7 %dense_far.1 = (bf16[48,2048]{1,0:T(8,128)(2,1)S(1)}, bf16[48,2048]{1,0:T(8,128)(2,1)S(1)}, bf16[48,2048]{1,0:T(8,128)(2,1)S(1)}, bf16[48,2048]{1,0:T(8,128)(2,1...) custom-call(s32[1]{0:T(128)} %bitcast.me_ref, ...), custom_call_target="tpu_custom_call" | custom-call | flops 786432000 | bytes 4194304 | tf_op jit(solution)/shard_map/dense_far/pallas_call | solution.py:346
  66.4 2.1 %collective-permute-start.13 = (f32[160,128]{1,0:T(8,128)S(1)}, f32[160,128]{1,0:T(8,128)S(1)}, u32[]{:S(2)}, u32[]{:S(2)}) collective-permute-start(f32[160,128]{1,0:T(8,128)S(1)} %get-tuple-element.68), channel_id=1, source_target_pairs={{0,3},{1,2},{2,1},{3,0},{4,7},{5,6},{6,5},{7,4},{8,11},{9,10},{10,... | collective-permute-start | bytes 245768 | tf_op jit(solution)/shard_map/ppermute | solution.py:433
  75.3 2.4 %collective-permute-start.18 = (f32[160,128]{1,0:T(8,128)S(1)}, f32[160,128]{1,0:T(8,128)S(1)}, u32[]{:S(2)}, u32[]{:S(2)}) collective-permute-start(f32[160,128]{1,0:T(8,128)S(1)} %add.54), channel_id=1, source_target_pairs={{0,128},{4,132},{8,136},{12,140},{16,144},{20,148},{24,152},{28,15... | collective-permute-start | bytes 245768 | tf_op jit(solution)/shard_map/ppermute | solution.py:433
  78.1 2.0 %collective-permute-start.16 = (f32[160,128]{1,0:T(8,128)S(1)}, f32[160,128]{1,0:T(8,128)S(1)}, u32[]{:S(2)}, u32[]{:S(2)}) collective-permute-start(f32[160,128]{1,0:T(8,128)S(1)} %add.54), channel_id=1, source_target_pairs={{0,64},{4,68},{8,72},{12,76},{16,80},{20,84},{24,88},{28,92},{32,9... | collective-permute-start | bytes 245768 | tf_op jit(solution)/shard_map/ppermute | solution.py:433
  80.0 1.6 %collective-permute-done.10.refs_2_ = bf16[48,2048]{1,0:T(8,128)(2,1)S(1)} collective-permute-done((bf16[48,2048]{1,0:T(8,128)(2,1)S(1)}, bf16[48,2048]{1,0:T(8,128)(2,1)S(1)}, u32[]{:S(2)}, u32[]{:S(2)}) %collective-permute-start.10) | collective-permute-done | bytes 196640 | tf_op jit(solution)/shard_map/ppermute | solution.py:433
  83.3 2.5 %collective-permute-start.19 = (f32[160,128]{1,0:T(8,128)S(1)}, f32[160,128]{1,0:T(8,128)S(1)}, u32[]{:S(2)}, u32[]{:S(2)}) collective-permute-start(f32[160,128]{1,0:T(8,128)S(1)} %add_add_fusion.1), channel_id=1, source_target_pairs={{0,32},{4,36},{8,40},{12,44},{16,48},{20,52},{24,56},{28,60},{32,0... | collective-permute-start | bytes 245768 | tf_op jit(solution)/shard_map/ppermute | solution.py:433
  85.7 4.0 %copy-done = bf16[32,10,128,128]{3,2,1,0:T(8,128)(2,1)S(1)} copy-done((bf16[32,10,128,128]{3,2,1,0:T(8,128)(2,1)S(1)}, bf16[32,10,128,128]{3,2,1,0:T(8,128)(2,1)}, u32[]{:S(2)}) %copy-start) | copy-done | bytes 10485784
  90.7 2.4 %collective-permute-done.19 = f32[160,128]{1,0:T(8,128)S(1)} collective-permute-done((f32[160,128]{1,0:T(8,128)S(1)}, f32[160,128]{1,0:T(8,128)S(1)}, u32[]{:S(2)}, u32[]{:S(2)}) %collective-permute-start.19) | collective-permute-done | bytes 81952 | tf_op jit(solution)/shard_map/ppermute | solution.py:433
  93.9 2.0 %collective-permute-start.21 = (f32[160,128]{1,0:T(8,128)S(1)}, f32[160,128]{1,0:T(8,128)S(1)}, u32[]{:S(2)}, u32[]{:S(2)}) collective-permute-start(f32[160,128]{1,0:T(8,128)S(1)} %add.58), channel_id=1, source_target_pairs={{0,16},{4,20},{8,24},{12,28},{16,0},{20,4},{24,8},{28,12},{32,48},... | collective-permute-start | bytes 245768 | tf_op jit(solution)/shard_map/ppermute | solution.py:433
  95.9 1.7 %collective-permute-start.20 = (f32[160,128]{1,0:T(8,128)S(1)}, f32[160,128]{1,0:T(8,128)S(1)}, u32[]{:S(2)}, u32[]{:S(2)}) collective-permute-start(f32[160,128]{1,0:T(8,128)S(1)} %add.58), channel_id=1, source_target_pairs={{0,8},{4,12},{8,0},{12,4},{16,24},{20,28},{24,16},{28,20},{32,40},... | collective-permute-start | bytes 245768 | tf_op jit(solution)/shard_map/ppermute | solution.py:433
  97.6 2.7 %agg_two.4.refs_1_ = bf16[43,2688]{1,0:T(8,128)(2,1)S(1)} custom-call(s32[10,32]{1,0:T(8,128)S(1)} %bitcast.21, bf16[64,48,128]{2,1,0:T(8,128)(2,1)S(1)} %spread.1.ext_ref, bf16[32,10,128,128]{3,2,1,0:T(8,128)(2,1)S(1)} %copy-done), custom_call_target="tpu_custom_call" | custom-call | flops 1321205760 | bytes 6930000 | tf_op jit(solution)/shard_map/agg_two/pallas_call | solution.py:394
  100.3 2.9 %collective-permute-done.21 = f32[160,128]{1,0:T(8,128)S(1)} collective-permute-done((f32[160,128]{1,0:T(8,128)S(1)}, f32[160,128]{1,0:T(8,128)S(1)}, u32[]{:S(2)}, u32[]{:S(2)}) %collective-permute-start.21) | collective-permute-done | bytes 81952 | tf_op jit(solution)/shard_map/ppermute | solution.py:433
  103.2 1.6 %collective-permute-start.25 = (f32[160,128]{1,0:T(8,128)S(1)}, f32[160,128]{1,0:T(8,128)S(1)}, u32[]{:S(2)}, u32[]{:S(2)}) collective-permute-start(f32[160,128]{1,0:T(8,128)S(1)} %add_add_fusion.g0), channel_id=1, source_target_pairs={{0,2},{1,3},{2,0},{3,1},{4,6},{5,7},{6,4},{7,5},{8,10},{9,11},{10,... | collective-permute-start | bytes 245768 | tf_op jit(solution)/shard_map/ppermute | solution.py:433
  106.8 2.4 %agg_two.5 = bf16[43,4096]{1,0:T(8,128)(2,1)} custom-call(s32[10,32]{1,0:T(8,128)S(1)} %bitcast.22, bf16[64,48,128]{2,1,0:T(8,128)(2,1)S(1)} %spread.1.ext_ref, bf16[32,10,128,128]{3,2,1,0:T(8,128)(2,1)S(1)} %copy-done, bf16[43,256]{1,0:T(8,128)(2,1)S(1)} %agg_two.3.refs_0_, bf16[43,2688]{1,0:T(8,128)(2,1)S(1)} %agg_two.4.refs_1_), custom_call_target="tpu_custom_call" | custom-call | flops 566231040 | bytes 2970000 | tf_op jit(solution)/shard_map/agg_two/pallas_call | solution.py:394
  (68 shorter events, 26.8 us)
Async XLA Ops:
  4.1 23.6 %all-to-all-start = ((bf16[64,16,128]{2,1,0:T(8,128)(2,1)}), bf16[64,16,128]{2,1,0:T(8,128)(2,1)S(1)}, u32[]{:S(2)}, u32[]{:S(2)}) async-start(bf16[64,16,128]{2,1,0:T(8,128)(2,1)} %get-tuple-element.46), calls=%async_computation | async-start | bytes 524288 | tf_op jit(solution)/shard_map/all_to_all | solution.py:465
  22.8 12.6 %collective-permute-start = (bf16[48,2048]{1,0:T(8,128)(2,1)S(1)}, bf16[48,2048]{1,0:T(8,128)(2,1)S(1)}, u32[]{:S(2)}, u32[]{:S(2)}) collective-permute-start(bf16[48,2048]{1,0:T(8,128)(2,1)S(1)} %get-tuple-element.51), channel_id=1, source_target_pairs={{0,1},{1,0},{2,3},{3,2},{4,5},{5,4},{6,7},{7,6},{8,9},{9,8},{10,11... | collective-permute-start | bytes 589832 | tf_op jit(solution)/shard_map/ppermute | solution.py:433
  24.4 10.9 %collective-permute-start.1 = (bf16[48,2048]{1,0:T(8,128)(2,1)S(1)}, bf16[48,2048]{1,0:T(8,128)(2,1)S(1)}, u32[]{:S(2)}, u32[]{:S(2)}) collective-permute-start(bf16[48,2048]{1,0:T(8,128)(2,1)S(1)} %get-tuple-element.52), channel_id=1, source_target_pairs={{0,3},{1,2},{2,1},{3,0},{4,7},{5,6},{6,5},{7,4},{8,11},{9,10},{10,... | collective-permute-start | bytes 589832 | tf_op jit(solution)/shard_map/ppermute | solution.py:433
  35.3 20.8 %all-to-all-start.1 = ((bf16[64,16,128]{2,1,0:T(8,128)(2,1)}), bf16[64,16,128]{2,1,0:T(8,128)(2,1)S(1)}, u32[]{:S(2)}, u32[]{:S(2)}) async-start(bf16[64,16,128]{2,1,0:T(8,128)(2,1)} %get-tuple-element.53), calls=%async_computation.1 | async-start | bytes 524288 | tf_op jit(solution)/shard_map/all_to_all | solution.py:471
  44.6 12.4 %collective-permute-start.5 = (bf16[48,2048]{1,0:T(8,128)(2,1)S(1)}, bf16[48,2048]{1,0:T(8,128)(2,1)S(1)}, u32[]{:S(2)}, u32[]{:S(2)}) collective-permute-start(bf16[48,2048]{1,0:T(8,128)(2,1)S(1)} %get-tuple-element.54), channel_id=1, source_target_pairs={{0,2},{1,3},{2,0},{3,1},{4,6},{5,7},{6,4},{7,5},{8,10},{9,11},{10,... | collective-permute-start | bytes 589832 | tf_op jit(solution)/shard_map/ppermute | solution.py:433
  45.7 13.9 %collective-permute-start.6 = (bf16[32,1024]{1,0:T(8,128)(2,1)S(1)}, bf16[32,1024]{1,0:T(8,128)(2,1)S(1)}, u32[]{:S(2)}, u32[]{:S(2)}) collective-permute-start(bf16[32,1024]{1,0:T(8,128)(2,1)S(1)} %get-tuple-element.57), channel_id=1, source_target_pairs={{0,1},{1,0},{2,3},{3,2},{4,5},{5,4},{6,7},{7,6},{8,9},{9,8},{10,11... | collective-permute-start | bytes 196616 | tf_op jit(solution)/shard_map/ppermute | solution.py:433
  47.0 12.8 %collective-permute-start.7 = (bf16[32,1024]{1,0:T(8,128)(2,1)S(1)}, bf16[32,1024]{1,0:T(8,128)(2,1)S(1)}, u32[]{:S(2)}, u32[]{:S(2)}) collective-permute-start(bf16[32,1024]{1,0:T(8,128)(2,1)S(1)} %get-tuple-element.58), channel_id=1, source_target_pairs={{0,2},{1,3},{2,0},{3,1},{4,6},{5,7},{6,4},{7,5},{8,10},{9,11},{10,... | collective-permute-start | bytes 196616 | tf_op jit(solution)/shard_map/ppermute | solution.py:433
  49.9 9.9 %collective-permute-start.8 = (bf16[32,1024]{1,0:T(8,128)(2,1)S(1)}, bf16[32,1024]{1,0:T(8,128)(2,1)S(1)}, u32[]{:S(2)}, u32[]{:S(2)}) collective-permute-start(bf16[32,1024]{1,0:T(8,128)(2,1)S(1)} %get-tuple-element.59), channel_id=1, source_target_pairs={{0,3},{1,2},{2,1},{3,0},{4,7},{5,6},{6,5},{7,4},{8,11},{9,10},{10,... | collective-permute-start | bytes 196616 | tf_op jit(solution)/shard_map/ppermute | solution.py:433
  56.2 6.1 %collective-permute-start.4 = (bf16[16,16,128]{2,1,0:T(8,128)(2,1)S(1)}, bf16[16,16,128]{2,1,0:T(8,128)(2,1)S(1)}, u32[]{:S(2)}, u32[]{:S(2)}) collective-permute-start(bf16[16,16,128]{2,1,0:T(8,128)(2,1)S(1)} %get-tuple-element.89), channel_id=1, source_target_pairs={{0,2},{1,3},{2,0},{3,1},{4,6},{5,7},{6,4},{7,5},{8,10},{9,11},{10,... | collective-permute-start | bytes 196616 | tf_op jit(solution)/shard_map/ppermute | solution.py:433
  57.0 6.3 %collective-permute-start.3 = (bf16[16,16,128]{2,1,0:T(8,128)(2,1)S(1)}, bf16[16,16,128]{2,1,0:T(8,128)(2,1)S(1)}, u32[]{:S(2)}, u32[]{:S(2)}) collective-permute-start(bf16[16,16,128]{2,1,0:T(8,128)(2,1)S(1)} %get-tuple-element.90), channel_id=1, source_target_pairs={{0,3},{1,2},{2,1},{3,0},{4,7},{5,6},{6,5},{7,4},{8,11},{9,10},{10,... | collective-permute-start | bytes 196616 | tf_op jit(solution)/shard_map/ppermute | solution.py:433
  65.6 6.9 %collective-permute-start.12 = (f32[160,128]{1,0:T(8,128)S(1)}, f32[160,128]{1,0:T(8,128)S(1)}, u32[]{:S(2)}, u32[]{:S(2)}) collective-permute-start(f32[160,128]{1,0:T(8,128)S(1)} %get-tuple-element.67), channel_id=1, source_target_pairs={{0,2},{1,3},{2,0},{3,1},{4,6},{5,7},{6,4},{7,5},{8,10},{9,11},{10,... | collective-permute-start | bytes 245768 | tf_op jit(solution)/shard_map/ppermute | solution.py:433
  66.4 7.4 %collective-permute-start.13 = (f32[160,128]{1,0:T(8,128)S(1)}, f32[160,128]{1,0:T(8,128)S(1)}, u32[]{:S(2)}, u32[]{:S(2)}) collective-permute-start(f32[160,128]{1,0:T(8,128)S(1)} %get-tuple-element.68), channel_id=1, source_target_pairs={{0,3},{1,2},{2,1},{3,0},{4,7},{5,6},{6,5},{7,4},{8,11},{9,10},{10,... | collective-permute-start | bytes 245768 | tf_op jit(solution)/shard_map/ppermute | solution.py:433
  68.5 5.4 %collective-permute-start.14 = (f32[160,128]{1,0:T(8,128)S(1)}, f32[160,128]{1,0:T(8,128)S(1)}, u32[]{:S(2)}, u32[]{:S(2)}) collective-permute-start(f32[160,128]{1,0:T(8,128)S(1)} %get-tuple-element.70), channel_id=1, source_target_pairs={{0,1},{1,0},{2,3},{3,2},{4,5},{5,4},{6,7},{7,6},{8,9},{9,8},{10,11... | collective-permute-start | bytes 245768 | tf_op jit(solution)/shard_map/ppermute | solution.py:433
  69.1 8.9 %collective-permute-start.9 = (bf16[48,2048]{1,0:T(8,128)(2,1)S(1)}, bf16[48,2048]{1,0:T(8,128)(2,1)S(1)}, u32[]{:S(2)}, u32[]{:S(2)}) collective-permute-start(bf16[48,2048]{1,0:T(8,128)(2,1)S(1)} %get-tuple-element.64), channel_id=1, source_target_pairs={{0,1},{1,0},{2,3},{3,2},{4,5},{5,4},{6,7},{7,6},{8,9},{9,8},{10,11... | collective-permute-start | bytes 589832 | tf_op jit(solution)/shard_map/ppermute | solution.py:433
  70.5 11.1 %collective-permute-start.10 = (bf16[48,2048]{1,0:T(8,128)(2,1)S(1)}, bf16[48,2048]{1,0:T(8,128)(2,1)S(1)}, u32[]{:S(2)}, u32[]{:S(2)}) collective-permute-start(bf16[48,2048]{1,0:T(8,128)(2,1)S(1)} %get-tuple-element.65), channel_id=1, source_target_pairs={{0,2},{1,3},{2,0},{3,1},{4,6},{5,7},{6,4},{7,5},{8,10},{9,11},{10,... | collective-permute-start | bytes 589832 | tf_op jit(solution)/shard_map/ppermute | solution.py:433
  72.5 10.4 %collective-permute-start.11 = (bf16[48,2048]{1,0:T(8,128)(2,1)S(1)}, bf16[48,2048]{1,0:T(8,128)(2,1)S(1)}, u32[]{:S(2)}, u32[]{:S(2)}) collective-permute-start(bf16[48,2048]{1,0:T(8,128)(2,1)S(1)} %get-tuple-element.66), channel_id=1, source_target_pairs={{0,3},{1,2},{2,1},{3,0},{4,7},{5,6},{6,5},{7,4},{8,11},{9,10},{10,... | collective-permute-start | bytes 589832 | tf_op jit(solution)/shard_map/ppermute | solution.py:433
  75.3 7.8 %collective-permute-start.18 = (f32[160,128]{1,0:T(8,128)S(1)}, f32[160,128]{1,0:T(8,128)S(1)}, u32[]{:S(2)}, u32[]{:S(2)}) collective-permute-start(f32[160,128]{1,0:T(8,128)S(1)} %add.54), channel_id=1, source_target_pairs={{0,128},{4,132},{8,136},{12,140},{16,144},{20,148},{24,152},{28,15... | collective-permute-start | bytes 245768 | tf_op jit(solution)/shard_map/ppermute | solution.py:433
  77.6 5.5 %collective-permute-start.17 = (f32[160,128]{1,0:T(8,128)S(1)}, f32[160,128]{1,0:T(8,128)S(1)}, u32[]{:S(2)}, u32[]{:S(2)}) collective-permute-start(f32[160,128]{1,0:T(8,128)S(1)} %add.54), channel_id=1, source_target_pairs={{0,192},{4,196},{8,200},{12,204},{16,208},{20,212},{24,216},{28,22... | collective-permute-start | bytes 245768 | tf_op jit(solution)/shard_map/ppermute | solution.py:433
  83.3 9.9 %collective-permute-start.19 = (f32[160,128]{1,0:T(8,128)S(1)}, f32[160,128]{1,0:T(8,128)S(1)}, u32[]{:S(2)}, u32[]{:S(2)}) collective-permute-start(f32[160,128]{1,0:T(8,128)S(1)} %add_add_fusion.1), channel_id=1, source_target_pairs={{0,32},{4,36},{8,40},{12,44},{16,48},{20,52},{24,56},{28,60},{32,0... | collective-permute-start | bytes 245768 | tf_op jit(solution)/shard_map/ppermute | solution.py:433
  93.2 7.1 %collective-permute-start.22 = (f32[160,128]{1,0:T(8,128)S(1)}, f32[160,128]{1,0:T(8,128)S(1)}, u32[]{:S(2)}, u32[]{:S(2)}) collective-permute-start(f32[160,128]{1,0:T(8,128)S(1)} %add.58), channel_id=1, source_target_pairs={{0,24},{4,28},{8,16},{12,20},{16,8},{20,12},{24,0},{28,4},{32,56},... | collective-permute-start | bytes 245768 | tf_op jit(solution)/shard_map/ppermute | solution.py:433
  93.9 9.3 %collective-permute-start.21 = (f32[160,128]{1,0:T(8,128)S(1)}, f32[160,128]{1,0:T(8,128)S(1)}, u32[]{:S(2)}, u32[]{:S(2)}) collective-permute-start(f32[160,128]{1,0:T(8,128)S(1)} %add.58), channel_id=1, source_target_pairs={{0,16},{4,20},{8,24},{12,28},{16,0},{20,4},{24,8},{28,12},{32,48},... | collective-permute-start | bytes 245768 | tf_op jit(solution)/shard_map/ppermute | solution.py:433
  95.9 7.3 %collective-permute-start.20 = (f32[160,128]{1,0:T(8,128)S(1)}, f32[160,128]{1,0:T(8,128)S(1)}, u32[]{:S(2)}, u32[]{:S(2)}) collective-permute-start(f32[160,128]{1,0:T(8,128)S(1)} %add.58), channel_id=1, source_target_pairs={{0,8},{4,12},{8,0},{12,4},{16,24},{20,28},{24,16},{28,20},{32,40},... | collective-permute-start | bytes 245768 | tf_op jit(solution)/shard_map/ppermute | solution.py:433
  103.2 6.1 %collective-permute-start.25 = (f32[160,128]{1,0:T(8,128)S(1)}, f32[160,128]{1,0:T(8,128)S(1)}, u32[]{:S(2)}, u32[]{:S(2)}) collective-permute-start(f32[160,128]{1,0:T(8,128)S(1)} %add_add_fusion.g0), channel_id=1, source_target_pairs={{0,2},{1,3},{2,0},{3,1},{4,6},{5,7},{6,4},{7,5},{8,10},{9,11},{10,... | collective-permute-start | bytes 245768 | tf_op jit(solution)/shard_map/ppermute | solution.py:433
  104.8 6.1 %collective-permute-start.24 = (f32[160,128]{1,0:T(8,128)S(1)}, f32[160,128]{1,0:T(8,128)S(1)}, u32[]{:S(2)}, u32[]{:S(2)}) collective-permute-start(f32[160,128]{1,0:T(8,128)S(1)} %add_add_fusion.g0), channel_id=1, source_target_pairs={{0,3},{1,2},{2,1},{3,0},{4,7},{5,6},{6,5},{7,4},{8,11},{9,10},{10,... | collective-permute-start | bytes 245768 | tf_op jit(solution)/shard_map/ppermute | solution.py:433
  (12 other events, 154.6 us)
